TPU v7x, 128 devices: a whole 4x4x4 slice. The times are simulated.
128 devices in a mesh: group: 4 (over z), dom: 32 (over y, x, core).
Axes of the slice: x: 4, y: 4, z: 4, core: 2. Of those that a mesh axis runs over, the one named last changes fastest.
Arguments:
- feats: bfloat16 [262144, 256], P(('group', 'dom')), may hold values from -6 to 6
- edge_src: int32 [128, 8192], P(('group', 'dom')), may hold values from 0 to 2047, as said below
- edge_slot: int32 [128, 8192], P(('group', 'dom')), may hold values from 0 to 1535
- slot_counts: int32 [128, 32], P(('group', 'dom')), may hold values from 36 to 48, as said below
- replica_row: int32 [128, 32, 48], P(('group', 'dom')), may hold values from 0 to 2047
- stale_agg: bfloat16 [262144, 256], P(('group', 'dom')), may hold values from -6 to 6
- bin_ages: int32 [2048], P(('group', 'dom')), may hold values from 0 to 7
- cotangent: bfloat16 [262144, 256], P(('group', 'dom')), may hold values from -6 to 6
- w_self: bfloat16 [256, 256], replicated, may hold values from -0.375 to 0.375
- w_neigh: bfloat16 [256, 256], replicated, may hold values from -0.375 to 0.375
Outputs:
- hidden: bfloat16 [262144, 256], P(('group', 'dom'))
- feat_grad: bfloat16 [262144, 256], P(('group', 'dom'))
- new_self: float32 [256, 256], replicated
- new_neigh: float32 [256, 256], replicated
Inputs may be any that keep to these rules, and one draw needn't show every extreme that they name: `slot_counts`: in every row some entry equals 48. `edge_src`: edges come in tiles of 128; the sources of tile t lie in rows 128 * (t mod (16)) to 128 * (t mod (16)) + 127.
All inputs are finite; a program needn't handle non-finite values.
Results may differ from a plain program's by a relative error of at most 0.0056.
Values may be sent and summed in bfloat16 or wider, within the bound.
No kernel may reach another device: no remote copies, remote signals or barrier semaphores. Data moves between devices by JAX's collectives and lax.ppermute only.
A program may use at most 64 MiB of HBM per device.

v0:
```python
import jax
import jax.numpy as jnp
from jax import lax
from jax.sharding import PartitionSpec as P


def body(
    feats,
    edge_src,
    edge_slot,
    slot_counts,
    replica_row,
    stale_agg,
    bin_ages,
    cotangent,
    w_self,
    w_neigh,
):
    verts, width = feats.shape
    dom_size = lax.axis_size("dom")
    capacity = replica_row.shape[2]
    slot_total = dom_size * capacity
    sources = edge_src[0]
    targets = edge_slot[0]
    edge_count = sources.shape[0]
    bin_count = verts // 128
    repeats = edge_count // verts
    contraction_row_dims = (((0,), (0,)), ((), ()))
    contract_cols = (((1,), (1,)), ((), ()))
    slot_live = jnp.arange(capacity)[None, :] < slot_counts[0][:, None]
    local_src = (sources % 128).reshape(repeats, bin_count, 128)
    source_indicator = (local_src[..., None] == jnp.arange(128, dtype=jnp.int32)).astype(
        jnp.bfloat16
    )
    feature_buckets = feats.reshape(bin_count, 128, width)
    edge_feats = jnp.einsum(
        "glnv,lvu->glnu", source_indicator, feature_buckets, preferred_element_type=jnp.float32
    )
    edge_feats = edge_feats.astype(jnp.bfloat16).reshape(edge_count, width)
    slot_indicator = (targets[:, None] == jnp.arange(slot_total, dtype=jnp.int32)[None, :]).astype(
        jnp.bfloat16
    )
    partial_value_rows = lax.dot_general(
        slot_indicator, edge_feats, contraction_row_dims, preferred_element_type=jnp.float32
    )
    partial_value_rows = partial_value_rows.reshape(dom_size, capacity, width)
    partial_value_rows = jnp.where(slot_live[:, :, None], partial_value_rows, 0.0).astype(
        jnp.bfloat16
    )
    arrived, master_rows = (
        lax.all_to_all(partial_value_rows, "dom", split_axis=0, concat_axis=0, tiled=True),
        lax.all_to_all(replica_row[0], "dom", split_axis=0, concat_axis=0, tiled=True),
    )
    master_flat = master_rows.reshape(-1)
    master_onehot = (master_flat[:, None] == jnp.arange(verts, dtype=jnp.int32)[None, :]).astype(
        jnp.bfloat16
    )
    summed = lax.dot_general(
        master_onehot,
        arrived.reshape(-1, width),
        contraction_row_dims,
        preferred_element_type=jnp.float32,
    )
    age_factor = jnp.repeat(1.0 / (1.0 + bin_ages.astype(jnp.float32)), 128)
    aggregate = summed + stale_agg.astype(jnp.float32) * age_factor[:, None]
    inverse = lax.rsqrt(jnp.mean(aggregate * aggregate, axis=1, keepdims=True) + 1e-05)
    normed = (aggregate * inverse).astype(jnp.bfloat16)
    preact = jnp.dot(feats, w_self, preferred_element_type=jnp.float32) + jnp.dot(
        normed, w_neigh, preferred_element_type=jnp.float32
    )
    sigmoid_pre = jax.nn.sigmoid(preact)
    hidden = (preact * sigmoid_pre).astype(jnp.bfloat16)
    grad_pre = (
        cotangent.astype(jnp.float32) * sigmoid_pre * (1.0 + preact * (1.0 - sigmoid_pre))
    ).astype(jnp.bfloat16)
    grad_self = lax.dot_general(
        feats, grad_pre, contraction_row_dims, preferred_element_type=jnp.float32
    )
    grad_neigh = lax.dot_general(
        normed, grad_pre, contraction_row_dims, preferred_element_type=jnp.float32
    )
    grad_normed = lax.dot_general(
        grad_pre, w_neigh, contract_cols, preferred_element_type=jnp.float32
    )
    inner = jnp.mean(grad_normed * aggregate, axis=1, keepdims=True)
    grad_agg = (inverse * (grad_normed - aggregate * inverse * inverse * inner)).astype(
        jnp.bfloat16
    )
    outgoing = grad_agg[master_flat].reshape(dom_size, capacity, width)
    returned = lax.all_to_all(outgoing, "dom", split_axis=0, concat_axis=0, tiled=True)
    slot_grads = jnp.where(slot_live[:, :, None], returned, jnp.zeros((), jnp.bfloat16)).reshape(
        -1, width
    )
    edge_value_rows = jnp.dot(
        slot_indicator, slot_grads, preferred_element_type=jnp.float32
    ).astype(jnp.bfloat16)
    edge_value_rows = edge_value_rows.reshape(repeats, bin_count, 128, width)
    edge_grads = jnp.einsum(
        "govq,govw->oqw", source_indicator, edge_value_rows, preferred_element_type=jnp.float32
    ).reshape(verts, width)
    self_back = lax.dot_general(grad_pre, w_self, contract_cols, preferred_element_type=jnp.float32)
    feat_grad = (self_back + edge_grads).astype(jnp.bfloat16)
    total_self, total_neigh = lax.psum((grad_self, grad_neigh), ("group", "dom"))
    grad_norm = jnp.sqrt(jnp.sum(total_self * total_self) + jnp.sum(total_neigh * total_neigh))
    clip_scale = jnp.minimum(1.0, 1.0 / grad_norm)
    new_self = w_self.astype(jnp.float32) - 8.0 * clip_scale * total_self
    new_neigh = w_neigh.astype(jnp.float32) - 8.0 * clip_scale * total_neigh
    return (hidden, feat_grad, new_self, new_neigh)


def solution(mesh):
    placed = (
        P(("group", "dom"), None),
        P(("group", "dom"), None),
        P(("group", "dom"), None),
        P(("group", "dom"), None),
        P(("group", "dom"), None, None),
        P(("group", "dom"), None),
        P(("group", "dom")),
        P(("group", "dom"), None),
        P(),
        P(),
    )
    return jax.shard_map(
        body,
        mesh=mesh,
        in_specs=placed,
        out_specs=(P(("group", "dom"), None), P(("group", "dom"), None), P(), P()),
        check_vma=False,
    )
```

profile of v0, /device:TPU:1, one launch (start us, length us, event | category | flops | bytes accessed | tf_op | source)
XLA Modules:
  0.0 240.8 jit_solution(10672064789846155135)
XLA Ops:
  7.2 0.0 copy-start
  7.2 8.7 %all-to-all-start = ((s32[32,1,48]{2,1,0:T(1,128)}), s32[32,1,48]{2,1,0:T(1,128)S(1)}, u32[]{:S(2)}, u32[]{:S(2)}) async-start(s32[32,1,48]{2,1,0:T(1,128)} %bitcast.48), calls=%async_computation | async-start | bytes 32768 | tf_op jit(solution)/shard_map/all_to_all | solution.py:52
  15.9 0.8 add_select_fusion
  16.7 1.3 convert_bitcast_fusion
  18.0 0.0 copy-start.8
  18.1 0.0 copy-start.10
  18.1 2.2 copy.37
  20.3 0.1 iota_compare_fusion.13
  20.4 0.0 copy-done.10
  20.4 10.6 %select_convert_fusion = bf16[32,48,256]{2,1,0:T(8,128)(2,1)} fusion(bf16[8192,256,1]{1,0,2:T(8,128)(2,1)} %bitcast.42, s32[32,48]{1,0:T(8,128)S(1)} %multiply_add_fusion, s32[8192]{0:T(1024)S(1)} %bitcast.50, pred[32,48]{1,0:T(8,128)(4,1)S(1)} %iota_compare_fusion.13), kind=kOutput, calls=%fused_computation.30 | convolution fusion | flops 6455820288 | bytes 5021184 | tf_op jit(solution)/shard_map/dot_general | solution.py:43
  31.0 0.0 all-to-all-done
  31.0 7.5 %all-to-all-start.1 = ((bf16[32,48,256]{2,1,0:T(8,128)(2,1)}), bf16[32,48,256]{2,1,0:T(8,128)(2,1)S(1)}, u32[]{:S(2)}, u32[]{:S(2)}) async-start(bf16[32,48,256]{2,1,0:T(8,128)(2,1)} %select_convert_fusion), calls=%async_computation.1 | async-start | bytes 1572864 | tf_op jit(solution)/shard_map/all_to_all | solution.py:51
  38.5 0.2 all-reduce.3.cloned.1.call-start
  38.7 0.0 copy-done.11
  38.8 1.4 copy.38
  40.2 0.1 broadcast_bitcast_fusion
  40.3 1.8 fusion.21
  42.1 0.5 broadcast.118
  42.6 0.7 reduce.7
  43.3 0.1 eq.67
  43.4 0.1 reshape.147
  43.5 9.3 %all-to-all-done.1 = bf16[32,48,256]{2,1,0:T(8,128)(2,1)S(1)} async-done(((bf16[32,48,256]{2,1,0:T(8,128)(2,1)}), bf16[32,48,256]{2,1,0:T(8,128)(2,1)S(1)}, u32[]{:S(2)}, u32[]{:S(2)}) %all-to-all-start.1) | async-done | bytes 786464 | tf_op jit(solution)/shard_map/all_to_all | solution.py:51
  52.7 0.9 copy-done.6
  53.6 4.5 %multiply_reduce_fusion.1 = (f32[2048]{0:T(1024)S(1)}, f32[2048,256]{0,1:T(8,128)S(1)}) fusion(f32[2048]{0:T(1024)S(1)} %broadcast_bitcast_fusion, bf16[2048,256]{0,1:T(8,128)(2,1)} %copy.38, bf16[1536,256]{1,0:T(8,128)(2,1)} %bitcast.44, s32[1536]{0:T(1024)S(1)} %eq.67), kind=kOutput, calls=%fused_computation.26 | convolution fusion | flops 1616377856 | bytes 3954688 | tf_op jit(solution)/shard_map/dot_general | solution.py:58
  58.2 2.2 multiply_convert_fusion.1
  60.4 1.3 fusion.18
  61.7 1.2 convolution_bitcast_fusion
  62.9 3.0 %multiply_reduce_fusion = (f32[2048]{0:T(1024)S(1)}, f32[2048,256]{0,1:T(8,128)}) fusion(f32[2048,256]{0,1:T(8,128)S(1)} %get-tuple-element.21, bf16[2048,256]{1,0:T(8,128)(2,1)} %copy-done.1, bf16[256,256]{1,0:T(8,128)(2,1)S(1)} %copy-done.7), kind=kOutput, calls=%fused_computation.22 | convolution fusion | flops 269481984 | bytes 5382144 | tf_op jit(solution)/shard_map/dot_general | solution.py:82
  66.0 0.0 all-reduce.3.cloned.1.call-update
  66.0 3.1 %multiply_convert_fusion = bf16[2048,256]{0,1:T(8,128)(2,1)} fusion(f32[2048,256]{0,1:T(8,128)} %get-tuple-element.23, f32[2048,256]{0,1:T(8,128)S(1)} %get-tuple-element.21, f32[2048]{0:T(1024)S(1)} %broadcast_multiply_fusion, f32[2048]{0:T(1024)S(1)} %add_rsqrt_fusion), kind=kLoop, calls=%fused_computation.21 | loop fusion | flops 3145728 | bytes 5259264 | tf_op jit(solution)/shard_map/convert_element_type | solution.py:86
  69.1 1.5 copy.39
  70.5 5.4 %gather_fusion = bf16[1536,256]{1,0:T(8,128)(2,1)} fusion(bf16[2048,256]{1,0:T(8,128)(2,1)S(1)} %copy.39, s32[2048]{0:T(1024)S(1)} %pad_clamp_fusion), kind=kCustom, calls=%fused_computation | custom fusion | bytes 1579008 | tf_op jit(solution)/shard_map/gather | solution.py:89
  75.9 4.1 %all-to-all-start.2 = ((bf16[32,48,256]{2,1,0:T(8,128)(2,1)}), bf16[32,48,256]{2,1,0:T(8,128)(2,1)S(1)}, u32[]{:S(2)}, u32[]{:S(2)}) async-start(bf16[32,48,256]{2,1,0:T(8,128)(2,1)} %bitcast.12), calls=%async_computation.2 | async-start | bytes 1572864 | tf_op jit(solution)/shard_map/all_to_all | solution.py:90
  80.0 0.1 copy.41
  80.1 0.1 copy.43
  80.2 134.1 %all-reduce.3.cloned.1.call-done = (f32[256,256]{0,1:T(8,128)}, f32[256,256]{0,1:T(8,128)}) async-done(((f32[256,256]{0,1:T(8,128)}, f32[256,256]{0,1:T(8,128)}), (f32[256,256]{0,1:T(8,128)}, f32[256,256]{0,1:T(8,128)})) %all-reduce.3.cloned.1.call-update) | async-done | bytes 524304 | tf_op jit(solution)/shard_map/psum | solution.py:103
  214.3 1.6 multiply_reduce_fusion.2
  215.9 1.6 multiply_reduce_fusion.3
  218.9 1.1 multiply_subtract_fusion
  220.0 0.8 copy.44
  220.8 0.8 copy.45
  221.7 0.0 all-to-all-done.2
  221.7 0.3 broadcast_select_fusion
  221.9 9.3 %fusion.7 = bf16[8192,256]{1,0:T(8,128)(2,1)S(1)} fusion(bf16[1536,256]{1,0:T(8,128)(2,1)S(1)} %bitcast.45, s32[8192]{0:T(1024)S(1)} %bitcast.51), kind=kOutput, calls=%fused_computation.10 | convolution fusion | flops 6457131008 | bytes 5013504 | tf_op jit(solution)/shard_map/dot_general | solution.py:94
  231.3 0.0 copy-start.2
  231.3 0.8 fusion.9
  232.0 0.5 copy-done.2
  232.5 1.4 fusion.13
  (23 shorter events, 0.1 us)
Async XLA Ops:
  7.2 9.6 %copy-start = (bf16[2048,256]{1,0:T(8,128)(2,1)S(1)}, bf16[2048,256]{1,0:T(8,128)(2,1)}, u32[]{:S(2)}) copy-start(bf16[2048,256]{1,0:T(8,128)(2,1)} %param.10) | copy-start | bytes 3145732
  7.2 23.8 %all-to-all-start = ((s32[32,1,48]{2,1,0:T(1,128)}), s32[32,1,48]{2,1,0:T(1,128)S(1)}, u32[]{:S(2)}, u32[]{:S(2)}) async-start(s32[32,1,48]{2,1,0:T(1,128)} %bitcast.48), calls=%async_computation | async-start | bytes 32768 | tf_op jit(solution)/shard_map/all_to_all | solution.py:52
  18.0 2.2 copy-start.8
  18.1 2.3 copy-start.10
  20.4 18.4 %copy-start.11 = (s32[16]{0:T(128)S(1)}, s32[16]{0:T(128)}, u32[]{:S(2)}) copy-start(s32[16]{0:T(128)} %param.16) | copy-start | bytes 196
  31.0 7.8 %copy-start.5 = (bf16[2048,256]{1,0:T(8,128)(2,1)S(1)}, bf16[2048,256]{1,0:T(8,128)(2,1)}, u32[]{:S(2)}) copy-start(bf16[2048,256]{1,0:T(8,128)(2,1)} %param.15) | copy-start | bytes 3145732
  31.0 9.3 %copy-start.4 = (bf16[256,256]{1,0:T(8,128)(2,1)S(1)}, bf16[256,256]{1,0:T(8,128)(2,1)}, u32[]{:S(2)}) copy-start(bf16[256,256]{1,0:T(8,128)(2,1)} %param.18) | copy-start | bytes 393220
  31.0 21.8 %all-to-all-start.1 = ((bf16[32,48,256]{2,1,0:T(8,128)(2,1)}), bf16[32,48,256]{2,1,0:T(8,128)(2,1)S(1)}, u32[]{:S(2)}, u32[]{:S(2)}) async-start(bf16[32,48,256]{2,1,0:T(8,128)(2,1)} %select_convert_fusion), calls=%async_computation.1 | async-start | bytes 1572864 | tf_op jit(solution)/shard_map/all_to_all | solution.py:51
  38.5 175.8 %all-reduce.3.cloned.1.call-start = ((), (), s32[]{:S(2)}) async-start(), calls=%async_computation.3 | async-start | bytes 1048576 | tf_op jit(solution)/shard_map/psum | solution.py:103
  52.7 0.9 copy-start.6
  53.6 4.6 %copy-start.3 = (f32[2048,256]{1,0:T(8,128)S(1)}, f32[2048,256]{1,0:T(8,128)}, u32[]{:S(2)}) copy-start(f32[2048,256]{1,0:T(8,128)} %fusion.21) | copy-start | bytes 6291460
  53.6 4.6 %copy-start.7 = (bf16[256,256]{1,0:T(8,128)(2,1)S(1)}, bf16[256,256]{1,0:T(8,128)(2,1)}, u32[]{:S(2)}) copy-start(bf16[256,256]{1,0:T(8,128)(2,1)} %param.19) | copy-start | bytes 393220
  53.6 4.6 %copy-start.9 = (bf16[2048,256]{1,0:T(8,128)(2,1)S(1)}, bf16[2048,256]{1,0:T(8,128)(2,1)}, u32[]{:S(2)}) copy-start(bf16[2048,256]{1,0:T(8,128)(2,1)} %param.17) | copy-start | bytes 3145732
  60.4 1.3 copy-start.1
  75.9 145.8 %all-to-all-start.2 = ((bf16[32,48,256]{2,1,0:T(8,128)(2,1)}), bf16[32,48,256]{2,1,0:T(8,128)(2,1)S(1)}, u32[]{:S(2)}, u32[]{:S(2)}) async-start(bf16[32,48,256]{2,1,0:T(8,128)(2,1)} %bitcast.12), calls=%async_computation.2 | async-start | bytes 1572864 | tf_op jit(solution)/shard_map/all_to_all | solution.py:90
  231.3 1.2 copy-start.2
Sparse Core Ops, SparseCore 0:
  66.1 148.1 all-reduce.2
where the time goes:
time: 241 us
  waiting for transfers between devices  143 us (59%)
  matrix products  37.5 us (16%)
  starting transfers between devices  20.6 us (9%)
  between operations  15.6 us (6%)
  local copies, waits for them, and re-layouts  14.5 us (6%)
  other arithmetic  9.25 us (4%)
    psum x1, waiting for transfers between devices, body(): lax.psum((grad_self, grad_neigh), ('group', 'dom'))  134 us
    dot_general x1, matrix products, body(): lax.dot_general(slot_indicator, edge_feats, contraction_row_dims, preferr...  10.6 us
    dot_general x1, matrix products, body(): jnp.dot(slot_indicator, slot_grads, preferred_element_type=jnp.float32)  9.32 us
    all_to_all x1, waiting for transfers between devices, body(): lax.all_to_all(partial_value_rows, 'dom', split_axis=0, concat_axis=0, ti...  9.26 us
    all_to_all x1, starting transfers between devices, body(): lax.all_to_all(replica_row[0], 'dom', split_axis=0, concat_axis=0, tiled=...  8.73 us
    all_to_all x1, starting transfers between devices, body(): lax.all_to_all(partial_value_rows, 'dom', split_axis=0, concat_axis=0, ti...  7.52 us
    gather x1, local copies, waits for them, and re-layouts, body(): outgoing = grad_agg[master_flat].reshape(dom_size, capacity, width)  5.36 us
  transfers between devices with their start and end apart: 4, of which 2 were waited for; matrix products, arithmetic and copies ran while one was open for 15% of the time, Pallas kernels for 0%

commit v1 on v0

v1 whole, which is shorter than its diff:
```python
import functools

import jax
import jax.numpy as jnp
from jax import lax
from jax.experimental import pallas as pl
from jax.experimental.pallas import tpu as pltpu
from jax.sharding import PartitionSpec as P

BF = jnp.bfloat16
F32 = jnp.float32
TILE = 128
ROWS = 512
INDEX_ROWS = 16
NN = (((1,), (0,)), ((), ()))
NT = (((1,), (1,)), ((), ()))
TN = (((0,), (0,)), ((), ()))
VMEM_BYTES = 48 * 1024 * 1024


def dot(a, b, dims):
    return lax.dot_general(a, b, dims, preferred_element_type=F32)


def mask(cond):
    return jnp.where(cond, 1.0, 0.0).astype(BF)


def bin_edges(ref, b, bins, repeats):
    return jnp.concatenate(
        [ref[:, pl.ds(pl.multiple_of((g * bins + b) * TILE, TILE), TILE)] for g in range(repeats)],
        axis=1,
    )


def bin_indicators(src_ref, slot_ref, b, bins, repeats, slots):
    src = bin_edges(src_ref, b, bins, repeats) & (TILE - 1)
    slot = bin_edges(slot_ref, b, bins, repeats)
    row = lax.broadcasted_iota(jnp.int32, (TILE, src.shape[1]), 0)
    source = mask(row == src)
    low = mask(row == (slot & (TILE - 1)))
    high = slot >> 7
    blocks = [low * mask(high == h) for h in range(slots // TILE)]
    return source, blocks


def scatter_kernel(counts_ref, rows_ref, src_ref, slot_ref, feats_ref, out_ref, adj_ref):
    slots, verts = adj_ref.shape
    peers, cap = rows_ref.shape
    bins = verts // TILE
    repeats = src_ref.shape[1] // verts

    def one_bin(b, carry):
        source, blocks = bin_indicators(src_ref, slot_ref, b, bins, repeats, slots)
        column = pl.ds(pl.multiple_of(b * TILE, TILE), TILE)
        for h, block in enumerate(blocks):
            adj_ref[h * TILE : (h + 1) * TILE, column] = dot(block, source, NT).astype(BF)
        return carry

    lax.fori_loop(0, bins, one_bin, 0)
    sub = lax.broadcasted_iota(jnp.int32, (INDEX_ROWS, cap), 0)
    slot_in_peer = lax.broadcasted_iota(jnp.int32, (cap, 2 * TILE), 0)
    step = 8
    for first in range(0, peers, step):
        rows = dot(adj_ref[first * cap : (first + step) * cap, :], feats_ref[...], NN)
        for q in range(first, first + step):
            part = rows[(q - first) * cap : (q - first + 1) * cap, :]
            part = jnp.where(slot_in_peer < counts_ref[0, q], part, 0.0).astype(BF)
            out_ref[q, 0:cap, :] = part[:, :TILE]
            out_ref[q, cap : 2 * cap, :] = part[:, TILE:]
            out_ref[q, 2 * cap :, :] = jnp.zeros((INDEX_ROWS, TILE), BF)
            index = rows_ref[q : q + 1, :]
            value = jnp.where(sub == 0, index >> 7, jnp.where(sub == 1, index & (TILE - 1), 0))
            out_ref[q, 2 * cap :, 0:cap] = value.astype(F32).astype(BF)


def adjacency_kernel(src_ref, slot_ref, out_ref):
    verts, slots = out_ref.shape
    bins = verts // TILE
    repeats = src_ref.shape[1] // verts

    def one_bin(b, carry):
        source, blocks = bin_indicators(src_ref, slot_ref, b, bins, repeats, slots)
        row = pl.ds(pl.multiple_of(b * TILE, TILE), TILE)
        for h, block in enumerate(blocks):
            out_ref[row, h * TILE : (h + 1) * TILE] = dot(source, block, NT).astype(BF)
        return carry

    lax.fori_loop(0, bins, one_bin, 0)


def master_kernel(
    cap,
    ages_ref,
    got_ref,
    feats_ref,
    stale_ref,
    cot_ref,
    ws_ref,
    wn_ref,
    hidden_ref,
    gp_ref,
    out_ref,
    ga_ref,
    arr_ref,
):
    verts, width = feats_ref.shape
    peers = got_ref.shape[0]
    slots = peers * cap
    arr_ref[:, :TILE] = got_ref[:, 0:cap, :].reshape(slots, TILE)
    arr_ref[:, TILE:] = got_ref[:, cap : 2 * cap, :].reshape(slots, TILE)
    coded = got_ref[:, 2 * cap :, :].reshape(peers * INDEX_ROWS, TILE)
    pick_row = lax.broadcasted_iota(jnp.int32, (peers, peers * INDEX_ROWS), 1)
    pick_peer = lax.broadcasted_iota(jnp.int32, (peers, peers * INDEX_ROWS), 0) * INDEX_ROWS
    high = dot(mask(pick_row == pick_peer), coded, NN).astype(BF)
    low = dot(mask(pick_row == pick_peer + 1), coded, NN).astype(BF)
    slot = lax.broadcasted_iota(jnp.int32, (TILE, slots), 1)
    lane = lax.broadcasted_iota(jnp.int32, (TILE, slots), 0)
    spread = mask(slot % cap == lane)
    value = dot(high, spread, NN) * float(TILE) + dot(low, spread, NN)
    own = slot[:peers] // cap == lane[:peers]
    row_index = jnp.sum(jnp.where(own, value, 0.0), axis=0, keepdims=True).astype(jnp.int32)
    slot_c = lax.broadcasted_iota(jnp.int32, (slots, TILE), 0)
    lane_c = lax.broadcasted_iota(jnp.int32, (slots, TILE), 1)
    peer_c = mask(slot_c[:, :peers] // cap == lane_c[:, :peers])
    value_c = dot(peer_c, high, NN) * float(TILE) + dot(peer_c, low, NN)
    col_index = jnp.sum(
        jnp.where(slot_c % cap == lane_c, value_c, 0.0), axis=1, keepdims=True
    ).astype(jnp.int32)

    sub = lax.broadcasted_iota(jnp.int32, (TILE, slots), 0)
    low_hot = mask(sub == (row_index & (TILE - 1)))
    row_high = row_index >> 7
    total = None
    per = ROWS // TILE
    for block in range(verts // ROWS):
        rows = slice(block * ROWS, (block + 1) * ROWS)
        hot = jnp.concatenate(
            [low_hot * mask(row_high == block * per + k) for k in range(per)], axis=0
        )
        agg = dot(hot, arr_ref[...], NN)
        aged = jnp.concatenate(
            [
                stale_ref[(block * per + k) * TILE : (block * per + k + 1) * TILE, :].astype(F32)
                * ages_ref[block * per + k]
                for k in range(per)
            ],
            axis=0,
        )
        agg = agg + aged
        inverse = lax.rsqrt(jnp.mean(agg * agg, axis=1, keepdims=True) + 1e-05)
        normed = (agg * inverse).astype(BF)
        feats = feats_ref[rows, :]
        pre = dot(feats, ws_ref[...], NN) + dot(normed, wn_ref[...], NN)
        sig = jax.nn.sigmoid(pre)
        hidden_ref[rows, :] = (pre * sig).astype(BF)
        gp = (cot_ref[rows, :].astype(F32) * sig * (1.0 + pre * (1.0 - sig))).astype(BF)
        gp_ref[rows, :] = gp
        grads = jnp.concatenate([dot(feats, gp, TN), dot(normed, gp, TN)], axis=0)
        total = grads if total is None else total + grads
        gn = dot(gp, wn_ref[...], NT)
        inner = jnp.mean(gn * agg, axis=1, keepdims=True)
        ga_ref[rows, :] = (inverse * (gn - agg * (inverse * inverse * inner))).astype(BF)
    total = total.astype(BF)
    share = 2 * width // peers
    out_ref[:, 2 * cap : 2 * cap + share, :] = total[:, :TILE].reshape(peers, share, TILE)
    out_ref[:, 2 * cap + share :, :] = total[:, TILE:].reshape(peers, share, TILE)
    step = 8
    for first in range(0, peers, step):
        part = slice(first * cap, (first + step) * cap)
        lanes = lax.broadcasted_iota(jnp.int32, (step * cap, verts), 1)
        rows = dot(mask(lanes == col_index[part, :]), ga_ref[...], NN).astype(BF)
        out_ref[first : first + step, 0:cap, :] = rows[:, :TILE].reshape(step, cap, TILE)
        out_ref[first : first + step, cap : 2 * cap, :] = rows[:, TILE:].reshape(step, cap, TILE)


def back_kernel(cap, counts_ref, got_ref, adj_ref, gp_ref, ws_ref, out_ref, grad_ref):
    peers = got_ref.shape[0]
    slot_in_peer = lax.broadcasted_iota(jnp.int32, (cap, TILE), 0)
    for q in range(peers):
        live = slot_in_peer < counts_ref[0, q]
        for half in range(2):
            rows = got_ref[q, half * cap : (half + 1) * cap, :]
            grad_ref[q * cap : (q + 1) * cap, half * TILE : (half + 1) * TILE] = jnp.where(
                live, rows.astype(F32), 0.0
            ).astype(BF)
    for block in range(out_ref.shape[0] // ROWS):
        rows = slice(block * ROWS, (block + 1) * ROWS)
        out_ref[rows, :] = (
            dot(adj_ref[rows, :], grad_ref[...], NN) + dot(gp_ref[rows, :], ws_ref[...], NT)
        ).astype(BF)


def update_kernel(sum_ref, ws_ref, wn_ref, new_s_ref, new_n_ref):
    peers, share = sum_ref.shape[0], sum_ref.shape[1] // 2
    left = sum_ref[:, :share, :].astype(F32).reshape(peers * share, TILE)
    right = sum_ref[:, share:, :].astype(F32).reshape(peers * share, TILE)
    total = jnp.concatenate([left, right], axis=1)
    norm = jnp.sqrt(jnp.sum(total * total, keepdims=True))
    scale = 8.0 * jnp.minimum(1.0, 1.0 / norm)
    half = new_s_ref.shape[0]
    new_s_ref[...] = ws_ref[...].astype(F32) - scale * total[:half]
    new_n_ref[...] = wn_ref[...].astype(F32) - scale * total[half:]


SMEM = pl.BlockSpec(memory_space=pltpu.SMEM)
VMEM = pl.BlockSpec(memory_space=pltpu.VMEM)


def call(kernel, name, smem, args, outs, scratch=(), flops=10**9):
    size = sum(a.size * a.dtype.itemsize for a in args)
    return pl.pallas_call(
        kernel,
        name=name,
        in_specs=[SMEM] * smem + [VMEM] * (len(args) - smem),
        out_specs=[VMEM] * len(outs),
        out_shape=outs,
        scratch_shapes=list(scratch),
        compiler_params=pltpu.CompilerParams(vmem_limit_bytes=VMEM_BYTES),
        cost_estimate=pl.CostEstimate(flops=flops, bytes_accessed=size, transcendentals=0),
    )(*args)


def shape(dims, dtype=BF):
    return jax.ShapeDtypeStruct(dims, dtype)


def scatter(slot_counts, rows, edge_src, edge_slot, feats):
    peers, cap = rows.shape
    slots = peers * cap
    return call(
        scatter_kernel,
        "scatter",
        1,
        (slot_counts, rows, edge_src, edge_slot, feats),
        [shape((peers, 2 * cap + INDEX_ROWS, TILE))],
        [pltpu.VMEM((slots, feats.shape[0]), BF)],
    )[0]


def adjacency(edge_src, edge_slot, verts, slots):
    return call(
        adjacency_kernel, "adjacency", 0, (edge_src, edge_slot), [shape((verts, slots))], flops=6 * 10**9
    )[0]


def masters(cap, ages, got, feats, stale, cot, ws, wn):
    verts, width = feats.shape
    peers = got.shape[0]
    share = 2 * width // peers
    return call(
        functools.partial(master_kernel, cap),
        "masters",
        1,
        (ages, got, feats, stale, cot, ws, wn),
        [shape((verts, width)), shape((verts, width)), shape((peers, 2 * cap + 2 * share, TILE))],
        [pltpu.VMEM((verts, width), BF), pltpu.VMEM((peers * cap, width), BF)],
    )


def back(cap, slot_counts, got, adj, gp, ws):
    return call(
        functools.partial(back_kernel, cap),
        "back",
        1,
        (slot_counts, got, adj, gp, ws),
        [shape(gp.shape)],
        [pltpu.VMEM((got.shape[0] * cap, gp.shape[1]), BF)],
    )[0]


def update(sums, ws, wn):
    return call(update_kernel, "update", 0, (sums, ws, wn), [shape(ws.shape, F32)] * 2)


def exchange(x):
    return lax.all_to_all(x, "dom", split_axis=0, concat_axis=0, tiled=True)


def body(
    feats, edge_src, edge_slot, slot_counts, replica_row, stale_agg, bin_ages, cotangent, w_self, w_neigh
):
    verts, width = feats.shape
    peers, cap = replica_row.shape[1:]
    arrived = exchange(scatter(slot_counts, replica_row[0], edge_src, edge_slot, feats))
    adj = adjacency(edge_src, edge_slot, verts, peers * cap)
    age_factor = 1.0 / (1.0 + bin_ages.astype(F32))
    hidden, grad_pre, outgoing = masters(
        cap, age_factor, arrived, feats, stale_agg, cotangent, w_self, w_neigh
    )
    returned = exchange(outgoing)
    partial = jnp.sum(returned[:, 2 * cap :, :].astype(F32), axis=0)
    groups = lax.axis_size("group")
    if groups & (groups - 1):
        partial = lax.psum(partial, "group")
    else:
        step = 1
        while step < groups:
            pairs = [(k, k ^ (2 * step - 1)) for k in range(groups)]
            partial = partial + lax.ppermute(partial, "group", pairs)
            step *= 2
    share = partial.astype(BF)
    sums = exchange(jnp.broadcast_to(share[None], (peers,) + share.shape))
    feat_grad = back(cap, slot_counts, returned, adj, grad_pre, w_self)
    new_self, new_neigh = update(sums, w_self, w_neigh)
    return (hidden, feat_grad, new_self, new_neigh)


def solution(mesh):
    both = ("group", "dom")
    wide = P(both, None)
    placed = (wide, wide, wide, wide, P(both, None, None), wide, P(both), wide, P(), P())
    return jax.shard_map(
        body,
        mesh=mesh,
        in_specs=placed,
        out_specs=(wide, wide, P(), P()),
        check_vma=False,
    )
```

time: 241 us -> 111 us (0.46)
  waiting for transfers between devices: 143 us -> 17.4 us
  Pallas kernels: 0 us -> 41.7 us
  matrix products: 37.5 us -> 0 us
  blocking collectives: 0 us -> 20.7 us
  between operations: 15.6 us -> 0.71 us
  other arithmetic: 9.25 us -> 0.72 us
  local copies, waits for them, and re-layouts: 14.5 us -> 9.13 us
    psum x1 -> x0, waiting for transfers between devices: 134 us -> none  [body(): lax.psum((grad_self, grad_neigh), ('group', 'dom'))]
    pallas_call x0 -> x5, Pallas kernels: none -> 41.7 us  [call(): pl.pallas_call(kernel, name=name, in_specs=[SMEM] * smem + [VMEM] * (len(...]
    dot_general x11 -> x0, matrix products: 37.5 us -> none  [the longest x1 10.6 us: body(): lax.dot_general(slot_indicator, edge_feats, contraction_row_dims, preferr...]
    all_to_all x0 -> x1, blocking collectives: none -> 20.7 us  [exchange(): return lax.all_to_all(x, 'dom', split_axis=0, concat_axis=0, tiled=True)]
    all_to_all x3 -> x2, starting transfers between devices: 20.4 us -> 14.5 us  [exchange(): return lax.all_to_all(x, 'dom', split_axis=0, concat_axis=0, tiled=True)]
    all_to_all x3 -> x2, waiting for transfers between devices: 9.26 us -> 15.1 us  [exchange(): return lax.all_to_all(x, 'dom', split_axis=0, concat_axis=0, tiled=True)]
    gather x1 -> x0, local copies, waits for them, and re-layouts: 5.36 us -> none  [body(): outgoing = grad_agg[master_flat].reshape(dom_size, capacity, width)]
    ppermute x0 -> x2, starting transfers between devices: none -> 5.29 us  [body(): partial = partial + lax.ppermute(partial, 'group', pairs)]
  transfers between devices with their start and end apart: 4 -> 4, of which waited for: 2 -> 3; matrix products, arithmetic and copies ran while one was open for 15% -> 1% of each run, Pallas kernels for 0% -> 16%
where the time goes in v1:
time: 111 us; the launch traced here: 110 us
  Pallas kernels  41.7 us (38%)
  blocking collectives  20.7 us (19%)
  starting transfers between devices  19.8 us (18%)
  waiting for transfers between devices  17.4 us (16%)
  local copies, waits for them, and re-layouts  9.13 us (8%)
    pallas_call x5, Pallas kernels, call(): pl.pallas_call(kernel, name=name, in_specs=[SMEM] * smem + [VMEM] * (len(...  41.7 us
    all_to_all x1, blocking collectives, exchange(): return lax.all_to_all(x, 'dom', split_axis=0, concat_axis=0, tiled=True)  20.7 us
    all_to_all x2, waiting for transfers between devices, exchange(): return lax.all_to_all(x, 'dom', split_axis=0, concat_axis=0, tiled=True)  15.1 us
    all_to_all x2, starting transfers between devices, exchange(): return lax.all_to_all(x, 'dom', split_axis=0, concat_axis=0, tiled=True)  14.5 us
    unnamed x28, local copies, waits for them, and re-layouts  8.39 us
    ppermute x2, starting transfers between devices, body(): partial = partial + lax.ppermute(partial, 'group', pairs)  5.29 us
    ppermute x2, waiting for transfers between devices, body(): partial = partial + lax.ppermute(partial, 'group', pairs)  2.26 us
  transfers between devices with their start and end apart: 4, of which 3 were waited for; matrix products, arithmetic and copies ran while one was open for 1% of the time, Pallas kernels for 16%

profile of v1, /device:TPU:1, one launch (start us, length us, event | category | flops | bytes accessed | tf_op | source)
XLA Modules:
  0.0 110.1 jit_solution(14628189394281139963)
XLA Ops:
  0.6 0.0 copy-start
  0.6 1.2 %copy-done = bf16[2048,256]{1,0:T(8,128)(2,1)S(1)} copy-done((bf16[2048,256]{1,0:T(8,128)(2,1)S(1)}, bf16[2048,256]{1,0:T(8,128)(2,1)}, u32[]{:S(2)}) %copy-start) | copy-done | bytes 1048600
  1.9 0.0 copy-start.7
  1.9 0.7 copy-done.7
  2.5 0.0 copy-start.9
  2.5 0.8 copy-done.9
  3.3 0.0 copy-start.11
  3.3 0.8 copy-done.11
  4.0 0.0 copy-start.13
  4.0 0.7 copy-done.13
  4.8 0.0 copy-start.10
  4.8 0.0 copy-start.12
  4.8 12.6 %scatter.1 = bf16[32,112,128]{2,1,0:T(8,128)(2,1)} custom-call(s32[1,32]{1,0:T(1,128)S(1)} %copy-done.7, s32[32,48]{1,0:T(8,128)S(1)} %bitcast.1, s32[1,8192]{1,0:T(1,128)S(1)} %copy-done.9, s32[1,8192]{1,0:T(1,128)S(1)} %copy-done.11, bf16[2048,256]{1,0:T(8,128)(2,1)S(1)} %copy-done), custom_call_target="tpu_custom_call" | custom-call | flops 1000000000 | bytes 1120384 | tf_op jit(solution)/shard_map/scatter/pallas_call | solution.py:212
  17.3 8.6 %all-to-all-start = ((bf16[32,112,128]{2,1,0:T(8,128)(2,1)}), bf16[32,112,128]{2,1,0:T(8,128)(2,1)S(1)}, u32[]{:S(2)}, u32[]{:S(2)}) async-start(bf16[32,112,128]{2,1,0:T(8,128)(2,1)} %scatter.1), calls=%async_computation | async-start | bytes 1835008 | tf_op jit(solution)/shard_map/all_to_all | solution.py:277
  25.9 0.7 add_divide_fusion.ages_ref
  26.6 15.1 %all-to-all-done.got_ref = bf16[32,112,128]{2,1,0:T(8,128)(2,1)S(1)} async-done(((bf16[32,112,128]{2,1,0:T(8,128)(2,1)}), bf16[32,112,128]{2,1,0:T(8,128)(2,1)S(1)}, u32[]{:S(2)}, u32[]{:S(2)}) %all-to-all-start) | async-done | bytes 917536 | tf_op jit(solution)/shard_map/all_to_all | solution.py:277
  41.7 0.0 copy-start.1
  41.7 1.2 %copy-done.1 = bf16[2048,256]{1,0:T(8,128)(2,1)S(1)} copy-done((bf16[2048,256]{1,0:T(8,128)(2,1)S(1)}, bf16[2048,256]{1,0:T(8,128)(2,1)}, u32[]{:S(2)}) %copy-start.1) | copy-done | bytes 1048600
  42.9 0.0 copy-start.2
  42.9 1.2 %copy-done.2 = bf16[2048,256]{1,0:T(8,128)(2,1)S(1)} copy-done((bf16[2048,256]{1,0:T(8,128)(2,1)S(1)}, bf16[2048,256]{1,0:T(8,128)(2,1)}, u32[]{:S(2)}) %copy-start.2) | copy-done | bytes 1048600
  44.1 0.0 copy-start.3
  44.1 0.9 copy-done.3
  45.0 0.0 copy-start.5
  45.0 0.9 copy-done.5
  45.9 10.0 %masters.1 = (bf16[2048,256]{1,0:T(8,128)(2,1)}, bf16[2048,256]{1,0:T(8,128)(2,1)S(1)}, bf16[32,128,128]{2,1,0:T(8,128)(2,1)S(1)}) custom-call(f32[16]{0:T(128)S(1)} %add_divide_fusion.ages_ref, bf16[32,112,128]{2,1,0:T(8,128)(2,1)S(1)} %all-to-all-done.got_ref, bf16[2048,256]{1,0:T(8,128)(2,1)S(1)} %copy-done.1, bf16[2048,256]{1,0:T(8,128)(2,1)S(1)} %copy-done.2, ...), custom_call_target="tpu_custom_call" | custom-call | flops 1000000000 | bytes 4325440 | tf_op jit(solution)/shard_map/masters/pallas_call | solution.py:212
  55.9 20.7 %all_to_all.15.got_ref = bf16[32,128,128]{2,1,0:T(8,128)(2,1)S(1)} all-to-all(bf16[32,128,128]{2,1,0:T(8,128)(2,1)S(1)} %get-tuple-element.10), channel_id=1, replica_groups=mesh['group'=4,'dom'=32] {'dom'}, dimensions={0} | all-to-all | bytes 2097152 | tf_op jit(solution)/shard_map/all_to_all | solution.py:277
  76.7 1.7 %collective-permute-start = (f32[32,128]{1,0:T(8,128)S(1)}, f32[32,128]{1,0:T(8,128)S(1)}, u32[]{:S(2)}, u32[]{:S(2)}) collective-permute-start(f32[32,128]{1,0:T(8,128)S(1)} %convert_reduce_fusion), channel_id=1, source_target_pairs={{0,32},{32,0},{64,96},{96,64},{1,33},{33,1},{65,97},{97,65},{2,34}... | collective-permute-start | bytes 49160 | tf_op jit(solution)/shard_map/ppermute | solution.py:300
  78.4 1.1 %collective-permute-done = f32[32,128]{1,0:T(8,128)S(1)} collective-permute-done((f32[32,128]{1,0:T(8,128)S(1)}, f32[32,128]{1,0:T(8,128)S(1)}, u32[]{:S(2)}, u32[]{:S(2)}) %collective-permute-start) | collective-permute-done | bytes 16416 | tf_op jit(solution)/shard_map/ppermute | solution.py:300
  79.5 3.6 %collective-permute-start.1 = (f32[32,128]{1,0:T(8,128)S(1)}, f32[32,128]{1,0:T(8,128)S(1)}, u32[]{:S(2)}, u32[]{:S(2)}) collective-permute-start(f32[32,128]{1,0:T(8,128)S(1)} %add.10), channel_id=1, source_target_pairs={{0,96},{32,64},{64,32},{96,0},{1,97},{33,65},{65,33},{97,1},{2,98}... | collective-permute-start | bytes 49160 | tf_op jit(solution)/shard_map/ppermute | solution.py:300
  83.1 1.1 %collective-permute-done.1 = f32[32,128]{1,0:T(8,128)S(1)} collective-permute-done((f32[32,128]{1,0:T(8,128)S(1)}, f32[32,128]{1,0:T(8,128)S(1)}, u32[]{:S(2)}, u32[]{:S(2)}) %collective-permute-start.1) | collective-permute-done | bytes 16416 | tf_op jit(solution)/shard_map/ppermute | solution.py:300
  84.2 0.7 broadcast_in_dim.2
  85.0 5.9 %all-to-all-start.2 = ((bf16[32,32,128]{2,1,0:T(8,128)(2,1)}), bf16[32,32,128]{2,1,0:T(8,128)(2,1)S(1)}, u32[]{:S(2)}, u32[]{:S(2)}) async-start(bf16[32,32,128]{2,1,0:T(8,128)(2,1)} %broadcast_in_dim.2), calls=%async_computation.2 | async-start | bytes 524288 | tf_op jit(solution)/shard_map/all_to_all | solution.py:277
  90.9 0.0 copy-done.10
  90.9 0.0 copy-done.12
  90.9 0.0 copy-start.4
  90.9 0.0 copy-start.8
  91.0 12.1 %adjacency.1.adj_ref = bf16[2048,1536]{1,0:T(8,128)(2,1)} custom-call(s32[1,8192]{1,0:T(1,128)S(1)} %copy-done.10, s32[1,8192]{1,0:T(1,128)S(1)} %copy-done.12), custom_call_target="tpu_custom_call" | custom-call | flops 6000000000 | bytes 65536 | tf_op jit(solution)/shard_map/adjacency/pallas_call | solution.py:212
  103.1 0.0 copy-start.6
  103.1 0.0 copy-done.4
  103.1 0.0 copy-done.8
  103.1 6.0 %back.1 = bf16[2048,256]{1,0:T(8,128)(2,1)} custom-call(s32[1,32]{1,0:T(1,128)S(1)} %copy-done.8, bf16[32,128,128]{2,1,0:T(8,128)(2,1)S(1)} %all_to_all.15.got_ref, bf16[2048,1536]{1,0:T(8,128)(2,1)} %adjacency.1.adj_ref, bf16[2048,256]{1,0:T(8,128)(2,1)S(1)} %get-tuple-element.11.gp_ref, bf16[256,256]{1,0:T(8,128)(2,1)S(1)} %copy-done.4), custom_call_target="tpu_custom_call" | custom-call | flops 1000000000 | bytes 8519808 | tf_op jit(solution)/shard_map/back/pallas_call | solution.py:212
  109.0 0.0 all-to-all-done.2.sum_ref
  109.0 0.0 copy-done.6
  109.0 1.1 update.1
  (3 shorter events, 0.1 us)
Async XLA Ops:
  0.6 1.2 %copy-start = (bf16[2048,256]{1,0:T(8,128)(2,1)S(1)}, bf16[2048,256]{1,0:T(8,128)(2,1)}, u32[]{:S(2)}) copy-start(bf16[2048,256]{1,0:T(8,128)(2,1)} %feats_ref.3) | copy-start | bytes 3145732
  1.9 0.7 copy-start.7
  2.5 0.8 copy-start.9
  3.3 0.8 copy-start.11
  4.0 0.7 copy-start.13
  4.8 86.2 %copy-start.10 = (s32[1,8192]{1,0:T(1,128)S(1)}, s32[1,8192]{1,0:T(1,128)}, u32[]{:S(2)}) copy-start(s32[1,8192]{1,0:T(1,128)} %src_ref.3) | copy-start | bytes 98308
  4.8 86.2 %copy-start.12 = (s32[1,8192]{1,0:T(1,128)S(1)}, s32[1,8192]{1,0:T(1,128)}, u32[]{:S(2)}) copy-start(s32[1,8192]{1,0:T(1,128)} %slot_ref.3) | copy-start | bytes 98308
  17.3 24.4 %all-to-all-start = ((bf16[32,112,128]{2,1,0:T(8,128)(2,1)}), bf16[32,112,128]{2,1,0:T(8,128)(2,1)S(1)}, u32[]{:S(2)}, u32[]{:S(2)}) async-start(bf16[32,112,128]{2,1,0:T(8,128)(2,1)} %scatter.1), calls=%async_computation | async-start | bytes 1835008 | tf_op jit(solution)/shard_map/all_to_all | solution.py:277
  41.7 1.2 %copy-start.1 = (bf16[2048,256]{1,0:T(8,128)(2,1)S(1)}, bf16[2048,256]{1,0:T(8,128)(2,1)}, u32[]{:S(2)}) copy-start(bf16[2048,256]{1,0:T(8,128)(2,1)} %feats_ref.3) | copy-start | bytes 3145732
  42.9 1.2 %copy-start.2 = (bf16[2048,256]{1,0:T(8,128)(2,1)S(1)}, bf16[2048,256]{1,0:T(8,128)(2,1)}, u32[]{:S(2)}) copy-start(bf16[2048,256]{1,0:T(8,128)(2,1)} %stale_ref.1) | copy-start | bytes 3145732
  44.1 0.9 copy-start.3
  45.0 0.9 copy-start.5
  76.7 2.8 %collective-permute-start = (f32[32,128]{1,0:T(8,128)S(1)}, f32[32,128]{1,0:T(8,128)S(1)}, u32[]{:S(2)}, u32[]{:S(2)}) collective-permute-start(f32[32,128]{1,0:T(8,128)S(1)} %convert_reduce_fusion), channel_id=1, source_target_pairs={{0,32},{32,0},{64,96},{96,64},{1,33},{33,1},{65,97},{97,65},{2,34}... | collective-permute-start | bytes 49160 | tf_op jit(solution)/shard_map/ppermute | solution.py:300
  79.5 4.7 %collective-permute-start.1 = (f32[32,128]{1,0:T(8,128)S(1)}, f32[32,128]{1,0:T(8,128)S(1)}, u32[]{:S(2)}, u32[]{:S(2)}) collective-permute-start(f32[32,128]{1,0:T(8,128)S(1)} %add.10), channel_id=1, source_target_pairs={{0,96},{32,64},{64,32},{96,0},{1,97},{33,65},{65,33},{97,1},{2,98}... | collective-permute-start | bytes 49160 | tf_op jit(solution)/shard_map/ppermute | solution.py:300
  85.0 24.1 %all-to-all-start.2 = ((bf16[32,32,128]{2,1,0:T(8,128)(2,1)}), bf16[32,32,128]{2,1,0:T(8,128)(2,1)S(1)}, u32[]{:S(2)}, u32[]{:S(2)}) async-start(bf16[32,32,128]{2,1,0:T(8,128)(2,1)} %broadcast_in_dim.2), calls=%async_computation.2 | async-start | bytes 524288 | tf_op jit(solution)/shard_map/all_to_all | solution.py:277
  90.9 12.1 %copy-start.4 = (bf16[256,256]{1,0:T(8,128)(2,1)S(1)}, bf16[256,256]{1,0:T(8,128)(2,1)}, u32[]{:S(2)}) copy-start(bf16[256,256]{1,0:T(8,128)(2,1)} %ws_ref.5) | copy-start | bytes 393220
  90.9 12.1 %copy-start.8 = (s32[1,32]{1,0:T(1,128)S(1)}, s32[1,32]{1,0:T(1,128)}, u32[]{:S(2)}) copy-start(s32[1,32]{1,0:T(1,128)} %counts_ref.3) | copy-start | bytes 388
  103.1 6.0 %copy-start.6 = (bf16[256,256]{1,0:T(8,128)(2,1)S(1)}, bf16[256,256]{1,0:T(8,128)(2,1)}, u32[]{:S(2)}) copy-start(bf16[256,256]{1,0:T(8,128)(2,1)} %wn_ref.3) | copy-start | bytes 393220

commit v2 on v1

v2 whole, which is shorter than its diff:
```python
import functools

import jax
import jax.numpy as jnp
from jax import lax
from jax.experimental import pallas as pl
from jax.experimental.pallas import tpu as pltpu
from jax.sharding import PartitionSpec as P

BF = jnp.bfloat16
F8 = jnp.float8_e4m3fn
F32 = jnp.float32
TILE = 128
ROWS = 512
INDEX_ROWS = 16
NN = (((1,), (0,)), ((), ()))
NT = (((1,), (1,)), ((), ()))
TN = (((0,), (0,)), ((), ()))
MIB = 1024 * 1024


def dot(a, b, dims):
    return lax.dot_general(a, b, dims, preferred_element_type=F32)


def mask(cond):
    return jnp.where(cond, 1.0, 0.0).astype(BF)


def start_all(pairs, sems):
    copies = [pltpu.make_async_copy(src, dst, sems.at[k]) for k, (src, dst) in enumerate(pairs)]
    for copy in copies:
        copy.start()
    return copies


def bin_edges(ref, b, bins, repeats):
    return jnp.concatenate(
        [ref[:, (g * bins + b) * TILE : (g * bins + b + 1) * TILE] for g in range(repeats)], axis=1
    )


def bin_indicators(src_ref, slot_ref, b, bins, repeats, slots):
    src = bin_edges(src_ref, b, bins, repeats) & (TILE - 1)
    slot = bin_edges(slot_ref, b, bins, repeats)
    row = lax.broadcasted_iota(jnp.int32, (TILE, src.shape[1]), 0)
    source = mask(row == src).astype(F8)
    low = mask(row == (slot & (TILE - 1)))
    high = slot >> 7
    return source, [(low * mask(high == h)).astype(F8) for h in range(slots // TILE)]


def scatter_kernel(
    counts_hbm, rows_hbm, src_hbm, slot_hbm, feats_hbm, out_ref, adj_ref, counts_ref, rows_ref, src_ref, slot_ref, feats_ref, sems
):
    copies = start_all(
        [
            (src_hbm, src_ref),
            (slot_hbm, slot_ref),
            (feats_hbm, feats_ref),
            (rows_hbm, rows_ref),
            (counts_hbm, counts_ref),
        ],
        sems,
    )
    slots, verts = adj_ref.shape
    peers, cap = rows_ref.shape[1:]
    bins = verts // TILE
    repeats = src_ref.shape[1] // verts
    copies[0].wait()
    copies[1].wait()
    for b in range(bins):
        source, blocks = bin_indicators(src_ref, slot_ref, b, bins, repeats, slots)
        for h, block in enumerate(blocks):
            adj_ref[h * TILE : (h + 1) * TILE, b * TILE : (b + 1) * TILE] = dot(block, source, NT).astype(BF)
    for copy in copies[2:]:
        copy.wait()
    sub = lax.broadcasted_iota(jnp.int32, (INDEX_ROWS, cap), 0)
    slot_in_peer = lax.broadcasted_iota(jnp.int32, (cap, 2 * TILE), 0)
    step = 8
    for first in range(0, peers, step):
        rows = dot(adj_ref[first * cap : (first + step) * cap, :], feats_ref[...], NN)
        for q in range(first, first + step):
            part = rows[(q - first) * cap : (q - first + 1) * cap, :]
            part = jnp.where(slot_in_peer < counts_ref[0, q], part, 0.0).astype(BF)
            out_ref[q, 0:cap, :] = part[:, :TILE]
            out_ref[q, cap : 2 * cap, :] = part[:, TILE:]
            out_ref[q, 2 * cap :, :] = jnp.zeros((INDEX_ROWS, TILE), BF)
            index = rows_ref[0, q : q + 1, :]
            value = jnp.where(sub == 0, index >> 7, jnp.where(sub == 1, index & (TILE - 1), 0))
            out_ref[q, 2 * cap :, 0:cap] = value.astype(F32).astype(BF)


def adjacency_kernel(src_hbm, slot_hbm, out_hbm, src_ref, slot_ref, adj_ref, sems, out_sems):
    copies = start_all([(src_hbm, src_ref), (slot_hbm, slot_ref)], sems)
    verts, slots = adj_ref.shape
    bins = verts // TILE
    repeats = src_ref.shape[1] // verts
    for copy in copies:
        copy.wait()
    outs = []
    per = ROWS // TILE
    for b in range(bins):
        source, blocks = bin_indicators(src_ref, slot_ref, b, bins, repeats, slots)
        for h, block in enumerate(blocks):
            adj_ref[b * TILE : (b + 1) * TILE, h * TILE : (h + 1) * TILE] = dot(source, block, NT).astype(BF)
        if b % per == per - 1:
            rows = pl.ds((b // per) * ROWS, ROWS)
            copy = pltpu.make_async_copy(adj_ref.at[rows], out_hbm.at[rows], out_sems.at[b // per])
            copy.start()
            outs.append(copy)
    for copy in outs:
        copy.wait()


def master_kernel(
    cap,
    got_ref,
    adj_hbm,
    ages_hbm,
    feats_hbm,
    stale_hbm,
    cot_hbm,
    ws_hbm,
    wn_hbm,
    hidden_hbm,
    gp_ref,
    out_ref,
    ages_ref,
    feats_ref,
    stale_ref,
    cot_ref,
    ws_ref,
    wn_ref,
    hidden_ref,
    ga_ref,
    arr_ref,
    sems,
    out_sems,
):
    copies = start_all(
        [
            (ages_hbm, ages_ref),
            (stale_hbm, stale_ref),
            (feats_hbm, feats_ref),
            (ws_hbm, ws_ref),
            (wn_hbm, wn_ref),
            (cot_hbm, cot_ref),
        ],
        sems,
    )
    verts, width = feats_ref.shape
    peers = got_ref.shape[0]
    slots = peers * cap
    arr_ref[:, :TILE] = got_ref[:, 0:cap, :].reshape(slots, TILE)
    arr_ref[:, TILE:] = got_ref[:, cap : 2 * cap, :].reshape(slots, TILE)
    coded = got_ref[:, 2 * cap :, :].reshape(peers * INDEX_ROWS, TILE)
    pick_row = lax.broadcasted_iota(jnp.int32, (peers, peers * INDEX_ROWS), 1)
    pick_peer = lax.broadcasted_iota(jnp.int32, (peers, peers * INDEX_ROWS), 0) * INDEX_ROWS
    high = dot(mask(pick_row == pick_peer), coded, NN).astype(BF)
    low = dot(mask(pick_row == pick_peer + 1), coded, NN).astype(BF)
    place = lax.broadcasted_iota(jnp.int32, (peers, cap, TILE), 1).reshape(slots, TILE)
    peer = lax.broadcasted_iota(jnp.int32, (peers, cap, TILE), 0).reshape(slots, TILE)
    lane = lax.broadcasted_iota(jnp.int32, (slots, TILE), 1)
    at_place = place == lane
    at_peer = mask(peer == lane)[:, :peers]
    value_c = dot(at_peer, high, NN) * float(TILE) + dot(at_peer, low, NN)
    col_index = jnp.sum(jnp.where(at_place, value_c, 0.0), axis=1, keepdims=True).astype(jnp.int32)
    spread = mask(at_place)
    value = dot(high, spread, NT) * float(TILE) + dot(low, spread, NT)
    slot = lax.broadcasted_iota(jnp.int32, (peers, slots), 1)
    least = lax.broadcasted_iota(jnp.int32, (peers, slots), 0) * cap
    own = (slot >= least) & (slot < least + cap)
    row_index = jnp.sum(jnp.where(own, value, 0.0), axis=0, keepdims=True).astype(jnp.int32)

    sub = lax.broadcasted_iota(jnp.int32, (TILE, slots), 0)
    low_hot = mask(sub == (row_index & (TILE - 1)))
    row_high = row_index >> 7
    total = None
    outs = []
    per = ROWS // TILE
    for block in range(verts // ROWS):
        rows = slice(block * ROWS, (block + 1) * ROWS)
        hot = jnp.concatenate([low_hot * mask(row_high == block * per + k) for k in range(per)], axis=0)
        agg = dot(hot, arr_ref[...], NN)
        if block == 0:
            copies[0].wait()
            copies[1].wait()
        aged = []
        for k in range(block * per, (block + 1) * per):
            age = jnp.full((1, width), ages_ref[k], jnp.int32).astype(F32)
            aged.append(stale_ref[k * TILE : (k + 1) * TILE, :].astype(F32) * (1.0 / (1.0 + age)))
        agg = agg + jnp.concatenate(aged, axis=0)
        inverse = lax.rsqrt(jnp.mean(agg * agg, axis=1, keepdims=True) + 1e-05)
        normed = (agg * inverse).astype(BF)
        if block == 0:
            for copy in copies[2:]:
                copy.wait()
        feats = feats_ref[rows, :]
        pre = dot(feats, ws_ref[...], NN) + dot(normed, wn_ref[...], NN)
        sig = jax.nn.sigmoid(pre)
        hidden_ref[rows, :] = (pre * sig).astype(BF)
        gp = (cot_ref[rows, :].astype(F32) * sig * (1.0 + pre * (1.0 - sig))).astype(BF)
        gp_ref[rows, :] = gp
        part = pl.ds(block * ROWS, ROWS)
        copy = pltpu.make_async_copy(hidden_ref.at[part], hidden_hbm.at[part], out_sems.at[block])
        copy.start()
        outs.append(copy)
        grads = jnp.concatenate([dot(feats, gp, TN), dot(normed, gp, TN)], axis=0)
        total = grads if total is None else total + grads
        gn = dot(gp, wn_ref[...], NT)
        inner = jnp.mean(gn * agg, axis=1, keepdims=True)
        ga_ref[rows, :] = (inverse * (gn - agg * (inverse * inverse * inner))).astype(BF)
    total = total.astype(BF)
    share = 2 * width // peers
    out_ref[:, 2 * cap : 2 * cap + share, :] = total[:, :TILE].reshape(peers, share, TILE)
    out_ref[:, 2 * cap + share :, :] = total[:, TILE:].reshape(peers, share, TILE)
    step = 8
    for first in range(0, peers, step):
        part = slice(first * cap, (first + step) * cap)
        lanes = lax.broadcasted_iota(jnp.int32, (step * cap, verts), 1)
        rows = dot(mask(lanes == col_index[part, :]), ga_ref[...], NN).astype(BF)
        out_ref[first : first + step, 0:cap, :] = rows[:, :TILE].reshape(step, cap, TILE)
        out_ref[first : first + step, cap : 2 * cap, :] = rows[:, TILE:].reshape(step, cap, TILE)
    for copy in outs:
        copy.wait()


def back_kernel(cap, got_ref, gp_ref, counts_hbm, adj_hbm, ws_hbm, out_hbm, counts_ref, adj_ref, ws_ref, grad_ref, out_ref, sems, out_sems):
    verts = out_ref.shape[0]
    blocks = verts // ROWS
    pairs = [(counts_hbm, counts_ref), (ws_hbm, ws_ref)]
    for block in range(blocks):
        part = pl.ds(block * ROWS, ROWS)
        pairs.append((adj_hbm.at[part], adj_ref.at[part]))
    copies = start_all(pairs, sems)
    peers = got_ref.shape[0]
    copies[0].wait()
    copies[1].wait()
    slot_in_peer = lax.broadcasted_iota(jnp.int32, (cap, TILE), 0)
    for q in range(peers):
        live = slot_in_peer < counts_ref[0, q]
        for half in range(2):
            rows = got_ref[q, half * cap : (half + 1) * cap, :]
            grad_ref[q * cap : (q + 1) * cap, half * TILE : (half + 1) * TILE] = jnp.where(
                live, rows.astype(F32), 0.0
            ).astype(BF)
    outs = []
    for block in range(blocks):
        rows = slice(block * ROWS, (block + 1) * ROWS)
        own = dot(gp_ref[rows, :], ws_ref[...], NT)
        copies[2 + block].wait()
        out_ref[rows, :] = (dot(adj_ref[rows, :], grad_ref[...], NN) + own).astype(BF)
        part = pl.ds(block * ROWS, ROWS)
        copy = pltpu.make_async_copy(out_ref.at[part], out_hbm.at[part], out_sems.at[block])
        copy.start()
        outs.append(copy)
    for copy in outs:
        copy.wait()


def update_kernel(sum_ref, ws_ref, wn_ref, new_s_ref, new_n_ref):
    peers, share = sum_ref.shape[0], sum_ref.shape[1] // 2
    left = sum_ref[:, :share, :].astype(F32).reshape(peers * share, TILE)
    right = sum_ref[:, share:, :].astype(F32).reshape(peers * share, TILE)
    total = jnp.concatenate([left, right], axis=1)
    norm = jnp.sqrt(jnp.sum(total * total, keepdims=True))
    scale = 8.0 * jnp.minimum(1.0, 1.0 / norm)
    half = new_s_ref.shape[0]
    new_s_ref[...] = ws_ref[...].astype(F32) - scale * total[:half]
    new_n_ref[...] = wn_ref[...].astype(F32) - scale * total[half:]


HBM = pl.BlockSpec(memory_space=pltpu.HBM)
VMEM = pl.BlockSpec(memory_space=pltpu.VMEM)


def call(kernel, name, args, near, outs, out_near, scratch=(), flops=10**9, limit=56):
    size = sum(a.size * a.dtype.itemsize for a in args)
    return pl.pallas_call(
        kernel,
        name=name,
        in_specs=[VMEM if k < near else HBM for k in range(len(args))],
        out_specs=[VMEM if k in out_near else HBM for k in range(len(outs))],
        out_shape=outs,
        scratch_shapes=list(scratch),
        compiler_params=pltpu.CompilerParams(vmem_limit_bytes=limit * MIB),
        cost_estimate=pl.CostEstimate(flops=flops, bytes_accessed=size, transcendentals=0),
    )(*args)


def shape(dims, dtype=BF):
    return jax.ShapeDtypeStruct(dims, dtype)


def like(x):
    return pltpu.VMEM(x.shape, x.dtype)


def scatter(slot_counts, replica_row, edge_src, edge_slot, feats):
    peers, cap = replica_row.shape[1:]
    return call(
        scatter_kernel,
        "scatter",
        (slot_counts, replica_row, edge_src, edge_slot, feats),
        0,
        [shape((peers, 2 * cap + INDEX_ROWS, TILE))],
        (0,),
        [
            pltpu.VMEM((peers * cap, feats.shape[0]), BF),
            pltpu.SMEM(slot_counts.shape, jnp.int32),
            like(replica_row),
            like(edge_src),
            like(edge_slot),
            like(feats),
            pltpu.SemaphoreType.DMA((5,)),
        ],
    )[0]


def adjacency(edge_src, edge_slot, verts, slots):
    return call(
        adjacency_kernel,
        "adjacency",
        (edge_src, edge_slot),
        0,
        [shape((verts, slots))],
        (),
        [
            like(edge_src),
            like(edge_slot),
            pltpu.VMEM((verts, slots), BF),
            pltpu.SemaphoreType.DMA((2,)),
            pltpu.SemaphoreType.DMA((verts // ROWS,)),
        ],
        flops=6 * 10**9,
    )[0]


def masters(cap, got, adj, ages, feats, stale, cot, ws, wn):
    verts, width = feats.shape
    peers = got.shape[0]
    share = 2 * width // peers
    return call(
        functools.partial(master_kernel, cap),
        "masters",
        (got, adj, ages, feats, stale, cot, ws, wn),
        1,
        [shape((verts, width)), shape((verts, width)), shape((peers, 2 * cap + 2 * share, TILE))],
        (1, 2),
        [
            pltpu.SMEM(ages.shape, jnp.int32),
            like(feats),
            like(stale),
            like(cot),
            like(ws),
            like(wn),
            like(feats),
            like(feats),
            pltpu.VMEM((peers * cap, width), BF),
            pltpu.SemaphoreType.DMA((6,)),
            pltpu.SemaphoreType.DMA((verts // ROWS,)),
        ],
    )


def back(cap, got, gp, slot_counts, adj, ws):
    blocks = gp.shape[0] // ROWS
    return call(
        functools.partial(back_kernel, cap),
        "back",
        (got, gp, slot_counts, adj, ws),
        2,
        [shape(gp.shape)],
        (),
        [
            pltpu.SMEM(slot_counts.shape, jnp.int32),
            like(adj),
            like(ws),
            pltpu.VMEM((got.shape[0] * cap, gp.shape[1]), BF),
            like(gp),
            pltpu.SemaphoreType.DMA((2 + blocks,)),
            pltpu.SemaphoreType.DMA((blocks,)),
        ],
    )[0]


def update(sums, ws, wn):
    return call(update_kernel, "update", (sums, ws, wn), 3, [shape(ws.shape, F32)] * 2, (0, 1))


def exchange(x):
    return lax.all_to_all(x, "dom", split_axis=0, concat_axis=0, tiled=True)


def body(
    feats, edge_src, edge_slot, slot_counts, replica_row, stale_agg, bin_ages, cotangent, w_self, w_neigh
):
    verts, width = feats.shape
    peers, cap = replica_row.shape[1:]
    arrived = exchange(scatter(slot_counts, replica_row, edge_src, edge_slot, feats))
    adj = adjacency(edge_src, edge_slot, verts, peers * cap)
    hidden, grad_pre, outgoing = masters(
        cap, arrived, adj, bin_ages, feats, stale_agg, cotangent, w_self, w_neigh
    )
    returned = exchange(outgoing)
    partial = jnp.sum(returned[:, 2 * cap :, :].astype(F32), axis=0)
    groups = lax.axis_size("group")
    step = 1
    while step < groups:
        pairs = [(k, k ^ (2 * step - 1)) for k in range(groups)]
        partial = partial + lax.ppermute(partial, "group", pairs)
        step *= 2
    share = partial.astype(BF)
    sums = exchange(jnp.broadcast_to(share[None], (peers,) + share.shape))
    feat_grad = back(cap, returned, grad_pre, slot_counts, adj, w_self)
    new_self, new_neigh = update(sums, w_self, w_neigh)
    return (hidden, feat_grad, new_self, new_neigh)


def solution(mesh):
    both = ("group", "dom")
    wide = P(both, None)
    placed = (wide, wide, wide, wide, P(both, None, None), wide, P(both), wide, P(), P())
    return jax.shard_map(
        body,
        mesh=mesh,
        in_specs=placed,
        out_specs=(wide, wide, P(), P()),
        check_vma=False,
    )
```

time: 111 us -> 93.5 us (0.84)
  Pallas kernels: 41.7 us -> 34.8 us
  local copies, waits for them, and re-layouts: 9.13 us -> 2.38 us
  waiting for transfers between devices: 17.4 us -> 13.7 us
    pallas_call x5, Pallas kernels: 41.7 us -> 34.8 us  [call(): pl.pallas_call(kernel, name=name, in_specs=[VMEM if k < near else HBM for...]
    unnamed x28 -> x6, local copies, waits for them, and re-layouts: 8.39 us -> 1.64 us
    all_to_all x2, waiting for transfers between devices: 15.1 us -> 11.5 us  [exchange(): return lax.all_to_all(x, 'dom', split_axis=0, concat_axis=0, tiled=True)]
  transfers between devices with their start and end apart: 4 -> 4, of which waited for: 3 -> 4; matrix products, arithmetic and copies ran while one was open for 1% -> 0% of each run, Pallas kernels for 16% -> 14%
where the time goes in v2:
time: 93.5 us; the launch traced here: 93 us
  Pallas kernels  34.8 us (37%)
  blocking collectives  21.3 us (23%)
  starting transfers between devices  20.1 us (21%)
  waiting for transfers between devices  13.7 us (15%)
  local copies, waits for them, and re-layouts  2.38 us (3%)
    pallas_call x5, Pallas kernels, call(): pl.pallas_call(kernel, name=name, in_specs=[VMEM if k < near else HBM for...  34.8 us
    all_to_all x1, blocking collectives, exchange(): return lax.all_to_all(x, 'dom', split_axis=0, concat_axis=0, tiled=True)  21.3 us
    all_to_all x2, starting transfers between devices, exchange(): return lax.all_to_all(x, 'dom', split_axis=0, concat_axis=0, tiled=True)  14.8 us
    all_to_all x2, waiting for transfers between devices, exchange(): return lax.all_to_all(x, 'dom', split_axis=0, concat_axis=0, tiled=True)  11.5 us
    ppermute x2, starting transfers between devices, body(): partial = partial + lax.ppermute(partial, 'group', pairs)  5.29 us
    ppermute x2, waiting for transfers between devices, body(): partial = partial + lax.ppermute(partial, 'group', pairs)  2.26 us
  transfers between devices with their start and end apart: 4, of which 4 were waited for; matrix products, arithmetic and copies ran while one was open for 0% of the time, Pallas kernels for 14%

profile of v2, /device:TPU:1, one launch (start us, length us, event | category | flops | bytes accessed | tf_op | source)
XLA Modules:
  0.0 93.0 jit_solution(14005726287942860131)
XLA Ops:
  0.6 7.2 %scatter.1 = bf16[32,112,128]{2,1,0:T(8,128)(2,1)} custom-call(s32[1,32]{1,0:T(1,128)} %counts_hbm.3, s32[1,32,48]{2,1,0:T(8,128)} %rows_hbm.1, s32[1,8192]{1,0:T(1,128)} %src_hbm.3, s32[1,8192]{1,0:T(1,128)} %slot_hbm.3, bf16[2048,256]{1,0:T(8,128)(2,1)} %feats_hbm.3), custom_call_target="tpu_custom_call" | custom-call | flops 1000000000 | bytes 1120384 | tf_op jit(solution)/shard_map/scatter/pallas_call | solution.py:280
  7.8 8.6 %all-to-all-start = ((bf16[32,112,128]{2,1,0:T(8,128)(2,1)}), bf16[32,112,128]{2,1,0:T(8,128)(2,1)S(1)}, u32[]{:S(2)}, u32[]{:S(2)}) async-start(bf16[32,112,128]{2,1,0:T(8,128)(2,1)} %scatter.1), calls=%async_computation | async-start | bytes 1835008 | tf_op jit(solution)/shard_map/all_to_all | solution.py:393
  16.5 5.6 %adjacency.1.adj_hbm = bf16[2048,1536]{1,0:T(8,128)(2,1)} custom-call(s32[1,8192]{1,0:T(1,128)} %src_hbm.3, s32[1,8192]{1,0:T(1,128)} %slot_hbm.3), custom_call_target="tpu_custom_call" | custom-call | flops 6000000000 | bytes 65536 | tf_op jit(solution)/shard_map/adjacency/pallas_call | solution.py:280
  22.1 10.2 %all-to-all-done.got_ref = bf16[32,112,128]{2,1,0:T(8,128)(2,1)S(1)} async-done(((bf16[32,112,128]{2,1,0:T(8,128)(2,1)}), bf16[32,112,128]{2,1,0:T(8,128)(2,1)S(1)}, u32[]{:S(2)}, u32[]{:S(2)}) %all-to-all-start) | async-done | bytes 917536 | tf_op jit(solution)/shard_map/all_to_all | solution.py:393
  32.2 0.0 copy-start.1
  32.2 0.9 %copy-done.1 = bf16[32,112,128]{2,1,0:T(8,128)(2,1)} copy-done((bf16[32,112,128]{2,1,0:T(8,128)(2,1)}, bf16[32,112,128]{2,1,0:T(8,128)(2,1)S(1)}, u32[]{:S(2)}) %copy-start.1) | copy-done | bytes 917528
  33.1 12.2 %masters.1 = (bf16[2048,256]{1,0:T(8,128)(2,1)}, bf16[2048,256]{1,0:T(8,128)(2,1)}, bf16[32,128,128]{2,1,0:T(8,128)(2,1)}) custom-call(bf16[32,112,128]{2,1,0:T(8,128)(2,1)} %copy-done.1, bf16[2048,1536]{1,0:T(8,128)(2,1)} %adjacency.1.adj_hbm, s32[16]{0:T(128)} %ages_hbm.1, bf16[2048,256]{1,0:T(8,128)(2,1)} %feats_hbm.3, bf16[2048,256]{1,0:T(8,128)(2,1)} %stale_hbm.1, ...), custom_call_target="tpu_custom_call" | custom-call | flops 1000000000 | bytes 10616896 | tf_op jit(solution)/shard_map/masters/pallas_call | solution.py:280
  45.3 21.3 %all_to_all.15.got_ref = bf16[32,128,128]{2,1,0:T(8,128)(2,1)S(1)} all-to-all(bf16[32,128,128]{2,1,0:T(8,128)(2,1)} %get-tuple-element.10), channel_id=1, replica_groups=mesh['group'=4,'dom'=32] {'dom'}, dimensions={0} | all-to-all | bytes 2097152 | tf_op jit(solution)/shard_map/all_to_all | solution.py:393
  66.6 0.0 copy-start
  66.6 1.7 %collective-permute-start = (f32[32,128]{1,0:T(8,128)S(1)}, f32[32,128]{1,0:T(8,128)S(1)}, u32[]{:S(2)}, u32[]{:S(2)}) collective-permute-start(f32[32,128]{1,0:T(8,128)S(1)} %convert_reduce_fusion), channel_id=1, source_target_pairs={{0,32},{32,0},{64,96},{96,64},{1,33},{33,1},{65,97},{97,65},{2,34}... | collective-permute-start | bytes 49160 | tf_op jit(solution)/shard_map/ppermute | solution.py:412
  68.4 1.1 %collective-permute-done = f32[32,128]{1,0:T(8,128)S(1)} collective-permute-done((f32[32,128]{1,0:T(8,128)S(1)}, f32[32,128]{1,0:T(8,128)S(1)}, u32[]{:S(2)}, u32[]{:S(2)}) %collective-permute-start) | collective-permute-done | bytes 16416 | tf_op jit(solution)/shard_map/ppermute | solution.py:412
  69.5 3.6 %collective-permute-start.1 = (f32[32,128]{1,0:T(8,128)S(1)}, f32[32,128]{1,0:T(8,128)S(1)}, u32[]{:S(2)}, u32[]{:S(2)}) collective-permute-start(f32[32,128]{1,0:T(8,128)S(1)} %add.6), channel_id=1, source_target_pairs={{0,96},{32,64},{64,32},{96,0},{1,97},{33,65},{65,33},{97,1},{2,98}... | collective-permute-start | bytes 49160 | tf_op jit(solution)/shard_map/ppermute | solution.py:412
  73.1 1.1 %collective-permute-done.1 = f32[32,128]{1,0:T(8,128)S(1)} collective-permute-done((f32[32,128]{1,0:T(8,128)S(1)}, f32[32,128]{1,0:T(8,128)S(1)}, u32[]{:S(2)}, u32[]{:S(2)}) %collective-permute-start.1) | collective-permute-done | bytes 16416 | tf_op jit(solution)/shard_map/ppermute | solution.py:412
  74.2 0.7 broadcast_in_dim.2
  74.9 6.2 %all-to-all-start.2 = ((bf16[32,32,128]{2,1,0:T(8,128)(2,1)}), bf16[32,32,128]{2,1,0:T(8,128)(2,1)S(1)}, u32[]{:S(2)}, u32[]{:S(2)}) async-start(bf16[32,32,128]{2,1,0:T(8,128)(2,1)} %broadcast_in_dim.2), calls=%async_computation.2 | async-start | bytes 524288 | tf_op jit(solution)/shard_map/all_to_all | solution.py:393
  81.1 0.0 copy-done
  81.1 7.7 %back.1 = bf16[2048,256]{1,0:T(8,128)(2,1)} custom-call(bf16[32,128,128]{2,1,0:T(8,128)(2,1)} %copy-done, bf16[2048,256]{1,0:T(8,128)(2,1)} %get-tuple-element.11.gp_ref, s32[1,32]{1,0:T(1,128)} %counts_hbm.3, bf16[2048,1536]{1,0:T(8,128)(2,1)} %adjacency.1.adj_hbm, bf16[256,256]{1,0:T(8,128)(2,1)} %ws_ref.1), custom_call_target="tpu_custom_call" | custom-call | flops 1000000000 | bytes 8519808 | tf_op jit(solution)/shard_map/back/pallas_call | solution.py:280
  88.8 1.3 %all-to-all-done.2.sum_ref = bf16[32,32,128]{2,1,0:T(8,128)(2,1)S(1)} async-done(((bf16[32,32,128]{2,1,0:T(8,128)(2,1)}), bf16[32,32,128]{2,1,0:T(8,128)(2,1)S(1)}, u32[]{:S(2)}, u32[]{:S(2)}) %all-to-all-start.2) | async-done | bytes 262176 | tf_op jit(solution)/shard_map/all_to_all | solution.py:393
  90.1 0.0 copy-start.2
  90.1 0.7 copy-done.2
  90.8 2.1 %update.1 = (f32[256,256]{1,0:T(8,128)}, f32[256,256]{1,0:T(8,128)}) custom-call(bf16[32,32,128]{2,1,0:T(8,128)(2,1)} %copy-done.2, bf16[256,256]{1,0:T(8,128)(2,1)} %ws_ref.1, bf16[256,256]{1,0:T(8,128)(2,1)} %wn_ref.1), custom_call_target="tpu_custom_call" | custom-call | flops 1000000000 | bytes 524288 | tf_op jit(solution)/shard_map/update/pallas_call | solution.py:280
  (3 shorter events, 0.1 us)
Async XLA Ops:
  7.8 24.4 %all-to-all-start = ((bf16[32,112,128]{2,1,0:T(8,128)(2,1)}), bf16[32,112,128]{2,1,0:T(8,128)(2,1)S(1)}, u32[]{:S(2)}, u32[]{:S(2)}) async-start(bf16[32,112,128]{2,1,0:T(8,128)(2,1)} %scatter.1), calls=%async_computation | async-start | bytes 1835008 | tf_op jit(solution)/shard_map/all_to_all | solution.py:393
  32.2 0.9 %copy-start.1 = (bf16[32,112,128]{2,1,0:T(8,128)(2,1)}, bf16[32,112,128]{2,1,0:T(8,128)(2,1)S(1)}, u32[]{:S(2)}) copy-start(bf16[32,112,128]{2,1,0:T(8,128)(2,1)S(1)} %all-to-all-done.got_ref) | copy-start | bytes 2752516
  66.6 14.5 %copy-start = (bf16[32,128,128]{2,1,0:T(8,128)(2,1)}, bf16[32,128,128]{2,1,0:T(8,128)(2,1)S(1)}, u32[]{:S(2)}) copy-start(bf16[32,128,128]{2,1,0:T(8,128)(2,1)S(1)} %all_to_all.15.got_ref) | copy-start | bytes 3145732
  66.6 2.8 %collective-permute-start = (f32[32,128]{1,0:T(8,128)S(1)}, f32[32,128]{1,0:T(8,128)S(1)}, u32[]{:S(2)}, u32[]{:S(2)}) collective-permute-start(f32[32,128]{1,0:T(8,128)S(1)} %convert_reduce_fusion), channel_id=1, source_target_pairs={{0,32},{32,0},{64,96},{96,64},{1,33},{33,1},{65,97},{97,65},{2,34}... | collective-permute-start | bytes 49160 | tf_op jit(solution)/shard_map/ppermute | solution.py:412
  69.5 4.7 %collective-permute-start.1 = (f32[32,128]{1,0:T(8,128)S(1)}, f32[32,128]{1,0:T(8,128)S(1)}, u32[]{:S(2)}, u32[]{:S(2)}) collective-permute-start(f32[32,128]{1,0:T(8,128)S(1)} %add.6), channel_id=1, source_target_pairs={{0,96},{32,64},{64,32},{96,0},{1,97},{33,65},{65,33},{97,1},{2,98}... | collective-permute-start | bytes 49160 | tf_op jit(solution)/shard_map/ppermute | solution.py:412
  74.9 15.2 %all-to-all-start.2 = ((bf16[32,32,128]{2,1,0:T(8,128)(2,1)}), bf16[32,32,128]{2,1,0:T(8,128)(2,1)S(1)}, u32[]{:S(2)}, u32[]{:S(2)}) async-start(bf16[32,32,128]{2,1,0:T(8,128)(2,1)} %broadcast_in_dim.2), calls=%async_computation.2 | async-start | bytes 524288 | tf_op jit(solution)/shard_map/all_to_all | solution.py:393
  90.1 0.7 copy-start.2

commit v3 on v2

--- a/solution.py
+++ b/solution.py
@@ -13,6 +13,7 @@
 TILE = 128
 ROWS = 512
 INDEX_ROWS = 16
+GATHER_STEPS = 4
 NN = (((1,), (0,)), ((), ()))
 NT = (((1,), (1,)), ((), ()))
 TN = (((0,), (0,)), ((), ()))
@@ -51,7 +52,7 @@
 
 
 def scatter_kernel(
-    counts_hbm, rows_hbm, src_hbm, slot_hbm, feats_hbm, out_ref, adj_ref, counts_ref, rows_ref, src_ref, slot_ref, feats_ref, sems
+    counts_hbm, rows_hbm, src_hbm, slot_hbm, feats_hbm, out_hbm, out_ref, adj_ref, counts_ref, rows_ref, src_ref, slot_ref, feats_ref, sems, out_sems
 ):
     copies = start_all(
         [
@@ -77,7 +78,8 @@
         copy.wait()
     sub = lax.broadcasted_iota(jnp.int32, (INDEX_ROWS, cap), 0)
     slot_in_peer = lax.broadcasted_iota(jnp.int32, (cap, 2 * TILE), 0)
-    step = 8
+    outs = []
+    step = peers // GATHER_STEPS
     for first in range(0, peers, step):
         rows = dot(adj_ref[first * cap : (first + step) * cap, :], feats_ref[...], NN)
         for q in range(first, first + step):
@@ -89,6 +91,12 @@
             index = rows_ref[0, q : q + 1, :]
             value = jnp.where(sub == 0, index >> 7, jnp.where(sub == 1, index & (TILE - 1), 0))
             out_ref[q, 2 * cap :, 0:cap] = value.astype(F32).astype(BF)
+        those = pl.ds(first, step)
+        copy = pltpu.make_async_copy(out_ref.at[those], out_hbm.at[those], out_sems.at[first // step])
+        copy.start()
+        outs.append(copy)
+    for copy in outs:
+        copy.wait()
 
 
 def adjacency_kernel(src_hbm, slot_hbm, out_hbm, src_ref, slot_ref, adj_ref, sems, out_sems):
@@ -115,7 +123,7 @@
 
 def master_kernel(
     cap,
-    got_ref,
+    got_hbm,
     adj_hbm,
     ages_hbm,
     feats_hbm,
@@ -124,8 +132,10 @@
     ws_hbm,
     wn_hbm,
     hidden_hbm,
-    gp_ref,
-    out_ref,
+    gp_hbm,
+    out_hbm,
+    arr_ref,
+    coded_ref,
     ages_ref,
     feats_ref,
     stale_ref,
@@ -133,13 +143,23 @@
     ws_ref,
     wn_ref,
     hidden_ref,
+    gp_ref,
     ga_ref,
-    arr_ref,
+    back_ref,
+    share_ref,
+    agg_ref,
     sems,
     out_sems,
 ):
+    peers = arr_ref.shape[0]
+    verts, width = feats_ref.shape
+    slots = peers * cap
+    blocks = verts // ROWS
     copies = start_all(
         [
+            (got_hbm.at[:, pl.ds(2 * cap, INDEX_ROWS), :], coded_ref),
+            (got_hbm.at[:, pl.ds(0, cap), :], arr_ref.at[:, :, pl.ds(0, TILE)]),
+            (got_hbm.at[:, pl.ds(cap, cap), :], arr_ref.at[:, :, pl.ds(TILE, TILE)]),
             (ages_hbm, ages_ref),
             (stale_hbm, stale_ref),
             (feats_hbm, feats_ref),
@@ -149,12 +169,8 @@
         ],
         sems,
     )
-    verts, width = feats_ref.shape
-    peers = got_ref.shape[0]
-    slots = peers * cap
-    arr_ref[:, :TILE] = got_ref[:, 0:cap, :].reshape(slots, TILE)
-    arr_ref[:, TILE:] = got_ref[:, cap : 2 * cap, :].reshape(slots, TILE)
-    coded = got_ref[:, 2 * cap :, :].reshape(peers * INDEX_ROWS, TILE)
+    copies[0].wait()
+    coded = coded_ref[...].reshape(peers * INDEX_ROWS, TILE)
     pick_row = lax.broadcasted_iota(jnp.int32, (peers, peers * INDEX_ROWS), 1)
     pick_peer = lax.broadcasted_iota(jnp.int32, (peers, peers * INDEX_ROWS), 0) * INDEX_ROWS
     high = dot(mask(pick_row == pick_peer), coded, NN).astype(BF)
@@ -163,29 +179,38 @@
     peer = lax.broadcasted_iota(jnp.int32, (peers, cap, TILE), 0).reshape(slots, TILE)
     lane = lax.broadcasted_iota(jnp.int32, (slots, TILE), 1)
     at_place = place == lane
-    at_peer = mask(peer == lane)[:, :peers]
-    value_c = dot(at_peer, high, NN) * float(TILE) + dot(at_peer, low, NN)
-    col_index = jnp.sum(jnp.where(at_place, value_c, 0.0), axis=1, keepdims=True).astype(jnp.int32)
     spread = mask(at_place)
     value = dot(high, spread, NT) * float(TILE) + dot(low, spread, NT)
     slot = lax.broadcasted_iota(jnp.int32, (peers, slots), 1)
     least = lax.broadcasted_iota(jnp.int32, (peers, slots), 0) * cap
     own = (slot >= least) & (slot < least + cap)
     row_index = jnp.sum(jnp.where(own, value, 0.0), axis=0, keepdims=True).astype(jnp.int32)
-
     sub = lax.broadcasted_iota(jnp.int32, (TILE, slots), 0)
     low_hot = mask(sub == (row_index & (TILE - 1)))
     row_high = row_index >> 7
+    at_peer = mask(peer == lane)[:, :peers]
+    value_c = dot(at_peer, high, NN) * float(TILE) + dot(at_peer, low, NN)
+    col_index = jnp.sum(jnp.where(at_place, value_c, 0.0), axis=1, keepdims=True).astype(jnp.int32)
+    for copy in copies[1:3]:
+        copy.wait()
     total = None
     outs = []
     per = ROWS // TILE
-    for block in range(verts // ROWS):
+
+    def send(src, dst):
+        copy = pltpu.make_async_copy(src, dst, out_sems.at[len(outs)])
+        copy.start()
+        outs.append(copy)
+
+    for block in range(blocks):
+        hot = jnp.concatenate([low_hot * mask(row_high == block * per + k) for k in range(per)], axis=0)
+        agg_ref[block * ROWS : (block + 1) * ROWS, :] = dot(hot, arr_ref[...].reshape(slots, width), NN)
+    for block in range(blocks):
         rows = slice(block * ROWS, (block + 1) * ROWS)
-        hot = jnp.concatenate([low_hot * mask(row_high == block * per + k) for k in range(per)], axis=0)
-        agg = dot(hot, arr_ref[...], NN)
+        agg = agg_ref[rows, :]
         if block == 0:
-            copies[0].wait()
-            copies[1].wait()
+            copies[3].wait()
+            copies[4].wait()
         aged = []
         for k in range(block * per, (block + 1) * per):
             age = jnp.full((1, width), ages_ref[k], jnp.int32).astype(F32)
@@ -194,7 +219,7 @@
         inverse = lax.rsqrt(jnp.mean(agg * agg, axis=1, keepdims=True) + 1e-05)
         normed = (agg * inverse).astype(BF)
         if block == 0:
-            for copy in copies[2:]:
+            for copy in copies[5:]:
                 copy.wait()
         feats = feats_ref[rows, :]
         pre = dot(feats, ws_ref[...], NN) + dot(normed, wn_ref[...], NN)
@@ -203,9 +228,8 @@
         gp = (cot_ref[rows, :].astype(F32) * sig * (1.0 + pre * (1.0 - sig))).astype(BF)
         gp_ref[rows, :] = gp
         part = pl.ds(block * ROWS, ROWS)
-        copy = pltpu.make_async_copy(hidden_ref.at[part], hidden_hbm.at[part], out_sems.at[block])
-        copy.start()
-        outs.append(copy)
+        send(hidden_ref.at[part], hidden_hbm.at[part])
+        send(gp_ref.at[part], gp_hbm.at[part])
         grads = jnp.concatenate([dot(feats, gp, TN), dot(normed, gp, TN)], axis=0)
         total = grads if total is None else total + grads
         gn = dot(gp, wn_ref[...], NT)
@@ -213,23 +237,33 @@
         ga_ref[rows, :] = (inverse * (gn - agg * (inverse * inverse * inner))).astype(BF)
     total = total.astype(BF)
     share = 2 * width // peers
-    out_ref[:, 2 * cap : 2 * cap + share, :] = total[:, :TILE].reshape(peers, share, TILE)
-    out_ref[:, 2 * cap + share :, :] = total[:, TILE:].reshape(peers, share, TILE)
-    step = 8
+    share_ref[:, :share, :] = total[:, :TILE].reshape(peers, share, TILE)
+    share_ref[:, share:, :] = total[:, TILE:].reshape(peers, share, TILE)
+    send(share_ref, out_hbm.at[:, pl.ds(2 * cap, 2 * share), :])
+    step = peers // GATHER_STEPS
     for first in range(0, peers, step):
         part = slice(first * cap, (first + step) * cap)
         lanes = lax.broadcasted_iota(jnp.int32, (step * cap, verts), 1)
         rows = dot(mask(lanes == col_index[part, :]), ga_ref[...], NN).astype(BF)
-        out_ref[first : first + step, 0:cap, :] = rows[:, :TILE].reshape(step, cap, TILE)
-        out_ref[first : first + step, cap : 2 * cap, :] = rows[:, TILE:].reshape(step, cap, TILE)
+        back_ref[first : first + step, 0:cap, :] = rows[:, :TILE].reshape(step, cap, TILE)
+        back_ref[first : first + step, cap:, :] = rows[:, TILE:].reshape(step, cap, TILE)
+        those = pl.ds(first, step)
+        send(back_ref.at[those], out_hbm.at[those, pl.ds(0, 2 * cap), :])
     for copy in outs:
         copy.wait()
 
 
-def back_kernel(cap, got_ref, gp_ref, counts_hbm, adj_hbm, ws_hbm, out_hbm, counts_ref, adj_ref, ws_ref, grad_ref, out_ref, sems, out_sems):
+def back_kernel(
+    cap, got_hbm, gp_hbm, counts_hbm, adj_hbm, ws_hbm, out_hbm, got_ref, gp_ref, counts_ref, adj_ref, ws_ref, grad_ref, out_ref, sems, out_sems
+):
     verts = out_ref.shape[0]
     blocks = verts // ROWS
-    pairs = [(counts_hbm, counts_ref), (ws_hbm, ws_ref)]
+    pairs = [
+        (counts_hbm, counts_ref),
+        (got_hbm.at[:, pl.ds(0, 2 * cap), :], got_ref),
+        (ws_hbm, ws_ref),
+        (gp_hbm, gp_ref),
+    ]
     for block in range(blocks):
         part = pl.ds(block * ROWS, ROWS)
         pairs.append((adj_hbm.at[part], adj_ref.at[part]))
@@ -246,10 +280,12 @@
                 live, rows.astype(F32), 0.0
             ).astype(BF)
     outs = []
+    copies[2].wait()
+    copies[3].wait()
     for block in range(blocks):
         rows = slice(block * ROWS, (block + 1) * ROWS)
         own = dot(gp_ref[rows, :], ws_ref[...], NT)
-        copies[2 + block].wait()
+        copies[4 + block].wait()
         out_ref[rows, :] = (dot(adj_ref[rows, :], grad_ref[...], NN) + own).astype(BF)
         part = pl.ds(block * ROWS, ROWS)
         copy = pltpu.make_async_copy(out_ref.at[part], out_hbm.at[part], out_sems.at[block])
@@ -305,8 +341,9 @@
         (slot_counts, replica_row, edge_src, edge_slot, feats),
         0,
         [shape((peers, 2 * cap + INDEX_ROWS, TILE))],
-        (0,),
-        [
+        (),
+        [
+            pltpu.VMEM((peers, 2 * cap + INDEX_ROWS, TILE), BF),
             pltpu.VMEM((peers * cap, feats.shape[0]), BF),
             pltpu.SMEM(slot_counts.shape, jnp.int32),
             like(replica_row),
@@ -314,6 +351,7 @@
             like(edge_slot),
             like(feats),
             pltpu.SemaphoreType.DMA((5,)),
+            pltpu.SemaphoreType.DMA((GATHER_STEPS,)),
         ],
     )[0]
 
@@ -345,10 +383,12 @@
         functools.partial(master_kernel, cap),
         "masters",
         (got, adj, ages, feats, stale, cot, ws, wn),
-        1,
+        0,
         [shape((verts, width)), shape((verts, width)), shape((peers, 2 * cap + 2 * share, TILE))],
-        (1, 2),
-        [
+        (),
+        [
+            pltpu.VMEM((peers, cap, width), BF),
+            pltpu.VMEM((peers, INDEX_ROWS, TILE), BF),
             pltpu.SMEM(ages.shape, jnp.int32),
             like(feats),
             like(stale),
@@ -357,9 +397,12 @@
             like(wn),
             like(feats),
             like(feats),
-            pltpu.VMEM((peers * cap, width), BF),
-            pltpu.SemaphoreType.DMA((6,)),
-            pltpu.SemaphoreType.DMA((verts // ROWS,)),
+            like(feats),
+            pltpu.VMEM((peers, 2 * cap, TILE), BF),
+            pltpu.VMEM((peers, 2 * share, TILE), BF),
+            pltpu.VMEM((verts, width), F32),
+            pltpu.SemaphoreType.DMA((9,)),
+            pltpu.SemaphoreType.DMA((2 * (verts // ROWS) + 1 + GATHER_STEPS,)),
         ],
     )
 
@@ -370,23 +413,25 @@
         functools.partial(back_kernel, cap),
         "back",
         (got, gp, slot_counts, adj, ws),
-        2,
+        0,
         [shape(gp.shape)],
         (),
         [
+            pltpu.VMEM((got.shape[0], 2 * cap, TILE), BF),
+            like(gp),
             pltpu.SMEM(slot_counts.shape, jnp.int32),
             like(adj),
             like(ws),
             pltpu.VMEM((got.shape[0] * cap, gp.shape[1]), BF),
             like(gp),
-            pltpu.SemaphoreType.DMA((2 + blocks,)),
+            pltpu.SemaphoreType.DMA((4 + blocks,)),
             pltpu.SemaphoreType.DMA((blocks,)),
         ],
     )[0]
 
 
 def update(sums, ws, wn):
-    return call(update_kernel, "update", (sums, ws, wn), 3, [shape(ws.shape, F32)] * 2, (0, 1))
+    return call(update_kernel, "update", (sums, ws, wn), 3, [shape(ws.shape, F32)] * 2, (0, 1), limit=16)
 
 
 def exchange(x):

time: 93.5 us -> 88.1 us (0.942)
  Pallas kernels: 34.8 us -> 29.2 us
  waiting for transfers between devices: 13.7 us -> 14.7 us
    pallas_call x5, Pallas kernels: 34.8 us -> 29.2 us  [call(): pl.pallas_call(kernel, name=name, in_specs=[VMEM if k < near else HBM for...]
    all_to_all x2, waiting for transfers between devices: 11.5 us -> 12.5 us  [exchange(): return lax.all_to_all(x, 'dom', split_axis=0, concat_axis=0, tiled=True)]
where the time goes in v3:
time: 88.1 us; the launch traced here: 87.7 us
  Pallas kernels  29.2 us (33%)
  blocking collectives  21.4 us (24%)
  starting transfers between devices  19.8 us (22%)
  waiting for transfers between devices  14.7 us (17%)
  local copies, waits for them, and re-layouts  1.69 us (2%)
    pallas_call x5, Pallas kernels, call(): pl.pallas_call(kernel, name=name, in_specs=[VMEM if k < near else HBM for...  29.2 us
    all_to_all x1, blocking collectives, exchange(): return lax.all_to_all(x, 'dom', split_axis=0, concat_axis=0, tiled=True)  21.4 us
    all_to_all x2, starting transfers between devices, exchange(): return lax.all_to_all(x, 'dom', split_axis=0, concat_axis=0, tiled=True)  14.5 us
    all_to_all x2, waiting for transfers between devices, exchange(): return lax.all_to_all(x, 'dom', split_axis=0, concat_axis=0, tiled=True)  12.5 us
    ppermute x2, starting transfers between devices, body(): partial = partial + lax.ppermute(partial, 'group', pairs)  5.3 us
    ppermute x2, waiting for transfers between devices, body(): partial = partial + lax.ppermute(partial, 'group', pairs)  2.26 us
  transfers between devices with their start and end apart: 4, of which 4 were waited for; matrix products, arithmetic and copies ran while one was open for 0% of the time, Pallas kernels for 14%

profile of v3, /device:TPU:1, one launch (start us, length us, event | category | flops | bytes accessed | tf_op | source)
XLA Modules:
  0.0 87.7 jit_solution(10489782879642684296)
XLA Ops:
  0.6 7.1 %scatter.1 = bf16[32,112,128]{2,1,0:T(8,128)(2,1)} custom-call(s32[1,32]{1,0:T(1,128)} %counts_hbm.3, s32[1,32,48]{2,1,0:T(8,128)} %rows_hbm.1, s32[1,8192]{1,0:T(1,128)} %src_hbm.3, s32[1,8192]{1,0:T(1,128)} %slot_hbm.3, bf16[2048,256]{1,0:T(8,128)(2,1)} %feats_hbm.3), custom_call_target="tpu_custom_call" | custom-call | flops 1000000000 | bytes 1120384 | tf_op jit(solution)/shard_map/scatter/pallas_call | solution.py:316
  7.7 8.6 %all-to-all-start = ((bf16[32,112,128]{2,1,0:T(8,128)(2,1)}), bf16[32,112,128]{2,1,0:T(8,128)(2,1)S(1)}, u32[]{:S(2)}, u32[]{:S(2)}) async-start(bf16[32,112,128]{2,1,0:T(8,128)(2,1)} %scatter.1), calls=%async_computation | async-start | bytes 1835008 | tf_op jit(solution)/shard_map/all_to_all | solution.py:438
  16.3 5.6 %adjacency.1.adj_hbm = bf16[2048,1536]{1,0:T(8,128)(2,1)} custom-call(s32[1,8192]{1,0:T(1,128)} %src_hbm.3, s32[1,8192]{1,0:T(1,128)} %slot_hbm.3), custom_call_target="tpu_custom_call" | custom-call | flops 6000000000 | bytes 65536 | tf_op jit(solution)/shard_map/adjacency/pallas_call | solution.py:316
  21.9 10.2 %all-to-all-done.got_hbm = bf16[32,112,128]{2,1,0:T(8,128)(2,1)S(1)} async-done(((bf16[32,112,128]{2,1,0:T(8,128)(2,1)}), bf16[32,112,128]{2,1,0:T(8,128)(2,1)S(1)}, u32[]{:S(2)}, u32[]{:S(2)}) %all-to-all-start) | async-done | bytes 917536 | tf_op jit(solution)/shard_map/all_to_all | solution.py:438
  32.1 0.0 copy-start.3
  32.1 0.9 %copy-done.3 = bf16[32,112,128]{2,1,0:T(8,128)(2,1)} copy-done((bf16[32,112,128]{2,1,0:T(8,128)(2,1)}, bf16[32,112,128]{2,1,0:T(8,128)(2,1)S(1)}, u32[]{:S(2)}) %copy-start.3) | copy-done | bytes 917528
  33.0 8.8 %masters.1 = (bf16[2048,256]{1,0:T(8,128)(2,1)}, bf16[2048,256]{1,0:T(8,128)(2,1)}, bf16[32,128,128]{2,1,0:T(8,128)(2,1)}) custom-call(bf16[32,112,128]{2,1,0:T(8,128)(2,1)} %copy-done.3, bf16[2048,1536]{1,0:T(8,128)(2,1)} %adjacency.1.adj_hbm, s32[16]{0:T(128)} %ages_hbm.1, bf16[2048,256]{1,0:T(8,128)(2,1)} %feats_hbm.3, bf16[2048,256]{1,0:T(8,128)(2,1)} %stale_hbm.1, ...), custom_call_target="tpu_custom_call" | custom-call | flops 1000000000 | bytes 10616896 | tf_op jit(solution)/shard_map/masters/pallas_call | solution.py:316
  41.8 0.0 copy-start
  41.8 0.0 copy-start.1
  41.9 21.4 %all_to_all.15.got_hbm = bf16[32,128,128]{2,1,0:T(8,128)(2,1)S(1)} all-to-all(bf16[32,128,128]{2,1,0:T(8,128)(2,1)} %get-tuple-element.10), channel_id=1, replica_groups=mesh['group'=4,'dom'=32] {'dom'}, dimensions={0} | all-to-all | bytes 2097152 | tf_op jit(solution)/shard_map/all_to_all | solution.py:438
  63.3 0.0 copy-start.2
  63.3 1.7 %collective-permute-start = (f32[32,128]{1,0:T(8,128)S(1)}, f32[32,128]{1,0:T(8,128)S(1)}, u32[]{:S(2)}, u32[]{:S(2)}) collective-permute-start(f32[32,128]{1,0:T(8,128)S(1)} %convert_reduce_fusion), channel_id=1, source_target_pairs={{0,32},{32,0},{64,96},{96,64},{1,33},{33,1},{65,97},{97,65},{2,34}... | collective-permute-start | bytes 49160 | tf_op jit(solution)/shard_map/ppermute | solution.py:457
  65.0 1.1 %collective-permute-done = f32[32,128]{1,0:T(8,128)S(1)} collective-permute-done((f32[32,128]{1,0:T(8,128)S(1)}, f32[32,128]{1,0:T(8,128)S(1)}, u32[]{:S(2)}, u32[]{:S(2)}) %collective-permute-start) | collective-permute-done | bytes 16416 | tf_op jit(solution)/shard_map/ppermute | solution.py:457
  66.2 3.6 %collective-permute-start.1 = (f32[32,128]{1,0:T(8,128)S(1)}, f32[32,128]{1,0:T(8,128)S(1)}, u32[]{:S(2)}, u32[]{:S(2)}) collective-permute-start(f32[32,128]{1,0:T(8,128)S(1)} %add.6), channel_id=1, source_target_pairs={{0,96},{32,64},{64,32},{96,0},{1,97},{33,65},{65,33},{97,1},{2,98}... | collective-permute-start | bytes 49160 | tf_op jit(solution)/shard_map/ppermute | solution.py:457
  69.7 1.1 %collective-permute-done.1 = f32[32,128]{1,0:T(8,128)S(1)} collective-permute-done((f32[32,128]{1,0:T(8,128)S(1)}, f32[32,128]{1,0:T(8,128)S(1)}, u32[]{:S(2)}, u32[]{:S(2)}) %collective-permute-start.1) | collective-permute-done | bytes 16416 | tf_op jit(solution)/shard_map/ppermute | solution.py:457
  70.9 0.7 broadcast_in_dim.2
  71.6 5.9 %all-to-all-start.2 = ((bf16[32,32,128]{2,1,0:T(8,128)(2,1)}), bf16[32,32,128]{2,1,0:T(8,128)(2,1)S(1)}, u32[]{:S(2)}, u32[]{:S(2)}) async-start(bf16[32,32,128]{2,1,0:T(8,128)(2,1)} %broadcast_in_dim.2), calls=%async_computation.2 | async-start | bytes 524288 | tf_op jit(solution)/shard_map/all_to_all | solution.py:438
  77.6 0.0 copy-done.2
  77.6 6.7 %back.1 = bf16[2048,256]{1,0:T(8,128)(2,1)} custom-call(bf16[32,128,128]{2,1,0:T(8,128)(2,1)} %copy-done.2, bf16[2048,256]{1,0:T(8,128)(2,1)} %get-tuple-element.11.gp_hbm, s32[1,32]{1,0:T(1,128)} %counts_hbm.3, bf16[2048,1536]{1,0:T(8,128)(2,1)} %adjacency.1.adj_hbm, bf16[256,256]{1,0:T(8,128)(2,1)} %ws_ref.1), custom_call_target="tpu_custom_call" | custom-call | flops 1000000000 | bytes 8519808 | tf_op jit(solution)/shard_map/back/pallas_call | solution.py:316
  84.2 2.3 %all-to-all-done.2.sum_ref = bf16[32,32,128]{2,1,0:T(8,128)(2,1)S(1)} async-done(((bf16[32,32,128]{2,1,0:T(8,128)(2,1)}), bf16[32,32,128]{2,1,0:T(8,128)(2,1)S(1)}, u32[]{:S(2)}, u32[]{:S(2)}) %all-to-all-start.2) | async-done | bytes 262176 | tf_op jit(solution)/shard_map/all_to_all | solution.py:438
  86.6 0.0 copy-done
  86.6 0.0 copy-done.1
  86.6 1.1 %update.1 = (f32[256,256]{1,0:T(8,128)}, f32[256,256]{1,0:T(8,128)}) custom-call(bf16[32,32,128]{2,1,0:T(8,128)(2,1)S(1)} %all-to-all-done.2.sum_ref, bf16[256,256]{1,0:T(8,128)(2,1)S(1)} %copy-done, bf16[256,256]{1,0:T(8,128)(2,1)S(1)} %copy-done.1), custom_call_target="tpu_custom_call" | custom-call | flops 1000000000 | bytes 524288 | tf_op jit(solution)/shard_map/update/pallas_call | solution.py:316
  (3 shorter events, 0.1 us)
Async XLA Ops:
  7.7 24.4 %all-to-all-start = ((bf16[32,112,128]{2,1,0:T(8,128)(2,1)}), bf16[32,112,128]{2,1,0:T(8,128)(2,1)S(1)}, u32[]{:S(2)}, u32[]{:S(2)}) async-start(bf16[32,112,128]{2,1,0:T(8,128)(2,1)} %scatter.1), calls=%async_computation | async-start | bytes 1835008 | tf_op jit(solution)/shard_map/all_to_all | solution.py:438
  32.1 0.9 %copy-start.3 = (bf16[32,112,128]{2,1,0:T(8,128)(2,1)}, bf16[32,112,128]{2,1,0:T(8,128)(2,1)S(1)}, u32[]{:S(2)}) copy-start(bf16[32,112,128]{2,1,0:T(8,128)(2,1)S(1)} %all-to-all-done.got_hbm) | copy-start | bytes 2752516
  41.8 44.7 %copy-start = (bf16[256,256]{1,0:T(8,128)(2,1)S(1)}, bf16[256,256]{1,0:T(8,128)(2,1)}, u32[]{:S(2)}) copy-start(bf16[256,256]{1,0:T(8,128)(2,1)} %ws_ref.1) | copy-start | bytes 393220
  41.8 44.7 %copy-start.1 = (bf16[256,256]{1,0:T(8,128)(2,1)S(1)}, bf16[256,256]{1,0:T(8,128)(2,1)}, u32[]{:S(2)}) copy-start(bf16[256,256]{1,0:T(8,128)(2,1)} %wn_ref.1) | copy-start | bytes 393220
  63.3 14.3 %copy-start.2 = (bf16[32,128,128]{2,1,0:T(8,128)(2,1)}, bf16[32,128,128]{2,1,0:T(8,128)(2,1)S(1)}, u32[]{:S(2)}) copy-start(bf16[32,128,128]{2,1,0:T(8,128)(2,1)S(1)} %all_to_all.15.got_hbm) | copy-start | bytes 3145732
  63.3 2.8 %collective-permute-start = (f32[32,128]{1,0:T(8,128)S(1)}, f32[32,128]{1,0:T(8,128)S(1)}, u32[]{:S(2)}, u32[]{:S(2)}) collective-permute-start(f32[32,128]{1,0:T(8,128)S(1)} %convert_reduce_fusion), channel_id=1, source_target_pairs={{0,32},{32,0},{64,96},{96,64},{1,33},{33,1},{65,97},{97,65},{2,34}... | collective-permute-start | bytes 49160 | tf_op jit(solution)/shard_map/ppermute | solution.py:457
  66.2 4.7 %collective-permute-start.1 = (f32[32,128]{1,0:T(8,128)S(1)}, f32[32,128]{1,0:T(8,128)S(1)}, u32[]{:S(2)}, u32[]{:S(2)}) collective-permute-start(f32[32,128]{1,0:T(8,128)S(1)} %add.6), channel_id=1, source_target_pairs={{0,96},{32,64},{64,32},{96,0},{1,97},{33,65},{65,33},{97,1},{2,98}... | collective-permute-start | bytes 49160 | tf_op jit(solution)/shard_map/ppermute | solution.py:457
  71.6 15.0 %all-to-all-start.2 = ((bf16[32,32,128]{2,1,0:T(8,128)(2,1)}), bf16[32,32,128]{2,1,0:T(8,128)(2,1)S(1)}, u32[]{:S(2)}, u32[]{:S(2)}) async-start(bf16[32,32,128]{2,1,0:T(8,128)(2,1)} %broadcast_in_dim.2), calls=%async_computation.2 | async-start | bytes 524288 | tf_op jit(solution)/shard_map/all_to_all | solution.py:438

commit v4 on v3

--- a/solution.py
+++ b/solution.py
@@ -404,6 +404,7 @@
             pltpu.SemaphoreType.DMA((9,)),
             pltpu.SemaphoreType.DMA((2 * (verts // ROWS) + 1 + GATHER_STEPS,)),
         ],
+        limit=50,
     )
 
 
@@ -427,6 +428,7 @@
             pltpu.SemaphoreType.DMA((4 + blocks,)),
             pltpu.SemaphoreType.DMA((blocks,)),
         ],
+        limit=50,
     )[0]
 
 
@@ -450,13 +452,11 @@
     )
     returned = exchange(outgoing)
     partial = jnp.sum(returned[:, 2 * cap :, :].astype(F32), axis=0)
-    groups = lax.axis_size("group")
-    step = 1
-    while step < groups:
-        pairs = [(k, k ^ (2 * step - 1)) for k in range(groups)]
-        partial = partial + lax.ppermute(partial, "group", pairs)
-        step *= 2
-    share = partial.astype(BF)
+    groups = range(lax.axis_size("group"))
+    near, far, across = (
+        lax.ppermute(partial, "group", [(k, k ^ other) for k in groups]) for other in (1, 2, 3)
+    )
+    share = ((partial + near) + (far + across)).astype(BF)
     sums = exchange(jnp.broadcast_to(share[None], (peers,) + share.shape))
     feat_grad = back(cap, returned, grad_pre, slot_counts, adj, w_self)
     new_self, new_neigh = update(sums, w_self, w_neigh)

time: 88.1 us -> 88 us (level)
  Pallas kernels: 29.2 us -> 30.8 us
  waiting for transfers between devices: 14.7 us -> 15.9 us
  starting transfers between devices: 19.8 us -> 18.7 us
  local copies, waits for them, and re-layouts: 1.69 us -> 0.76 us
    pallas_call x5, Pallas kernels: 29.2 us -> 30.8 us  [call(): pl.pallas_call(kernel, name=name, in_specs=[VMEM if k < near else HBM for...]
    ppermute x2 -> x3, waiting for transfers between devices: 2.26 us -> 3.2 us  [body(): lax.ppermute(partial, 'group', [(k, k ^ other) for k in groups])]
    unnamed x8, local copies, waits for them, and re-layouts: 0.95 us -> 0.03 us
    ppermute x2 -> x3, starting transfers between devices: 5.3 us -> 4.73 us  [body(): lax.ppermute(partial, 'group', [(k, k ^ other) for k in groups])]
  transfers between devices with their start and end apart: 4 -> 5, of which waited for: 4 -> 4; matrix products, arithmetic and copies ran while one was open for 0% -> 0% of each run, Pallas kernels for 14% -> 14%
where the time goes in v4:
time: 88 us; the launch traced here: 87.6 us
  Pallas kernels  30.8 us (35%)
  blocking collectives  20.7 us (24%)
  starting transfers between devices  18.7 us (21%)
  waiting for transfers between devices  15.9 us (18%)
    pallas_call x5, Pallas kernels, call(): pl.pallas_call(kernel, name=name, in_specs=[VMEM if k < near else HBM for...  30.8 us
    all_to_all x1, blocking collectives, exchange(): return lax.all_to_all(x, 'dom', split_axis=0, concat_axis=0, tiled=True)  20.7 us
    all_to_all x2, starting transfers between devices, exchange(): return lax.all_to_all(x, 'dom', split_axis=0, concat_axis=0, tiled=True)  14 us
    all_to_all x2, waiting for transfers between devices, exchange(): return lax.all_to_all(x, 'dom', split_axis=0, concat_axis=0, tiled=True)  12.7 us
    ppermute x3, starting transfers between devices, body(): lax.ppermute(partial, 'group', [(k, k ^ other) for k in groups])  4.73 us
    ppermute x3, waiting for transfers between devices, body(): lax.ppermute(partial, 'group', [(k, k ^ other) for k in groups])  3.2 us
  transfers between devices with their start and end apart: 5, of which 4 were waited for; matrix products, arithmetic and copies ran while one was open for 0% of the time, Pallas kernels for 14%

profile of v4, /device:TPU:1, one launch (start us, length us, event | category | flops | bytes accessed | tf_op | source)
XLA Modules:
  0.0 87.6 jit_solution(17597741122784216589)
XLA Ops:
  0.6 7.1 %scatter.1 = bf16[32,112,128]{2,1,0:T(8,128)(2,1)} custom-call(s32[1,32]{1,0:T(1,128)} %counts_hbm.3, s32[1,32,48]{2,1,0:T(8,128)} %rows_hbm.1, s32[1,8192]{1,0:T(1,128)} %src_hbm.3, s32[1,8192]{1,0:T(1,128)} %slot_hbm.3, bf16[2048,256]{1,0:T(8,128)(2,1)} %feats_hbm.3), custom_call_target="tpu_custom_call" | custom-call | flops 1000000000 | bytes 1120384 | tf_op jit(solution)/shard_map/scatter/pallas_call | solution.py:316
  7.7 8.6 %all-to-all-start = ((bf16[32,112,128]{2,1,0:T(8,128)(2,1)}), bf16[32,112,128]{2,1,0:T(8,128)(2,1)S(1)}, u32[]{:S(2)}, u32[]{:S(2)}) async-start(bf16[32,112,128]{2,1,0:T(8,128)(2,1)} %scatter.1), calls=%async_computation | async-start | bytes 1835008 | tf_op jit(solution)/shard_map/all_to_all | solution.py:440
  16.3 0.0 copy-start
  16.3 0.0 copy-start.1
  16.4 0.0 copy-start.2
  16.4 5.7 %adjacency.1.adj_hbm = bf16[2048,1536]{1,0:T(8,128)(2,1)} custom-call(s32[1,8192]{1,0:T(1,128)} %src_hbm.3, s32[1,8192]{1,0:T(1,128)} %slot_hbm.3), custom_call_target="tpu_custom_call" | custom-call | flops 6000000000 | bytes 65536 | tf_op jit(solution)/shard_map/adjacency/pallas_call | solution.py:316
  22.0 0.0 copy-start.3
  22.0 10.1 %all-to-all-done.got_hbm = bf16[32,112,128]{2,1,0:T(8,128)(2,1)S(1)} async-done(((bf16[32,112,128]{2,1,0:T(8,128)(2,1)}), bf16[32,112,128]{2,1,0:T(8,128)(2,1)S(1)}, u32[]{:S(2)}, u32[]{:S(2)}) %all-to-all-start) | async-done | bytes 917536 | tf_op jit(solution)/shard_map/all_to_all | solution.py:440
  32.1 0.0 copy-done
  32.1 0.0 copy-done.1
  32.1 0.0 copy-done.2
  32.1 10.6 %masters.1 = (bf16[2048,256]{1,0:T(8,128)(2,1)}, bf16[2048,256]{1,0:T(8,128)(2,1)S(1)}, bf16[32,128,128]{2,1,0:T(8,128)(2,1)S(1)}) custom-call(bf16[32,112,128]{2,1,0:T(8,128)(2,1)S(1)} %all-to-all-done.got_hbm, bf16[2048,1536]{1,0:T(8,128)(2,1)} %adjacency.1.adj_hbm, s32[16]{0:T(128)S(1)} %copy-done.2, bf16[2048,256]{1,0:T(8,128)(2,1)} %feats_hbm.3, ...), custom_call_target="tpu_custom_call" | custom-call | flops 1000000000 | bytes 10616896 | tf_op jit(solution)/shard_map/masters/pallas_call | solution.py:316
  42.7 20.7 %all_to_all.15.got_hbm = bf16[32,128,128]{2,1,0:T(8,128)(2,1)S(1)} all-to-all(bf16[32,128,128]{2,1,0:T(8,128)(2,1)S(1)} %get-tuple-element.10), channel_id=1, replica_groups=mesh['group'=4,'dom'=32] {'dom'}, dimensions={0} | all-to-all | bytes 2097152 | tf_op jit(solution)/shard_map/all_to_all | solution.py:440
  63.5 3.8 %collective-permute-start.2 = (f32[32,128]{1,0:T(8,128)S(1)}, f32[32,128]{1,0:T(8,128)S(1)}, u32[]{:S(2)}, u32[]{:S(2)}) collective-permute-start(f32[32,128]{1,0:T(8,128)S(1)} %convert_reduce_fusion), channel_id=1, source_target_pairs={{0,96},{32,64},{64,32},{96,0},{1,97},{33,65},{65,33},{97,1},{2,98}... | collective-permute-start | bytes 49160 | tf_op jit(solution)/shard_map/ppermute | solution.py:457
  67.3 0.2 collective-permute-start.1
  67.5 0.7 collective-permute-start
  68.2 0.2 collective-permute-done.2
  68.4 3.0 %collective-permute-done.1 = f32[32,128]{1,0:T(8,128)S(1)} collective-permute-done((f32[32,128]{1,0:T(8,128)S(1)}, f32[32,128]{1,0:T(8,128)S(1)}, u32[]{:S(2)}, u32[]{:S(2)}) %collective-permute-start.1) | collective-permute-done | bytes 16416 | tf_op jit(solution)/shard_map/ppermute | solution.py:457
  71.4 0.0 collective-permute-done
  71.4 0.7 broadcast_in_dim.2
  72.2 5.3 %all-to-all-start.2 = ((bf16[32,32,128]{2,1,0:T(8,128)(2,1)}), bf16[32,32,128]{2,1,0:T(8,128)(2,1)S(1)}, u32[]{:S(2)}, u32[]{:S(2)}) async-start(bf16[32,32,128]{2,1,0:T(8,128)(2,1)} %broadcast_in_dim.2), calls=%async_computation.2 | async-start | bytes 524288 | tf_op jit(solution)/shard_map/all_to_all | solution.py:440
  77.5 0.0 copy-done.3
  77.5 6.4 %back.1 = bf16[2048,256]{1,0:T(8,128)(2,1)} custom-call(bf16[32,128,128]{2,1,0:T(8,128)(2,1)S(1)} %all_to_all.15.got_hbm, bf16[2048,256]{1,0:T(8,128)(2,1)S(1)} %get-tuple-element.11.gp_hbm, s32[1,32]{1,0:T(1,128)S(1)} %copy-done.3, bf16[2048,1536]{1,0:T(8,128)(2,1)} %adjacency.1.adj_hbm, bf16[256,256]{1,0:T(8,128)(2,1)S(1)} %copy-done), custom_call_target="tpu_custom_call" | custom-call | flops 1000000000 | bytes 8519808 | tf_op jit(solution)/shard_map/back/pallas_call | solution.py:316
  83.9 2.6 %all-to-all-done.2.sum_ref = bf16[32,32,128]{2,1,0:T(8,128)(2,1)S(1)} async-done(((bf16[32,32,128]{2,1,0:T(8,128)(2,1)}), bf16[32,32,128]{2,1,0:T(8,128)(2,1)S(1)}, u32[]{:S(2)}, u32[]{:S(2)}) %all-to-all-start.2) | async-done | bytes 262176 | tf_op jit(solution)/shard_map/all_to_all | solution.py:440
  86.5 1.1 %update.1 = (f32[256,256]{1,0:T(8,128)}, f32[256,256]{1,0:T(8,128)}) custom-call(bf16[32,32,128]{2,1,0:T(8,128)(2,1)S(1)} %all-to-all-done.2.sum_ref, bf16[256,256]{1,0:T(8,128)(2,1)S(1)} %copy-done, bf16[256,256]{1,0:T(8,128)(2,1)S(1)} %copy-done.1), custom_call_target="tpu_custom_call" | custom-call | flops 1000000000 | bytes 524288 | tf_op jit(solution)/shard_map/update/pallas_call | solution.py:316
  (2 shorter events, 0.1 us)
Async XLA Ops:
  7.7 24.4 %all-to-all-start = ((bf16[32,112,128]{2,1,0:T(8,128)(2,1)}), bf16[32,112,128]{2,1,0:T(8,128)(2,1)S(1)}, u32[]{:S(2)}, u32[]{:S(2)}) async-start(bf16[32,112,128]{2,1,0:T(8,128)(2,1)} %scatter.1), calls=%async_computation | async-start | bytes 1835008 | tf_op jit(solution)/shard_map/all_to_all | solution.py:440
  16.3 15.8 %copy-start = (bf16[256,256]{1,0:T(8,128)(2,1)S(1)}, bf16[256,256]{1,0:T(8,128)(2,1)}, u32[]{:S(2)}) copy-start(bf16[256,256]{1,0:T(8,128)(2,1)} %ws_ref.1) | copy-start | bytes 393220
  16.3 15.7 %copy-start.1 = (bf16[256,256]{1,0:T(8,128)(2,1)S(1)}, bf16[256,256]{1,0:T(8,128)(2,1)}, u32[]{:S(2)}) copy-start(bf16[256,256]{1,0:T(8,128)(2,1)} %wn_ref.1) | copy-start | bytes 393220
  16.4 15.7 %copy-start.2 = (s32[16]{0:T(128)S(1)}, s32[16]{0:T(128)}, u32[]{:S(2)}) copy-start(s32[16]{0:T(128)} %ages_hbm.1) | copy-start | bytes 196
  22.0 55.5 %copy-start.3 = (s32[1,32]{1,0:T(1,128)S(1)}, s32[1,32]{1,0:T(1,128)}, u32[]{:S(2)}) copy-start(s32[1,32]{1,0:T(1,128)} %counts_hbm.3) | copy-start | bytes 388
  63.5 5.0 %collective-permute-start.2 = (f32[32,128]{1,0:T(8,128)S(1)}, f32[32,128]{1,0:T(8,128)S(1)}, u32[]{:S(2)}, u32[]{:S(2)}) collective-permute-start(f32[32,128]{1,0:T(8,128)S(1)} %convert_reduce_fusion), channel_id=1, source_target_pairs={{0,96},{32,64},{64,32},{96,0},{1,97},{33,65},{65,33},{97,1},{2,98}... | collective-permute-start | bytes 49160 | tf_op jit(solution)/shard_map/ppermute | solution.py:457
  67.3 4.1 %collective-permute-start.1 = (f32[32,128]{1,0:T(8,128)S(1)}, f32[32,128]{1,0:T(8,128)S(1)}, u32[]{:S(2)}, u32[]{:S(2)}) collective-permute-start(f32[32,128]{1,0:T(8,128)S(1)} %convert_reduce_fusion), channel_id=1, source_target_pairs={{0,64},{32,96},{64,0},{96,32},{1,65},{33,97},{65,1},{97,33},{2,66}... | collective-permute-start | bytes 49160 | tf_op jit(solution)/shard_map/ppermute | solution.py:457
  67.5 3.9 %collective-permute-start = (f32[32,128]{1,0:T(8,128)S(1)}, f32[32,128]{1,0:T(8,128)S(1)}, u32[]{:S(2)}, u32[]{:S(2)}) collective-permute-start(f32[32,128]{1,0:T(8,128)S(1)} %convert_reduce_fusion), channel_id=1, source_target_pairs={{0,32},{32,0},{64,96},{96,64},{1,33},{33,1},{65,97},{97,65},{2,34}... | collective-permute-start | bytes 49160 | tf_op jit(solution)/shard_map/ppermute | solution.py:457
  72.2 14.4 %all-to-all-start.2 = ((bf16[32,32,128]{2,1,0:T(8,128)(2,1)}), bf16[32,32,128]{2,1,0:T(8,128)(2,1)S(1)}, u32[]{:S(2)}, u32[]{:S(2)}) async-start(bf16[32,32,128]{2,1,0:T(8,128)(2,1)} %broadcast_in_dim.2), calls=%async_computation.2 | async-start | bytes 524288 | tf_op jit(solution)/shard_map/all_to_all | solution.py:440

commit v5 on v4

--- a/solution.py
+++ b/solution.py
@@ -121,65 +121,51 @@
         copy.wait()
 
 
+def index_digits(cap, got_ref):
+    peers = got_ref.shape[0]
+    coded = got_ref[:, 2 * cap :, :].reshape(peers * INDEX_ROWS, TILE)
+    pick_row = lax.broadcasted_iota(jnp.int32, (peers, peers * INDEX_ROWS), 1)
+    pick_peer = lax.broadcasted_iota(jnp.int32, (peers, peers * INDEX_ROWS), 0) * INDEX_ROWS
+    high = dot(mask(pick_row == pick_peer), coded, NN).astype(BF)
+    low = dot(mask(pick_row == pick_peer + 1), coded, NN).astype(BF)
+    return high, low
+
+
 def master_kernel(
     cap,
-    got_hbm,
+    got_ref,
+    ws_ref,
+    wn_ref,
     adj_hbm,
     ages_hbm,
     feats_hbm,
     stale_hbm,
     cot_hbm,
-    ws_hbm,
-    wn_hbm,
     hidden_hbm,
     gp_hbm,
-    out_hbm,
+    agg_hbm,
+    share_ref,
     arr_ref,
-    coded_ref,
     ages_ref,
     feats_ref,
     stale_ref,
     cot_ref,
-    ws_ref,
-    wn_ref,
     hidden_ref,
     gp_ref,
-    ga_ref,
-    back_ref,
-    share_ref,
     agg_ref,
     sems,
     out_sems,
 ):
-    peers = arr_ref.shape[0]
+    peers = got_ref.shape[0]
     verts, width = feats_ref.shape
     slots = peers * cap
     blocks = verts // ROWS
     copies = start_all(
-        [
-            (got_hbm.at[:, pl.ds(2 * cap, INDEX_ROWS), :], coded_ref),
-            (got_hbm.at[:, pl.ds(0, cap), :], arr_ref.at[:, :, pl.ds(0, TILE)]),
-            (got_hbm.at[:, pl.ds(cap, cap), :], arr_ref.at[:, :, pl.ds(TILE, TILE)]),
-            (ages_hbm, ages_ref),
-            (stale_hbm, stale_ref),
-            (feats_hbm, feats_ref),
-            (ws_hbm, ws_ref),
-            (wn_hbm, wn_ref),
-            (cot_hbm, cot_ref),
-        ],
-        sems,
-    )
-    copies[0].wait()
-    coded = coded_ref[...].reshape(peers * INDEX_ROWS, TILE)
-    pick_row = lax.broadcasted_iota(jnp.int32, (peers, peers * INDEX_ROWS), 1)
-    pick_peer = lax.broadcasted_iota(jnp.int32, (peers, peers * INDEX_ROWS), 0) * INDEX_ROWS
-    high = dot(mask(pick_row == pick_peer), coded, NN).astype(BF)
-    low = dot(mask(pick_row == pick_peer + 1), coded, NN).astype(BF)
+        [(ages_hbm, ages_ref), (stale_hbm, stale_ref), (feats_hbm, feats_ref), (cot_hbm, cot_ref)], sems
+    )
+    high, low = index_digits(cap, got_ref)
     place = lax.broadcasted_iota(jnp.int32, (peers, cap, TILE), 1).reshape(slots, TILE)
-    peer = lax.broadcasted_iota(jnp.int32, (peers, cap, TILE), 0).reshape(slots, TILE)
-    lane = lax.broadcasted_iota(jnp.int32, (slots, TILE), 1)
-    at_place = place == lane
-    spread = mask(at_place)
+    spread = mask(place == lax.broadcasted_iota(jnp.int32, (slots, TILE), 1))
     value = dot(high, spread, NT) * float(TILE) + dot(low, spread, NT)
     slot = lax.broadcasted_iota(jnp.int32, (peers, slots), 1)
     least = lax.broadcasted_iota(jnp.int32, (peers, slots), 0) * cap
@@ -188,39 +174,26 @@
     sub = lax.broadcasted_iota(jnp.int32, (TILE, slots), 0)
     low_hot = mask(sub == (row_index & (TILE - 1)))
     row_high = row_index >> 7
-    at_peer = mask(peer == lane)[:, :peers]
-    value_c = dot(at_peer, high, NN) * float(TILE) + dot(at_peer, low, NN)
-    col_index = jnp.sum(jnp.where(at_place, value_c, 0.0), axis=1, keepdims=True).astype(jnp.int32)
-    for copy in copies[1:3]:
+    arr_ref[:, :TILE] = got_ref[:, 0:cap, :].reshape(slots, TILE)
+    arr_ref[:, TILE:] = got_ref[:, cap : 2 * cap, :].reshape(slots, TILE)
+    per = ROWS // TILE
+    for block in range(blocks):
+        hot = jnp.concatenate([low_hot * mask(row_high == block * per + k) for k in range(per)], axis=0)
+        agg_ref[block * ROWS : (block + 1) * ROWS, :] = dot(hot, arr_ref[...], NN)
+    for copy in copies:
         copy.wait()
     total = None
     outs = []
-    per = ROWS // TILE
-
-    def send(src, dst):
-        copy = pltpu.make_async_copy(src, dst, out_sems.at[len(outs)])
-        copy.start()
-        outs.append(copy)
-
-    for block in range(blocks):
-        hot = jnp.concatenate([low_hot * mask(row_high == block * per + k) for k in range(per)], axis=0)
-        agg_ref[block * ROWS : (block + 1) * ROWS, :] = dot(hot, arr_ref[...].reshape(slots, width), NN)
     for block in range(blocks):
         rows = slice(block * ROWS, (block + 1) * ROWS)
-        agg = agg_ref[rows, :]
-        if block == 0:
-            copies[3].wait()
-            copies[4].wait()
         aged = []
         for k in range(block * per, (block + 1) * per):
             age = jnp.full((1, width), ages_ref[k], jnp.int32).astype(F32)
             aged.append(stale_ref[k * TILE : (k + 1) * TILE, :].astype(F32) * (1.0 / (1.0 + age)))
-        agg = agg + jnp.concatenate(aged, axis=0)
+        agg = agg_ref[rows, :] + jnp.concatenate(aged, axis=0)
+        agg_ref[rows, :] = agg
         inverse = lax.rsqrt(jnp.mean(agg * agg, axis=1, keepdims=True) + 1e-05)
         normed = (agg * inverse).astype(BF)
-        if block == 0:
-            for copy in copies[5:]:
-                copy.wait()
         feats = feats_ref[rows, :]
         pre = dot(feats, ws_ref[...], NN) + dot(normed, wn_ref[...], NN)
         sig = jax.nn.sigmoid(pre)
@@ -228,29 +201,61 @@
         gp = (cot_ref[rows, :].astype(F32) * sig * (1.0 + pre * (1.0 - sig))).astype(BF)
         gp_ref[rows, :] = gp
         part = pl.ds(block * ROWS, ROWS)
-        send(hidden_ref.at[part], hidden_hbm.at[part])
-        send(gp_ref.at[part], gp_hbm.at[part])
+        for near, far in ((agg_ref, agg_hbm), (gp_ref, gp_hbm), (hidden_ref, hidden_hbm)):
+            copy = pltpu.make_async_copy(near.at[part], far.at[part], out_sems.at[len(outs)])
+            copy.start()
+            outs.append(copy)
         grads = jnp.concatenate([dot(feats, gp, TN), dot(normed, gp, TN)], axis=0)
         total = grads if total is None else total + grads
-        gn = dot(gp, wn_ref[...], NT)
-        inner = jnp.mean(gn * agg, axis=1, keepdims=True)
-        ga_ref[rows, :] = (inverse * (gn - agg * (inverse * inverse * inner))).astype(BF)
     total = total.astype(BF)
     share = 2 * width // peers
     share_ref[:, :share, :] = total[:, :TILE].reshape(peers, share, TILE)
     share_ref[:, share:, :] = total[:, TILE:].reshape(peers, share, TILE)
-    send(share_ref, out_hbm.at[:, pl.ds(2 * cap, 2 * share), :])
+    for copy in outs:
+        copy.wait()
+
+
+def outgoing_kernel(cap, got_ref, wn_ref, gp_hbm, agg_hbm, out_ref, gp_ref, agg_ref, ga_ref, sems):
+    peers = got_ref.shape[0]
+    verts = gp_ref.shape[0]
+    slots = peers * cap
+    parts = [pl.ds(block * ROWS, ROWS) for block in range(verts // ROWS)]
+    copies = start_all(
+        [(far.at[part], near.at[part]) for part in parts for far, near in ((gp_hbm, gp_ref), (agg_hbm, agg_ref))],
+        sems,
+    )
+    for block in range(verts // ROWS):
+        rows = slice(block * ROWS, (block + 1) * ROWS)
+        copies[2 * block].wait()
+        copies[2 * block + 1].wait()
+        agg = agg_ref[rows, :]
+        inverse = lax.rsqrt(jnp.mean(agg * agg, axis=1, keepdims=True) + 1e-05)
+        gn = dot(gp_ref[rows, :], wn_ref[...], NT)
+        inner = jnp.mean(gn * agg, axis=1, keepdims=True)
+        ga_ref[rows, :] = (inverse * (gn - agg * (inverse * inverse * inner))).astype(BF)
+    high, low = index_digits(cap, got_ref)
+    place = lax.broadcasted_iota(jnp.int32, (peers, cap, TILE), 1).reshape(slots, TILE)
+    peer = lax.broadcasted_iota(jnp.int32, (peers, cap, TILE), 0).reshape(slots, TILE)
+    lane = lax.broadcasted_iota(jnp.int32, (slots, TILE), 1)
+    at_peer = mask(peer == lane)[:, :peers]
+    value = dot(at_peer, high, NN) * float(TILE) + dot(at_peer, low, NN)
+    index = jnp.sum(jnp.where(place == lane, value, 0.0), axis=1, keepdims=True).astype(jnp.int32)
     step = peers // GATHER_STEPS
     for first in range(0, peers, step):
         part = slice(first * cap, (first + step) * cap)
         lanes = lax.broadcasted_iota(jnp.int32, (step * cap, verts), 1)
-        rows = dot(mask(lanes == col_index[part, :]), ga_ref[...], NN).astype(BF)
-        back_ref[first : first + step, 0:cap, :] = rows[:, :TILE].reshape(step, cap, TILE)
-        back_ref[first : first + step, cap:, :] = rows[:, TILE:].reshape(step, cap, TILE)
-        those = pl.ds(first, step)
-        send(back_ref.at[those], out_hbm.at[those, pl.ds(0, 2 * cap), :])
-    for copy in outs:
-        copy.wait()
+        rows = dot(mask(lanes == index[part, :]), ga_ref[...], NN).astype(BF)
+        out_ref[first : first + step, 0:cap, :] = rows[:, :TILE].reshape(step, cap, TILE)
+        out_ref[first : first + step, cap:, :] = rows[:, TILE:].reshape(step, cap, TILE)
+
+
+def sum_kernel(parts_ref, after_hbm, out_ref):
+    out_ref[...] = jnp.sum(parts_ref[...].astype(F32), axis=0)
+
+
+def share_kernel(own_ref, near_ref, far_ref, across_ref, after_hbm, out_ref):
+    total = (own_ref[...] + near_ref[...]) + (far_ref[...] + across_ref[...])
+    out_ref[...] = jnp.broadcast_to(total.astype(BF)[None], out_ref.shape)
 
 
 def back_kernel(
@@ -260,7 +265,7 @@
     blocks = verts // ROWS
     pairs = [
         (counts_hbm, counts_ref),
-        (got_hbm.at[:, pl.ds(0, 2 * cap), :], got_ref),
+        (got_hbm, got_ref),
         (ws_hbm, ws_ref),
         (gp_hbm, gp_ref),
     ]
@@ -382,30 +387,53 @@
     return call(
         functools.partial(master_kernel, cap),
         "masters",
-        (got, adj, ages, feats, stale, cot, ws, wn),
-        0,
-        [shape((verts, width)), shape((verts, width)), shape((peers, 2 * cap + 2 * share, TILE))],
-        (),
+        (got, ws, wn, adj, ages, feats, stale, cot),
+        3,
         [
-            pltpu.VMEM((peers, cap, width), BF),
-            pltpu.VMEM((peers, INDEX_ROWS, TILE), BF),
+            shape((verts, width)),
+            shape((verts, width)),
+            shape((verts, width), F32),
+            shape((peers, 2 * share, TILE)),
+        ],
+        (3,),
+        [
+            pltpu.VMEM((peers * cap, width), BF),
             pltpu.SMEM(ages.shape, jnp.int32),
             like(feats),
             like(stale),
             like(cot),
-            like(ws),
-            like(wn),
             like(feats),
             like(feats),
-            like(feats),
-            pltpu.VMEM((peers, 2 * cap, TILE), BF),
-            pltpu.VMEM((peers, 2 * share, TILE), BF),
             pltpu.VMEM((verts, width), F32),
-            pltpu.SemaphoreType.DMA((9,)),
-            pltpu.SemaphoreType.DMA((2 * (verts // ROWS) + 1 + GATHER_STEPS,)),
+            pltpu.SemaphoreType.DMA((4,)),
+            pltpu.SemaphoreType.DMA((3 * (verts // ROWS),)),
         ],
-        limit=50,
-    )
+        limit=52,
+    )
+
+
+def outgoing(cap, got, gp, agg, wn):
+    return call(
+        functools.partial(outgoing_kernel, cap),
+        "outgoing",
+        (got, wn, gp, agg),
+        2,
+        [shape((got.shape[0], 2 * cap, TILE))],
+        (0,),
+        [like(gp), like(agg), like(gp), pltpu.SemaphoreType.DMA((2 * (gp.shape[0] // ROWS),))],
+        limit=52,
+    )[0]
+
+
+def summed(parts, after):
+    return call(sum_kernel, "summed", (parts, after), 1, [shape(parts.shape[1:], F32)], (0,), flops=10**6, limit=16)[0]
+
+
+def shares(parts, after):
+    peers = after.shape[0]
+    return call(
+        share_kernel, "shares", (*parts, after), 4, [shape((peers,) + parts[0].shape)], (0,), flops=10**6, limit=16
+    )[0]
 
 
 def back(cap, got, gp, slot_counts, adj, ws):
@@ -447,17 +475,16 @@
     peers, cap = replica_row.shape[1:]
     arrived = exchange(scatter(slot_counts, replica_row, edge_src, edge_slot, feats))
     adj = adjacency(edge_src, edge_slot, verts, peers * cap)
-    hidden, grad_pre, outgoing = masters(
+    hidden, grad_pre, aggregate, parts = masters(
         cap, arrived, adj, bin_ages, feats, stale_agg, cotangent, w_self, w_neigh
     )
-    returned = exchange(outgoing)
-    partial = jnp.sum(returned[:, 2 * cap :, :].astype(F32), axis=0)
+    parts = exchange(parts)
+    sent = outgoing(cap, arrived, grad_pre, aggregate, w_neigh)
+    own = summed(parts, sent)
     groups = range(lax.axis_size("group"))
-    near, far, across = (
-        lax.ppermute(partial, "group", [(k, k ^ other) for k in groups]) for other in (1, 2, 3)
-    )
-    share = ((partial + near) + (far + across)).astype(BF)
-    sums = exchange(jnp.broadcast_to(share[None], (peers,) + share.shape))
+    others = [lax.ppermute(own, "group", [(k, k ^ other) for k in groups]) for other in (1, 2, 3)]
+    returned = exchange(sent)
+    sums = exchange(shares((own, *others), returned))
     feat_grad = back(cap, returned, grad_pre, slot_counts, adj, w_self)
     new_self, new_neigh = update(sums, w_self, w_neigh)
     return (hidden, feat_grad, new_self, new_neigh)

time: 88 us -> 85.1 us (0.967)
  blocking collectives: 20.7 us -> 0 us
  waiting for transfers between devices: 15.9 us -> 25.5 us
  starting transfers between devices: 18.7 us -> 25.8 us
  Pallas kernels: 30.8 us -> 32.5 us
    all_to_all x1 -> x0, blocking collectives: 20.7 us -> none  [exchange(): return lax.all_to_all(x, 'dom', split_axis=0, concat_axis=0, tiled=True)]
    all_to_all x2 -> x4, waiting for transfers between devices: 12.7 us -> 21.8 us  [exchange(): return lax.all_to_all(x, 'dom', split_axis=0, concat_axis=0, tiled=True)]
    all_to_all x2 -> x4, starting transfers between devices: 14 us -> 21.3 us  [exchange(): return lax.all_to_all(x, 'dom', split_axis=0, concat_axis=0, tiled=True)]
    pallas_call x5 -> x8, Pallas kernels: 30.8 us -> 32.5 us  [call(): pl.pallas_call(kernel, name=name, in_specs=[VMEM if k < near else HBM for...]
  transfers between devices with their start and end apart: 5 -> 7, of which waited for: 4 -> 6; matrix products, arithmetic and copies ran while one was open for 0% -> 0% of each run, Pallas kernels for 14% -> 21%
where the time goes in v5:
time: 85.1 us; the launch traced here: 84.6 us
  Pallas kernels  32.5 us (38%)
  starting transfers between devices  25.8 us (30%)
  waiting for transfers between devices  25.5 us (30%)
    pallas_call x8, Pallas kernels, call(): pl.pallas_call(kernel, name=name, in_specs=[VMEM if k < near else HBM for...  32.5 us
    all_to_all x4, waiting for transfers between devices, exchange(): return lax.all_to_all(x, 'dom', split_axis=0, concat_axis=0, tiled=True)  21.8 us
    all_to_all x4, starting transfers between devices, exchange(): return lax.all_to_all(x, 'dom', split_axis=0, concat_axis=0, tiled=True)  21.3 us
    ppermute x3, starting transfers between devices, body(): lax.ppermute(own, 'group', [(k, k ^ other) for k in groups])  4.51 us
    ppermute x3, waiting for transfers between devices, body(): lax.ppermute(own, 'group', [(k, k ^ other) for k in groups])  3.72 us
  transfers between devices with their start and end apart: 7, of which 6 were waited for; matrix products, arithmetic and copies ran while one was open for 0% of the time, Pallas kernels for 21%

profile of v5, /device:TPU:1, one launch (start us, length us, event | category | flops | bytes accessed | tf_op | source)
XLA Modules:
  0.0 84.6 jit_solution(6492423609861783500)
XLA Ops:
  0.6 7.1 %scatter.1 = bf16[32,112,128]{2,1,0:T(8,128)(2,1)} custom-call(s32[1,32]{1,0:T(1,128)} %counts_hbm.3, s32[1,32,48]{2,1,0:T(8,128)} %rows_hbm.1, s32[1,8192]{1,0:T(1,128)} %src_hbm.3, s32[1,8192]{1,0:T(1,128)} %slot_hbm.3, bf16[2048,256]{1,0:T(8,128)(2,1)} %feats_hbm.3), custom_call_target="tpu_custom_call" | custom-call | flops 1000000000 | bytes 1120384 | tf_op jit(solution)/shard_map/scatter/pallas_call | solution.py:321
  7.7 8.6 %all-to-all-start = ((bf16[32,112,128]{2,1,0:T(8,128)(2,1)}), bf16[32,112,128]{2,1,0:T(8,128)(2,1)S(1)}, u32[]{:S(2)}, u32[]{:S(2)}) async-start(bf16[32,112,128]{2,1,0:T(8,128)(2,1)} %scatter.1), calls=%async_computation | async-start | bytes 1835008 | tf_op jit(solution)/shard_map/all_to_all | solution.py:468
  16.3 0.0 copy-start.1
  16.3 0.0 copy-start.2
  16.4 0.0 copy-start.3
  16.4 5.7 %adjacency.1.adj_hbm = bf16[2048,1536]{1,0:T(8,128)(2,1)} custom-call(s32[1,8192]{1,0:T(1,128)} %src_hbm.3, s32[1,8192]{1,0:T(1,128)} %slot_hbm.3), custom_call_target="tpu_custom_call" | custom-call | flops 6000000000 | bytes 65536 | tf_op jit(solution)/shard_map/adjacency/pallas_call | solution.py:321
  22.0 10.0 %all-to-all-done.got_ref = bf16[32,112,128]{2,1,0:T(8,128)(2,1)S(1)} async-done(((bf16[32,112,128]{2,1,0:T(8,128)(2,1)}), bf16[32,112,128]{2,1,0:T(8,128)(2,1)S(1)}, u32[]{:S(2)}, u32[]{:S(2)}) %all-to-all-start) | async-done | bytes 917536 | tf_op jit(solution)/shard_map/all_to_all | solution.py:468
  32.1 0.0 copy-done.1
  32.1 0.0 copy-done.2
  32.1 0.0 copy-done.3
  32.1 5.8 %masters.1 = (bf16[2048,256]{1,0:T(8,128)(2,1)}, bf16[2048,256]{1,0:T(8,128)(2,1)}, f32[2048,256]{1,0:T(8,128)}, bf16[32,32,128]{2,1,0:T(8,128)(2,1)}) custom-call(bf16[32,112,128]{2,1,0:T(8,128)(2,1)S(1)} %all-to-all-done.got_ref, bf16[256,256]{1,0:T(8,128)(2,1)S(1)} %copy-done.1, bf16[256,256]{1,0:T(8,128)(2,1)S(1)} %copy-done.2, ...), custom_call_target="tpu_custom_call" | custom-call | flops 1000000000 | bytes 10616896 | tf_op jit(solution)/shard_map/masters/pallas_call | solution.py:321
  37.9 0.0 copy-start
  37.9 0.0 copy-start.4
  37.9 4.1 %all-to-all-start.2 = ((bf16[32,32,128]{2,1,0:T(8,128)(2,1)}), bf16[32,32,128]{2,1,0:T(8,128)(2,1)S(1)}, u32[]{:S(2)}, u32[]{:S(2)}) async-start(bf16[32,32,128]{2,1,0:T(8,128)(2,1)} %get-tuple-element.13), calls=%async_computation.2 | async-start | bytes 524288 | tf_op jit(solution)/shard_map/all_to_all | solution.py:468
  42.0 5.8 %outgoing.1.after_hbm = bf16[32,96,128]{2,1,0:T(8,128)(2,1)} custom-call(bf16[32,112,128]{2,1,0:T(8,128)(2,1)S(1)} %all-to-all-done.got_ref, bf16[256,256]{1,0:T(8,128)(2,1)S(1)} %copy-done.2, bf16[2048,256]{1,0:T(8,128)(2,1)} %get-tuple-element.11.gp_hbm, f32[2048,256]{1,0:T(8,128)} %get-tuple-element.12.agg_hbm), custom_call_target="tpu_custom_call" | custom-call | flops 1000000000 | bytes 4194304 | tf_op jit(solution)/shard_map/outgoing/pallas_call | solution.py:321
  47.7 3.2 %all-to-all-done.2.parts_ref = bf16[32,32,128]{2,1,0:T(8,128)(2,1)S(1)} async-done(((bf16[32,32,128]{2,1,0:T(8,128)(2,1)}), bf16[32,32,128]{2,1,0:T(8,128)(2,1)S(1)}, u32[]{:S(2)}, u32[]{:S(2)}) %all-to-all-start.2) | async-done | bytes 262176 | tf_op jit(solution)/shard_map/all_to_all | solution.py:468
  51.0 4.3 %all-to-all-start.1 = ((bf16[32,96,128]{2,1,0:T(8,128)(2,1)}), bf16[32,96,128]{2,1,0:T(8,128)(2,1)S(1)}, u32[]{:S(2)}, u32[]{:S(2)}) async-start(bf16[32,96,128]{2,1,0:T(8,128)(2,1)} %outgoing.1.after_hbm), calls=%async_computation.1 | async-start | bytes 1572864 | tf_op jit(solution)/shard_map/all_to_all | solution.py:468
  55.3 0.1 summed.1.own_ref
  55.3 3.8 %collective-permute-start.2 = (f32[32,128]{1,0:T(8,128)S(1)}, f32[32,128]{1,0:T(8,128)S(1)}, u32[]{:S(2)}, u32[]{:S(2)}) collective-permute-start(f32[32,128]{1,0:T(8,128)S(1)} %summed.1.own_ref), channel_id=1, source_target_pairs={{0,96},{32,64},{64,32},{96,0},{1,97},{33,65},{65,33},{97,1},{2,98}... | collective-permute-start | bytes 49160 | tf_op jit(solution)/shard_map/ppermute | solution.py:485
  59.2 0.0 collective-permute-start.1
  59.2 0.7 collective-permute-start
  59.8 0.8 collective-permute-done.2.across_ref
  60.6 3.0 %collective-permute-done.1.far_ref = f32[32,128]{1,0:T(8,128)S(1)} collective-permute-done((f32[32,128]{1,0:T(8,128)S(1)}, f32[32,128]{1,0:T(8,128)S(1)}, u32[]{:S(2)}, u32[]{:S(2)}) %collective-permute-start.1) | collective-permute-done | bytes 16416 | tf_op jit(solution)/shard_map/ppermute | solution.py:485
  63.6 0.0 collective-permute-done.near_ref
  63.6 5.9 %all-to-all-done.1.got_hbm.after_hbm = bf16[32,96,128]{2,1,0:T(8,128)(2,1)S(1)} async-done(((bf16[32,96,128]{2,1,0:T(8,128)(2,1)}), bf16[32,96,128]{2,1,0:T(8,128)(2,1)S(1)}, u32[]{:S(2)}, u32[]{:S(2)}) %all-to-all-start.1) | async-done | bytes 786464 | tf_op jit(solution)/shard_map/all_to_all | solution.py:468
  69.5 0.7 shares.1
  70.2 4.3 %all-to-all-start.3 = ((bf16[32,32,128]{2,1,0:T(8,128)(2,1)}), bf16[32,32,128]{2,1,0:T(8,128)(2,1)S(1)}, u32[]{:S(2)}, u32[]{:S(2)}) async-start(bf16[32,32,128]{2,1,0:T(8,128)(2,1)} %shares.1), calls=%async_computation.3 | async-start | bytes 524288 | tf_op jit(solution)/shard_map/all_to_all | solution.py:468
  74.5 0.0 copy-done
  74.5 0.0 copy-done.4
  74.6 6.4 %back.1 = bf16[2048,256]{1,0:T(8,128)(2,1)} custom-call(bf16[32,96,128]{2,1,0:T(8,128)(2,1)S(1)} %all-to-all-done.1.got_hbm.after_hbm, bf16[2048,256]{1,0:T(8,128)(2,1)S(1)} %copy-done, s32[1,32]{1,0:T(1,128)S(1)} %copy-done.4, bf16[2048,1536]{1,0:T(8,128)(2,1)} %adjacency.1.adj_hbm, bf16[256,256]{1,0:T(8,128)(2,1)S(1)} %copy-done.1), custom_call_target="tpu_custom_call" | custom-call | flops 1000000000 | bytes 8257664 | tf_op jit(solution)/shard_map/back/pallas_call | solution.py:321
  80.9 2.6 %all-to-all-done.3.sum_ref = bf16[32,32,128]{2,1,0:T(8,128)(2,1)S(1)} async-done(((bf16[32,32,128]{2,1,0:T(8,128)(2,1)}), bf16[32,32,128]{2,1,0:T(8,128)(2,1)S(1)}, u32[]{:S(2)}, u32[]{:S(2)}) %all-to-all-start.3) | async-done | bytes 262176 | tf_op jit(solution)/shard_map/all_to_all | solution.py:468
  83.6 1.1 %update.1 = (f32[256,256]{1,0:T(8,128)}, f32[256,256]{1,0:T(8,128)}) custom-call(bf16[32,32,128]{2,1,0:T(8,128)(2,1)S(1)} %all-to-all-done.3.sum_ref, bf16[256,256]{1,0:T(8,128)(2,1)S(1)} %copy-done.1, bf16[256,256]{1,0:T(8,128)(2,1)S(1)} %copy-done.2), custom_call_target="tpu_custom_call" | custom-call | flops 1000000000 | bytes 524288 | tf_op jit(solution)/shard_map/update/pallas_call | solution.py:321
Async XLA Ops:
  7.7 24.4 %all-to-all-start = ((bf16[32,112,128]{2,1,0:T(8,128)(2,1)}), bf16[32,112,128]{2,1,0:T(8,128)(2,1)S(1)}, u32[]{:S(2)}, u32[]{:S(2)}) async-start(bf16[32,112,128]{2,1,0:T(8,128)(2,1)} %scatter.1), calls=%async_computation | async-start | bytes 1835008 | tf_op jit(solution)/shard_map/all_to_all | solution.py:468
  16.3 15.8 %copy-start.1 = (bf16[256,256]{1,0:T(8,128)(2,1)S(1)}, bf16[256,256]{1,0:T(8,128)(2,1)}, u32[]{:S(2)}) copy-start(bf16[256,256]{1,0:T(8,128)(2,1)} %ws_ref.3) | copy-start | bytes 393220
  16.3 15.7 %copy-start.2 = (bf16[256,256]{1,0:T(8,128)(2,1)S(1)}, bf16[256,256]{1,0:T(8,128)(2,1)}, u32[]{:S(2)}) copy-start(bf16[256,256]{1,0:T(8,128)(2,1)} %wn_ref.5) | copy-start | bytes 393220
  16.4 15.7 %copy-start.3 = (s32[16]{0:T(128)S(1)}, s32[16]{0:T(128)}, u32[]{:S(2)}) copy-start(s32[16]{0:T(128)} %ages_hbm.1) | copy-start | bytes 196
  37.9 36.7 %copy-start = (bf16[2048,256]{1,0:T(8,128)(2,1)S(1)}, bf16[2048,256]{1,0:T(8,128)(2,1)}, u32[]{:S(2)}) copy-start(bf16[2048,256]{1,0:T(8,128)(2,1)} %get-tuple-element.11.gp_hbm) | copy-start | bytes 3145732
  37.9 36.7 %copy-start.4 = (s32[1,32]{1,0:T(1,128)S(1)}, s32[1,32]{1,0:T(1,128)}, u32[]{:S(2)}) copy-start(s32[1,32]{1,0:T(1,128)} %counts_hbm.3) | copy-start | bytes 388
  37.9 13.1 %all-to-all-start.2 = ((bf16[32,32,128]{2,1,0:T(8,128)(2,1)}), bf16[32,32,128]{2,1,0:T(8,128)(2,1)S(1)}, u32[]{:S(2)}, u32[]{:S(2)}) async-start(bf16[32,32,128]{2,1,0:T(8,128)(2,1)} %get-tuple-element.13), calls=%async_computation.2 | async-start | bytes 524288 | tf_op jit(solution)/shard_map/all_to_all | solution.py:468
  51.0 18.5 %all-to-all-start.1 = ((bf16[32,96,128]{2,1,0:T(8,128)(2,1)}), bf16[32,96,128]{2,1,0:T(8,128)(2,1)S(1)}, u32[]{:S(2)}, u32[]{:S(2)}) async-start(bf16[32,96,128]{2,1,0:T(8,128)(2,1)} %outgoing.1.after_hbm), calls=%async_computation.1 | async-start | bytes 1572864 | tf_op jit(solution)/shard_map/all_to_all | solution.py:468
  55.3 5.3 %collective-permute-start.2 = (f32[32,128]{1,0:T(8,128)S(1)}, f32[32,128]{1,0:T(8,128)S(1)}, u32[]{:S(2)}, u32[]{:S(2)}) collective-permute-start(f32[32,128]{1,0:T(8,128)S(1)} %summed.1.own_ref), channel_id=1, source_target_pairs={{0,96},{32,64},{64,32},{96,0},{1,97},{33,65},{65,33},{97,1},{2,98}... | collective-permute-start | bytes 49160 | tf_op jit(solution)/shard_map/ppermute | solution.py:485
  59.2 4.4 %collective-permute-start.1 = (f32[32,128]{1,0:T(8,128)S(1)}, f32[32,128]{1,0:T(8,128)S(1)}, u32[]{:S(2)}, u32[]{:S(2)}) collective-permute-start(f32[32,128]{1,0:T(8,128)S(1)} %summed.1.own_ref), channel_id=1, source_target_pairs={{0,64},{32,96},{64,0},{96,32},{1,65},{33,97},{65,1},{97,33},{2,66}... | collective-permute-start | bytes 49160 | tf_op jit(solution)/shard_map/ppermute | solution.py:485
  59.2 4.4 %collective-permute-start = (f32[32,128]{1,0:T(8,128)S(1)}, f32[32,128]{1,0:T(8,128)S(1)}, u32[]{:S(2)}, u32[]{:S(2)}) collective-permute-start(f32[32,128]{1,0:T(8,128)S(1)} %summed.1.own_ref), channel_id=1, source_target_pairs={{0,32},{32,0},{64,96},{96,64},{1,33},{33,1},{65,97},{97,65},{2,34}... | collective-permute-start | bytes 49160 | tf_op jit(solution)/shard_map/ppermute | solution.py:485
  70.2 13.3 %all-to-all-start.3 = ((bf16[32,32,128]{2,1,0:T(8,128)(2,1)}), bf16[32,32,128]{2,1,0:T(8,128)(2,1)S(1)}, u32[]{:S(2)}, u32[]{:S(2)}) async-start(bf16[32,32,128]{2,1,0:T(8,128)(2,1)} %shares.1), calls=%async_computation.3 | async-start | bytes 524288 | tf_op jit(solution)/shard_map/all_to_all | solution.py:468

commit v6 on v5

--- a/solution.py
+++ b/solution.py
@@ -12,7 +12,8 @@
 F32 = jnp.float32
 TILE = 128
 ROWS = 512
-INDEX_ROWS = 16
+FINE = 256
+INDEX_ROWS = 8
 GATHER_STEPS = 4
 NN = (((1,), (0,)), ((), ()))
 NT = (((1,), (1,)), ((), ()))
@@ -123,7 +124,7 @@
 
 def index_digits(cap, got_ref):
     peers = got_ref.shape[0]
-    coded = got_ref[:, 2 * cap :, :].reshape(peers * INDEX_ROWS, TILE)
+    coded = got_ref[:, 2 * cap :, :].astype(F32).reshape(peers * INDEX_ROWS, TILE).astype(BF)
     pick_row = lax.broadcasted_iota(jnp.int32, (peers, peers * INDEX_ROWS), 1)
     pick_peer = lax.broadcasted_iota(jnp.int32, (peers, peers * INDEX_ROWS), 0) * INDEX_ROWS
     high = dot(mask(pick_row == pick_peer), coded, NN).astype(BF)
@@ -184,10 +185,11 @@
         copy.wait()
     total = None
     outs = []
-    for block in range(blocks):
-        rows = slice(block * ROWS, (block + 1) * ROWS)
+    fine = FINE // TILE
+    for block in range(verts // FINE):
+        rows = slice(block * FINE, (block + 1) * FINE)
         aged = []
-        for k in range(block * per, (block + 1) * per):
+        for k in range(block * fine, (block + 1) * fine):
             age = jnp.full((1, width), ages_ref[k], jnp.int32).astype(F32)
             aged.append(stale_ref[k * TILE : (k + 1) * TILE, :].astype(F32) * (1.0 / (1.0 + age)))
         agg = agg_ref[rows, :] + jnp.concatenate(aged, axis=0)
@@ -200,7 +202,7 @@
         hidden_ref[rows, :] = (pre * sig).astype(BF)
         gp = (cot_ref[rows, :].astype(F32) * sig * (1.0 + pre * (1.0 - sig))).astype(BF)
         gp_ref[rows, :] = gp
-        part = pl.ds(block * ROWS, ROWS)
+        part = pl.ds(block * FINE, FINE)
         for near, far in ((agg_ref, agg_hbm), (gp_ref, gp_hbm), (hidden_ref, hidden_hbm)):
             copy = pltpu.make_async_copy(near.at[part], far.at[part], out_sems.at[len(outs)])
             copy.start()
@@ -259,25 +261,15 @@
 
 
 def back_kernel(
-    cap, got_hbm, gp_hbm, counts_hbm, adj_hbm, ws_hbm, out_hbm, got_ref, gp_ref, counts_ref, adj_ref, ws_ref, grad_ref, out_ref, sems, out_sems
+    cap, got_ref, gp_ref, ws_ref, counts_hbm, adj_hbm, out_hbm, counts_ref, adj_ref, grad_ref, out_ref, sems, out_sems
 ):
-    verts = out_ref.shape[0]
-    blocks = verts // ROWS
-    pairs = [
-        (counts_hbm, counts_ref),
-        (got_hbm, got_ref),
-        (ws_hbm, ws_ref),
-        (gp_hbm, gp_ref),
-    ]
-    for block in range(blocks):
-        part = pl.ds(block * ROWS, ROWS)
-        pairs.append((adj_hbm.at[part], adj_ref.at[part]))
-    copies = start_all(pairs, sems)
-    peers = got_ref.shape[0]
+    parts = [pl.ds(block * ROWS, ROWS) for block in range(out_ref.shape[0] // ROWS)]
+    copies = start_all(
+        [(counts_hbm, counts_ref)] + [(adj_hbm.at[part], adj_ref.at[part]) for part in parts], sems
+    )
     copies[0].wait()
-    copies[1].wait()
     slot_in_peer = lax.broadcasted_iota(jnp.int32, (cap, TILE), 0)
-    for q in range(peers):
+    for q in range(got_ref.shape[0]):
         live = slot_in_peer < counts_ref[0, q]
         for half in range(2):
             rows = got_ref[q, half * cap : (half + 1) * cap, :]
@@ -285,14 +277,11 @@
                 live, rows.astype(F32), 0.0
             ).astype(BF)
     outs = []
-    copies[2].wait()
-    copies[3].wait()
-    for block in range(blocks):
+    for block, part in enumerate(parts):
         rows = slice(block * ROWS, (block + 1) * ROWS)
         own = dot(gp_ref[rows, :], ws_ref[...], NT)
-        copies[4 + block].wait()
+        copies[1 + block].wait()
         out_ref[rows, :] = (dot(adj_ref[rows, :], grad_ref[...], NN) + own).astype(BF)
-        part = pl.ds(block * ROWS, ROWS)
         copy = pltpu.make_async_copy(out_ref.at[part], out_hbm.at[part], out_sems.at[block])
         copy.start()
         outs.append(copy)
@@ -406,7 +395,7 @@
             like(feats),
             pltpu.VMEM((verts, width), F32),
             pltpu.SemaphoreType.DMA((4,)),
-            pltpu.SemaphoreType.DMA((3 * (verts // ROWS),)),
+            pltpu.SemaphoreType.DMA((3 * (verts // FINE),)),
         ],
         limit=52,
     )
@@ -441,19 +430,16 @@
     return call(
         functools.partial(back_kernel, cap),
         "back",
-        (got, gp, slot_counts, adj, ws),
-        0,
+        (got, gp, ws, slot_counts, adj),
+        3,
         [shape(gp.shape)],
         (),
         [
-            pltpu.VMEM((got.shape[0], 2 * cap, TILE), BF),
-            like(gp),
             pltpu.SMEM(slot_counts.shape, jnp.int32),
             like(adj),
-            like(ws),
             pltpu.VMEM((got.shape[0] * cap, gp.shape[1]), BF),
             like(gp),
-            pltpu.SemaphoreType.DMA((4 + blocks,)),
+            pltpu.SemaphoreType.DMA((1 + blocks,)),
             pltpu.SemaphoreType.DMA((blocks,)),
         ],
         limit=50,

time: 85.1 us -> 84.3 us (level)
  no operation moved by 1% of the time
where the time goes in v6:
time: 84.3 us; the launch traced here: 83.7 us
  Pallas kernels  32 us (38%)
  starting transfers between devices  25.8 us (31%)
  waiting for transfers between devices  25.2 us (30%)
    pallas_call x8, Pallas kernels, call(): pl.pallas_call(kernel, name=name, in_specs=[VMEM if k < near else HBM for...  32 us
    all_to_all x4, waiting for transfers between devices, exchange(): return lax.all_to_all(x, 'dom', split_axis=0, concat_axis=0, tiled=True)  21.5 us
    all_to_all x4, starting transfers between devices, exchange(): return lax.all_to_all(x, 'dom', split_axis=0, concat_axis=0, tiled=True)  21.2 us
    ppermute x3, starting transfers between devices, body(): lax.ppermute(own, 'group', [(k, k ^ other) for k in groups])  4.51 us
    ppermute x3, waiting for transfers between devices, body(): lax.ppermute(own, 'group', [(k, k ^ other) for k in groups])  3.72 us
  transfers between devices with their start and end apart: 7, of which 6 were waited for; matrix products, arithmetic and copies ran while one was open for 0% of the time, Pallas kernels for 21%

profile of v6, /device:TPU:1, one launch (start us, length us, event | category | flops | bytes accessed | tf_op | source)
XLA Modules:
  0.0 83.7 jit_solution(4277481667544019325)
XLA Ops:
  0.6 7.1 %scatter.1 = bf16[32,104,128]{2,1,0:T(8,128)(2,1)} custom-call(s32[1,32]{1,0:T(1,128)} %counts_hbm.3, s32[1,32,48]{2,1,0:T(8,128)} %rows_hbm.1, s32[1,8192]{1,0:T(1,128)} %src_hbm.3, s32[1,8192]{1,0:T(1,128)} %slot_hbm.3, bf16[2048,256]{1,0:T(8,128)(2,1)} %feats_hbm.3), custom_call_target="tpu_custom_call" | custom-call | flops 1000000000 | bytes 1120384 | tf_op jit(solution)/shard_map/scatter/pallas_call | solution.py:310
  7.7 8.6 %all-to-all-start = ((bf16[32,104,128]{2,1,0:T(8,128)(2,1)}), bf16[32,104,128]{2,1,0:T(8,128)(2,1)S(1)}, u32[]{:S(2)}, u32[]{:S(2)}) async-start(bf16[32,104,128]{2,1,0:T(8,128)(2,1)} %scatter.1), calls=%async_computation | async-start | bytes 1703936 | tf_op jit(solution)/shard_map/all_to_all | solution.py:454
  16.3 0.0 copy-start.1
  16.4 0.0 copy-start.2
  16.4 0.0 copy-start.4
  16.4 5.7 %adjacency.1.adj_hbm = bf16[2048,1536]{1,0:T(8,128)(2,1)} custom-call(s32[1,8192]{1,0:T(1,128)} %src_hbm.3, s32[1,8192]{1,0:T(1,128)} %slot_hbm.3), custom_call_target="tpu_custom_call" | custom-call | flops 6000000000 | bytes 65536 | tf_op jit(solution)/shard_map/adjacency/pallas_call | solution.py:310
  22.1 9.3 %all-to-all-done.got_ref = bf16[32,104,128]{2,1,0:T(8,128)(2,1)S(1)} async-done(((bf16[32,104,128]{2,1,0:T(8,128)(2,1)}), bf16[32,104,128]{2,1,0:T(8,128)(2,1)S(1)}, u32[]{:S(2)}, u32[]{:S(2)}) %all-to-all-start) | async-done | bytes 852000 | tf_op jit(solution)/shard_map/all_to_all | solution.py:454
  31.4 0.0 copy-done.1
  31.4 0.0 copy-done.2
  31.4 0.0 copy-done.4
  31.4 5.6 %masters.1 = (bf16[2048,256]{1,0:T(8,128)(2,1)}, bf16[2048,256]{1,0:T(8,128)(2,1)}, f32[2048,256]{1,0:T(8,128)}, bf16[32,32,128]{2,1,0:T(8,128)(2,1)}) custom-call(bf16[32,104,128]{2,1,0:T(8,128)(2,1)S(1)} %all-to-all-done.got_ref, bf16[256,256]{1,0:T(8,128)(2,1)S(1)} %copy-done.1, bf16[256,256]{1,0:T(8,128)(2,1)S(1)} %copy-done.2, ...), custom_call_target="tpu_custom_call" | custom-call | flops 1000000000 | bytes 10551360 | tf_op jit(solution)/shard_map/masters/pallas_call | solution.py:310
  37.0 0.0 copy-start
  37.0 0.0 copy-start.3
  37.0 4.1 %all-to-all-start.2 = ((bf16[32,32,128]{2,1,0:T(8,128)(2,1)}), bf16[32,32,128]{2,1,0:T(8,128)(2,1)S(1)}, u32[]{:S(2)}, u32[]{:S(2)}) async-start(bf16[32,32,128]{2,1,0:T(8,128)(2,1)} %get-tuple-element.13), calls=%async_computation.2 | async-start | bytes 524288 | tf_op jit(solution)/shard_map/all_to_all | solution.py:454
  41.1 5.8 %outgoing.1.after_hbm = bf16[32,96,128]{2,1,0:T(8,128)(2,1)} custom-call(bf16[32,104,128]{2,1,0:T(8,128)(2,1)S(1)} %all-to-all-done.got_ref, bf16[256,256]{1,0:T(8,128)(2,1)S(1)} %copy-done.2, bf16[2048,256]{1,0:T(8,128)(2,1)} %get-tuple-element.11.gp_hbm.gp_ref, f32[2048,256]{1,0:T(8,128)} %get-tuple-element.12.agg_hbm), custom_call_target="tpu_custom_call" | custom-call | flops 1000000000 | bytes 4128768 | tf_op jit(solution)/shard_map/outgoing/pallas_call | solution.py:310
  46.8 3.3 %all-to-all-done.2.parts_ref = bf16[32,32,128]{2,1,0:T(8,128)(2,1)S(1)} async-done(((bf16[32,32,128]{2,1,0:T(8,128)(2,1)}), bf16[32,32,128]{2,1,0:T(8,128)(2,1)S(1)}, u32[]{:S(2)}, u32[]{:S(2)}) %all-to-all-start.2) | async-done | bytes 262176 | tf_op jit(solution)/shard_map/all_to_all | solution.py:454
  50.1 4.3 %all-to-all-start.1 = ((bf16[32,96,128]{2,1,0:T(8,128)(2,1)}), bf16[32,96,128]{2,1,0:T(8,128)(2,1)S(1)}, u32[]{:S(2)}, u32[]{:S(2)}) async-start(bf16[32,96,128]{2,1,0:T(8,128)(2,1)} %outgoing.1.after_hbm), calls=%async_computation.1 | async-start | bytes 1572864 | tf_op jit(solution)/shard_map/all_to_all | solution.py:454
  54.4 0.1 summed.1.own_ref
  54.4 3.8 %collective-permute-start.2 = (f32[32,128]{1,0:T(8,128)S(1)}, f32[32,128]{1,0:T(8,128)S(1)}, u32[]{:S(2)}, u32[]{:S(2)}) collective-permute-start(f32[32,128]{1,0:T(8,128)S(1)} %summed.1.own_ref), channel_id=1, source_target_pairs={{0,96},{32,64},{64,32},{96,0},{1,97},{33,65},{65,33},{97,1},{2,98}... | collective-permute-start | bytes 49160 | tf_op jit(solution)/shard_map/ppermute | solution.py:471
  58.3 0.0 collective-permute-start.1
  58.3 0.7 collective-permute-start
  58.9 0.8 collective-permute-done.2.across_ref
  59.7 3.0 %collective-permute-done.1.far_ref = f32[32,128]{1,0:T(8,128)S(1)} collective-permute-done((f32[32,128]{1,0:T(8,128)S(1)}, f32[32,128]{1,0:T(8,128)S(1)}, u32[]{:S(2)}, u32[]{:S(2)}) %collective-permute-start.1) | collective-permute-done | bytes 16416 | tf_op jit(solution)/shard_map/ppermute | solution.py:471
  62.7 0.0 collective-permute-done.near_ref
  62.7 5.9 %all-to-all-done.1.got_ref.after_hbm = bf16[32,96,128]{2,1,0:T(8,128)(2,1)S(1)} async-done(((bf16[32,96,128]{2,1,0:T(8,128)(2,1)}), bf16[32,96,128]{2,1,0:T(8,128)(2,1)S(1)}, u32[]{:S(2)}, u32[]{:S(2)}) %all-to-all-start.1) | async-done | bytes 786464 | tf_op jit(solution)/shard_map/all_to_all | solution.py:454
  68.6 0.7 shares.1
  69.3 4.3 %all-to-all-start.3 = ((bf16[32,32,128]{2,1,0:T(8,128)(2,1)}), bf16[32,32,128]{2,1,0:T(8,128)(2,1)S(1)}, u32[]{:S(2)}, u32[]{:S(2)}) async-start(bf16[32,32,128]{2,1,0:T(8,128)(2,1)} %shares.1), calls=%async_computation.3 | async-start | bytes 524288 | tf_op jit(solution)/shard_map/all_to_all | solution.py:454
  73.6 0.0 copy-done
  73.7 0.0 copy-done.3
  73.7 6.0 %back.1 = bf16[2048,256]{1,0:T(8,128)(2,1)} custom-call(bf16[32,96,128]{2,1,0:T(8,128)(2,1)S(1)} %all-to-all-done.1.got_ref.after_hbm, bf16[2048,256]{1,0:T(8,128)(2,1)S(1)} %copy-done, bf16[256,256]{1,0:T(8,128)(2,1)S(1)} %copy-done.1, s32[1,32]{1,0:T(1,128)S(1)} %copy-done.3, bf16[2048,1536]{1,0:T(8,128)(2,1)} %adjacency.1.adj_hbm), custom_call_target="tpu_custom_call" | custom-call | flops 1000000000 | bytes 8257664 | tf_op jit(solution)/shard_map/back/pallas_call | solution.py:310
  79.7 2.9 %all-to-all-done.3.sum_ref = bf16[32,32,128]{2,1,0:T(8,128)(2,1)S(1)} async-done(((bf16[32,32,128]{2,1,0:T(8,128)(2,1)}), bf16[32,32,128]{2,1,0:T(8,128)(2,1)S(1)}, u32[]{:S(2)}, u32[]{:S(2)}) %all-to-all-start.3) | async-done | bytes 262176 | tf_op jit(solution)/shard_map/all_to_all | solution.py:454
  82.7 1.1 %update.1 = (f32[256,256]{1,0:T(8,128)}, f32[256,256]{1,0:T(8,128)}) custom-call(bf16[32,32,128]{2,1,0:T(8,128)(2,1)S(1)} %all-to-all-done.3.sum_ref, bf16[256,256]{1,0:T(8,128)(2,1)S(1)} %copy-done.1, bf16[256,256]{1,0:T(8,128)(2,1)S(1)} %copy-done.2), custom_call_target="tpu_custom_call" | custom-call | flops 1000000000 | bytes 524288 | tf_op jit(solution)/shard_map/update/pallas_call | solution.py:310
Async XLA Ops:
  7.7 23.7 %all-to-all-start = ((bf16[32,104,128]{2,1,0:T(8,128)(2,1)}), bf16[32,104,128]{2,1,0:T(8,128)(2,1)S(1)}, u32[]{:S(2)}, u32[]{:S(2)}) async-start(bf16[32,104,128]{2,1,0:T(8,128)(2,1)} %scatter.1), calls=%async_computation | async-start | bytes 1703936 | tf_op jit(solution)/shard_map/all_to_all | solution.py:454
  16.3 15.1 %copy-start.1 = (bf16[256,256]{1,0:T(8,128)(2,1)S(1)}, bf16[256,256]{1,0:T(8,128)(2,1)}, u32[]{:S(2)}) copy-start(bf16[256,256]{1,0:T(8,128)(2,1)} %ws_ref.5) | copy-start | bytes 393220
  16.4 15.0 %copy-start.2 = (bf16[256,256]{1,0:T(8,128)(2,1)S(1)}, bf16[256,256]{1,0:T(8,128)(2,1)}, u32[]{:S(2)}) copy-start(bf16[256,256]{1,0:T(8,128)(2,1)} %wn_ref.5) | copy-start | bytes 393220
  16.4 15.0 %copy-start.4 = (s32[16]{0:T(128)S(1)}, s32[16]{0:T(128)}, u32[]{:S(2)}) copy-start(s32[16]{0:T(128)} %ages_hbm.1) | copy-start | bytes 196
  37.0 36.7 %copy-start = (bf16[2048,256]{1,0:T(8,128)(2,1)S(1)}, bf16[2048,256]{1,0:T(8,128)(2,1)}, u32[]{:S(2)}) copy-start(bf16[2048,256]{1,0:T(8,128)(2,1)} %get-tuple-element.11.gp_hbm.gp_ref) | copy-start | bytes 3145732
  37.0 36.7 %copy-start.3 = (s32[1,32]{1,0:T(1,128)S(1)}, s32[1,32]{1,0:T(1,128)}, u32[]{:S(2)}) copy-start(s32[1,32]{1,0:T(1,128)} %counts_hbm.3) | copy-start | bytes 388
  37.0 13.1 %all-to-all-start.2 = ((bf16[32,32,128]{2,1,0:T(8,128)(2,1)}), bf16[32,32,128]{2,1,0:T(8,128)(2,1)S(1)}, u32[]{:S(2)}, u32[]{:S(2)}) async-start(bf16[32,32,128]{2,1,0:T(8,128)(2,1)} %get-tuple-element.13), calls=%async_computation.2 | async-start | bytes 524288 | tf_op jit(solution)/shard_map/all_to_all | solution.py:454
  50.1 18.5 %all-to-all-start.1 = ((bf16[32,96,128]{2,1,0:T(8,128)(2,1)}), bf16[32,96,128]{2,1,0:T(8,128)(2,1)S(1)}, u32[]{:S(2)}, u32[]{:S(2)}) async-start(bf16[32,96,128]{2,1,0:T(8,128)(2,1)} %outgoing.1.after_hbm), calls=%async_computation.1 | async-start | bytes 1572864 | tf_op jit(solution)/shard_map/all_to_all | solution.py:454
  54.4 5.3 %collective-permute-start.2 = (f32[32,128]{1,0:T(8,128)S(1)}, f32[32,128]{1,0:T(8,128)S(1)}, u32[]{:S(2)}, u32[]{:S(2)}) collective-permute-start(f32[32,128]{1,0:T(8,128)S(1)} %summed.1.own_ref), channel_id=1, source_target_pairs={{0,96},{32,64},{64,32},{96,0},{1,97},{33,65},{65,33},{97,1},{2,98}... | collective-permute-start | bytes 49160 | tf_op jit(solution)/shard_map/ppermute | solution.py:471
  58.3 4.4 %collective-permute-start.1 = (f32[32,128]{1,0:T(8,128)S(1)}, f32[32,128]{1,0:T(8,128)S(1)}, u32[]{:S(2)}, u32[]{:S(2)}) collective-permute-start(f32[32,128]{1,0:T(8,128)S(1)} %summed.1.own_ref), channel_id=1, source_target_pairs={{0,64},{32,96},{64,0},{96,32},{1,65},{33,97},{65,1},{97,33},{2,66}... | collective-permute-start | bytes 49160 | tf_op jit(solution)/shard_map/ppermute | solution.py:471
  58.3 4.4 %collective-permute-start = (f32[32,128]{1,0:T(8,128)S(1)}, f32[32,128]{1,0:T(8,128)S(1)}, u32[]{:S(2)}, u32[]{:S(2)}) collective-permute-start(f32[32,128]{1,0:T(8,128)S(1)} %summed.1.own_ref), channel_id=1, source_target_pairs={{0,32},{32,0},{64,96},{96,64},{1,33},{33,1},{65,97},{97,65},{2,34}... | collective-permute-start | bytes 49160 | tf_op jit(solution)/shard_map/ppermute | solution.py:471
  69.3 13.3 %all-to-all-start.3 = ((bf16[32,32,128]{2,1,0:T(8,128)(2,1)}), bf16[32,32,128]{2,1,0:T(8,128)(2,1)S(1)}, u32[]{:S(2)}, u32[]{:S(2)}) async-start(bf16[32,32,128]{2,1,0:T(8,128)(2,1)} %shares.1), calls=%async_computation.3 | async-start | bytes 524288 | tf_op jit(solution)/shard_map/all_to_all | solution.py:454

commit v7 on v6

--- a/solution.py
+++ b/solution.py
@@ -29,6 +29,10 @@
     return jnp.where(cond, 1.0, 0.0).astype(BF)
 
 
+def mask16(cond):
+    return jnp.where(cond, jnp.ones((), BF), jnp.zeros((), BF))
+
+
 def start_all(pairs, sems):
     copies = [pltpu.make_async_copy(src, dst, sems.at[k]) for k, (src, dst) in enumerate(pairs)]
     for copy in copies:
@@ -45,9 +49,9 @@
 def bin_indicators(src_ref, slot_ref, b, bins, repeats, slots):
     src = bin_edges(src_ref, b, bins, repeats) & (TILE - 1)
     slot = bin_edges(slot_ref, b, bins, repeats)
-    row = lax.broadcasted_iota(jnp.int32, (TILE, src.shape[1]), 0)
-    source = mask(row == src).astype(F8)
-    low = mask(row == (slot & (TILE - 1)))
+    row = lax.broadcasted_iota(jnp.int16, (TILE, src.shape[1]), 0)
+    source = mask16(row == src.astype(jnp.int16)).astype(F8)
+    low = mask16(row == (slot & (TILE - 1)).astype(jnp.int16))
     high = slot >> 7
     return source, [(low * mask(high == h)).astype(F8) for h in range(slots // TILE)]
 
@@ -172,8 +176,8 @@
     least = lax.broadcasted_iota(jnp.int32, (peers, slots), 0) * cap
     own = (slot >= least) & (slot < least + cap)
     row_index = jnp.sum(jnp.where(own, value, 0.0), axis=0, keepdims=True).astype(jnp.int32)
-    sub = lax.broadcasted_iota(jnp.int32, (TILE, slots), 0)
-    low_hot = mask(sub == (row_index & (TILE - 1)))
+    sub = lax.broadcasted_iota(jnp.int16, (TILE, slots), 0)
+    low_hot = mask16(sub == (row_index & (TILE - 1)).astype(jnp.int16))
     row_high = row_index >> 7
     arr_ref[:, :TILE] = got_ref[:, 0:cap, :].reshape(slots, TILE)
     arr_ref[:, TILE:] = got_ref[:, cap : 2 * cap, :].reshape(slots, TILE)
@@ -245,8 +249,8 @@
     step = peers // GATHER_STEPS
     for first in range(0, peers, step):
         part = slice(first * cap, (first + step) * cap)
-        lanes = lax.broadcasted_iota(jnp.int32, (step * cap, verts), 1)
-        rows = dot(mask(lanes == index[part, :]), ga_ref[...], NN).astype(BF)
+        lanes = lax.broadcasted_iota(jnp.int16, (step * cap, verts), 1)
+        rows = dot(mask16(lanes == index[part, :].astype(jnp.int16)), ga_ref[...], NN).astype(BF)
         out_ref[first : first + step, 0:cap, :] = rows[:, :TILE].reshape(step, cap, TILE)
         out_ref[first : first + step, cap:, :] = rows[:, TILE:].reshape(step, cap, TILE)
 
@@ -255,7 +259,11 @@
     out_ref[...] = jnp.sum(parts_ref[...].astype(F32), axis=0)
 
 
-def share_kernel(own_ref, near_ref, far_ref, across_ref, after_hbm, out_ref):
+def tie_kernel(values_hbm, after_hbm, out_hbm):
+    pass
+
+
+def share_kernel(own_ref, near_ref, far_ref, across_ref, out_ref):
     total = (own_ref[...] + near_ref[...]) + (far_ref[...] + across_ref[...])
     out_ref[...] = jnp.broadcast_to(total.astype(BF)[None], out_ref.shape)
 
@@ -418,11 +426,21 @@
     return call(sum_kernel, "summed", (parts, after), 1, [shape(parts.shape[1:], F32)], (0,), flops=10**6, limit=16)[0]
 
 
-def shares(parts, after):
-    peers = after.shape[0]
-    return call(
-        share_kernel, "shares", (*parts, after), 4, [shape((peers,) + parts[0].shape)], (0,), flops=10**6, limit=16
-    )[0]
+def shares(parts, peers):
+    return call(share_kernel, "shares", parts, 4, [shape((peers,) + parts[0].shape)], (0,), flops=10**6, limit=16)[0]
+
+
+def tied(values, after):
+    return pl.pallas_call(
+        tie_kernel,
+        name="tied",
+        in_specs=[HBM, HBM],
+        out_specs=HBM,
+        out_shape=shape(values.shape),
+        input_output_aliases={0: 0},
+        compiler_params=pltpu.CompilerParams(vmem_limit_bytes=16 * MIB),
+        cost_estimate=pl.CostEstimate(flops=0, bytes_accessed=0, transcendentals=0),
+    )(values, after)
 
 
 def back(cap, got, gp, slot_counts, adj, ws):
@@ -470,7 +488,7 @@
     groups = range(lax.axis_size("group"))
     others = [lax.ppermute(own, "group", [(k, k ^ other) for k in groups]) for other in (1, 2, 3)]
     returned = exchange(sent)
-    sums = exchange(shares((own, *others), returned))
+    sums = exchange(tied(shares((own, *others), peers), returned))
     feat_grad = back(cap, returned, grad_pre, slot_counts, adj, w_self)
     new_self, new_neigh = update(sums, w_self, w_neigh)
     return (hidden, feat_grad, new_self, new_neigh)

time: 84.3 us -> 83.1 us (0.986)
  transfers between devices with their start and end apart: 7 -> 7, of which waited for: 6 -> 6; matrix products, arithmetic and copies ran while one was open for 0% -> 0% of each run, Pallas kernels for 21% -> 22%
where the time goes in v7:
time: 83.1 us; the launch traced here: 82.5 us
  Pallas kernels  31.5 us (38%)
  starting transfers between devices  25.5 us (31%)
  waiting for transfers between devices  24.7 us (30%)
    pallas_call x8, Pallas kernels, call(): pl.pallas_call(kernel, name=name, in_specs=[VMEM if k < near else HBM for...  31.5 us
    all_to_all x4, waiting for transfers between devices, exchange(): return lax.all_to_all(x, 'dom', split_axis=0, concat_axis=0, tiled=True)  21 us
    all_to_all x4, starting transfers between devices, exchange(): return lax.all_to_all(x, 'dom', split_axis=0, concat_axis=0, tiled=True)  21 us
    ppermute x3, starting transfers between devices, body(): lax.ppermute(own, 'group', [(k, k ^ other) for k in groups])  4.5 us
    ppermute x3, waiting for transfers between devices, body(): lax.ppermute(own, 'group', [(k, k ^ other) for k in groups])  3.72 us
  transfers between devices with their start and end apart: 7, of which 6 were waited for; matrix products, arithmetic and copies ran while one was open for 0% of the time, Pallas kernels for 22%

profile of v7, /device:TPU:1, one launch (start us, length us, event | category | flops | bytes accessed | tf_op | source)
XLA Modules:
  0.0 82.5 jit_solution(13415914623869014851)
XLA Ops:
  0.6 6.9 %scatter.1 = bf16[32,104,128]{2,1,0:T(8,128)(2,1)} custom-call(s32[1,32]{1,0:T(1,128)} %counts_hbm.3, s32[1,32,48]{2,1,0:T(8,128)} %rows_hbm.1, s32[1,8192]{1,0:T(1,128)} %src_hbm.3, s32[1,8192]{1,0:T(1,128)} %slot_hbm.3, bf16[2048,256]{1,0:T(8,128)(2,1)} %feats_hbm.3), custom_call_target="tpu_custom_call" | custom-call | flops 1000000000 | bytes 1120384 | tf_op jit(solution)/shard_map/scatter/pallas_call | solution.py:318
  7.5 8.6 %all-to-all-start = ((bf16[32,104,128]{2,1,0:T(8,128)(2,1)}), bf16[32,104,128]{2,1,0:T(8,128)(2,1)S(1)}, u32[]{:S(2)}, u32[]{:S(2)}) async-start(bf16[32,104,128]{2,1,0:T(8,128)(2,1)} %scatter.1), calls=%async_computation | async-start | bytes 1703936 | tf_op jit(solution)/shard_map/all_to_all | solution.py:472
  16.1 0.0 copy-start.1
  16.2 0.0 copy-start.2
  16.2 0.0 copy-start.4
  16.2 5.5 %adjacency.1.adj_hbm = bf16[2048,1536]{1,0:T(8,128)(2,1)} custom-call(s32[1,8192]{1,0:T(1,128)} %src_hbm.3, s32[1,8192]{1,0:T(1,128)} %slot_hbm.3), custom_call_target="tpu_custom_call" | custom-call | flops 6000000000 | bytes 65536 | tf_op jit(solution)/shard_map/adjacency/pallas_call | solution.py:318
  21.6 9.6 %all-to-all-done.got_ref = bf16[32,104,128]{2,1,0:T(8,128)(2,1)S(1)} async-done(((bf16[32,104,128]{2,1,0:T(8,128)(2,1)}), bf16[32,104,128]{2,1,0:T(8,128)(2,1)S(1)}, u32[]{:S(2)}, u32[]{:S(2)}) %all-to-all-start) | async-done | bytes 852000 | tf_op jit(solution)/shard_map/all_to_all | solution.py:472
  31.2 0.0 copy-done.1
  31.2 0.0 copy-done.2
  31.2 0.0 copy-done.4
  31.2 5.6 %masters.1 = (bf16[2048,256]{1,0:T(8,128)(2,1)}, bf16[2048,256]{1,0:T(8,128)(2,1)}, f32[2048,256]{1,0:T(8,128)}, bf16[32,32,128]{2,1,0:T(8,128)(2,1)}) custom-call(bf16[32,104,128]{2,1,0:T(8,128)(2,1)S(1)} %all-to-all-done.got_ref, bf16[256,256]{1,0:T(8,128)(2,1)S(1)} %copy-done.1, bf16[256,256]{1,0:T(8,128)(2,1)S(1)} %copy-done.2, ...), custom_call_target="tpu_custom_call" | custom-call | flops 1000000000 | bytes 10551360 | tf_op jit(solution)/shard_map/masters/pallas_call | solution.py:318
  36.8 0.0 copy-start
  36.8 0.0 copy-start.3
  36.8 4.1 %all-to-all-start.2 = ((bf16[32,32,128]{2,1,0:T(8,128)(2,1)}), bf16[32,32,128]{2,1,0:T(8,128)(2,1)S(1)}, u32[]{:S(2)}, u32[]{:S(2)}) async-start(bf16[32,32,128]{2,1,0:T(8,128)(2,1)} %get-tuple-element.13), calls=%async_computation.2 | async-start | bytes 524288 | tf_op jit(solution)/shard_map/all_to_all | solution.py:472
  40.9 5.7 %outgoing.1.after_hbm = bf16[32,96,128]{2,1,0:T(8,128)(2,1)} custom-call(bf16[32,104,128]{2,1,0:T(8,128)(2,1)S(1)} %all-to-all-done.got_ref, bf16[256,256]{1,0:T(8,128)(2,1)S(1)} %copy-done.2, bf16[2048,256]{1,0:T(8,128)(2,1)} %get-tuple-element.11.gp_hbm.gp_ref, f32[2048,256]{1,0:T(8,128)} %get-tuple-element.12.agg_hbm), custom_call_target="tpu_custom_call" | custom-call | flops 1000000000 | bytes 4128768 | tf_op jit(solution)/shard_map/outgoing/pallas_call | solution.py:318
  46.6 3.3 %all-to-all-done.2.parts_ref = bf16[32,32,128]{2,1,0:T(8,128)(2,1)S(1)} async-done(((bf16[32,32,128]{2,1,0:T(8,128)(2,1)}), bf16[32,32,128]{2,1,0:T(8,128)(2,1)S(1)}, u32[]{:S(2)}, u32[]{:S(2)}) %all-to-all-start.2) | async-done | bytes 262176 | tf_op jit(solution)/shard_map/all_to_all | solution.py:472
  49.9 4.2 %all-to-all-start.1 = ((bf16[32,96,128]{2,1,0:T(8,128)(2,1)}), bf16[32,96,128]{2,1,0:T(8,128)(2,1)S(1)}, u32[]{:S(2)}, u32[]{:S(2)}) async-start(bf16[32,96,128]{2,1,0:T(8,128)(2,1)} %outgoing.1.after_hbm), calls=%async_computation.1 | async-start | bytes 1572864 | tf_op jit(solution)/shard_map/all_to_all | solution.py:472
  54.1 0.1 summed.1.own_ref
  54.2 3.8 %collective-permute-start.2 = (f32[32,128]{1,0:T(8,128)S(1)}, f32[32,128]{1,0:T(8,128)S(1)}, u32[]{:S(2)}, u32[]{:S(2)}) collective-permute-start(f32[32,128]{1,0:T(8,128)S(1)} %summed.1.own_ref), channel_id=1, source_target_pairs={{0,96},{32,64},{64,32},{96,0},{1,97},{33,65},{65,33},{97,1},{2,98}... | collective-permute-start | bytes 49160 | tf_op jit(solution)/shard_map/ppermute | solution.py:489
  58.0 0.0 collective-permute-start.1
  58.0 0.7 collective-permute-start
  58.7 0.8 collective-permute-done.2.across_ref
  59.4 3.0 %collective-permute-done.1.far_ref = f32[32,128]{1,0:T(8,128)S(1)} collective-permute-done((f32[32,128]{1,0:T(8,128)S(1)}, f32[32,128]{1,0:T(8,128)S(1)}, u32[]{:S(2)}, u32[]{:S(2)}) %collective-permute-start.1) | collective-permute-done | bytes 16416 | tf_op jit(solution)/shard_map/ppermute | solution.py:489
  62.4 0.0 collective-permute-done.near_ref
  62.4 0.7 shares.1.values_hbm
  63.1 5.2 %all-to-all-done.1.got_ref.after_hbm = bf16[32,96,128]{2,1,0:T(8,128)(2,1)S(1)} async-done(((bf16[32,96,128]{2,1,0:T(8,128)(2,1)}), bf16[32,96,128]{2,1,0:T(8,128)(2,1)S(1)}, u32[]{:S(2)}, u32[]{:S(2)}) %all-to-all-start.1) | async-done | bytes 786464 | tf_op jit(solution)/shard_map/all_to_all | solution.py:472
  68.3 4.1 %all-to-all-start.3 = ((bf16[32,32,128]{2,1,0:T(8,128)(2,1)}), bf16[32,32,128]{2,1,0:T(8,128)(2,1)S(1)}, u32[]{:S(2)}, u32[]{:S(2)}) async-start(bf16[32,32,128]{2,1,0:T(8,128)(2,1)} %tied.1), calls=%async_computation.3 | async-start | bytes 524288 | tf_op jit(solution)/shard_map/all_to_all | solution.py:472
  72.4 0.0 copy-done
  72.5 0.0 copy-done.3
  72.5 6.0 %back.1 = bf16[2048,256]{1,0:T(8,128)(2,1)} custom-call(bf16[32,96,128]{2,1,0:T(8,128)(2,1)S(1)} %all-to-all-done.1.got_ref.after_hbm, bf16[2048,256]{1,0:T(8,128)(2,1)S(1)} %copy-done, bf16[256,256]{1,0:T(8,128)(2,1)S(1)} %copy-done.1, s32[1,32]{1,0:T(1,128)S(1)} %copy-done.3, bf16[2048,1536]{1,0:T(8,128)(2,1)} %adjacency.1.adj_hbm), custom_call_target="tpu_custom_call" | custom-call | flops 1000000000 | bytes 8257664 | tf_op jit(solution)/shard_map/back/pallas_call | solution.py:318
  78.5 2.9 %all-to-all-done.3.sum_ref = bf16[32,32,128]{2,1,0:T(8,128)(2,1)S(1)} async-done(((bf16[32,32,128]{2,1,0:T(8,128)(2,1)}), bf16[32,32,128]{2,1,0:T(8,128)(2,1)S(1)}, u32[]{:S(2)}, u32[]{:S(2)}) %all-to-all-start.3) | async-done | bytes 262176 | tf_op jit(solution)/shard_map/all_to_all | solution.py:472
  81.5 1.1 %update.1 = (f32[256,256]{1,0:T(8,128)}, f32[256,256]{1,0:T(8,128)}) custom-call(bf16[32,32,128]{2,1,0:T(8,128)(2,1)S(1)} %all-to-all-done.3.sum_ref, bf16[256,256]{1,0:T(8,128)(2,1)S(1)} %copy-done.1, bf16[256,256]{1,0:T(8,128)(2,1)S(1)} %copy-done.2), custom_call_target="tpu_custom_call" | custom-call | flops 1000000000 | bytes 524288 | tf_op jit(solution)/shard_map/update/pallas_call | solution.py:318
  (1 shorter events, 0.0 us)
Async XLA Ops:
  7.5 23.7 %all-to-all-start = ((bf16[32,104,128]{2,1,0:T(8,128)(2,1)}), bf16[32,104,128]{2,1,0:T(8,128)(2,1)S(1)}, u32[]{:S(2)}, u32[]{:S(2)}) async-start(bf16[32,104,128]{2,1,0:T(8,128)(2,1)} %scatter.1), calls=%async_computation | async-start | bytes 1703936 | tf_op jit(solution)/shard_map/all_to_all | solution.py:472
  16.1 15.1 %copy-start.1 = (bf16[256,256]{1,0:T(8,128)(2,1)S(1)}, bf16[256,256]{1,0:T(8,128)(2,1)}, u32[]{:S(2)}) copy-start(bf16[256,256]{1,0:T(8,128)(2,1)} %ws_ref.5) | copy-start | bytes 393220
  16.2 15.0 %copy-start.2 = (bf16[256,256]{1,0:T(8,128)(2,1)S(1)}, bf16[256,256]{1,0:T(8,128)(2,1)}, u32[]{:S(2)}) copy-start(bf16[256,256]{1,0:T(8,128)(2,1)} %wn_ref.5) | copy-start | bytes 393220
  16.2 15.0 %copy-start.4 = (s32[16]{0:T(128)S(1)}, s32[16]{0:T(128)}, u32[]{:S(2)}) copy-start(s32[16]{0:T(128)} %ages_hbm.1) | copy-start | bytes 196
  36.8 35.7 %copy-start = (bf16[2048,256]{1,0:T(8,128)(2,1)S(1)}, bf16[2048,256]{1,0:T(8,128)(2,1)}, u32[]{:S(2)}) copy-start(bf16[2048,256]{1,0:T(8,128)(2,1)} %get-tuple-element.11.gp_hbm.gp_ref) | copy-start | bytes 3145732
  36.8 35.7 %copy-start.3 = (s32[1,32]{1,0:T(1,128)S(1)}, s32[1,32]{1,0:T(1,128)}, u32[]{:S(2)}) copy-start(s32[1,32]{1,0:T(1,128)} %counts_hbm.3) | copy-start | bytes 388
  36.8 13.1 %all-to-all-start.2 = ((bf16[32,32,128]{2,1,0:T(8,128)(2,1)}), bf16[32,32,128]{2,1,0:T(8,128)(2,1)S(1)}, u32[]{:S(2)}, u32[]{:S(2)}) async-start(bf16[32,32,128]{2,1,0:T(8,128)(2,1)} %get-tuple-element.13), calls=%async_computation.2 | async-start | bytes 524288 | tf_op jit(solution)/shard_map/all_to_all | solution.py:472
  49.9 18.5 %all-to-all-start.1 = ((bf16[32,96,128]{2,1,0:T(8,128)(2,1)}), bf16[32,96,128]{2,1,0:T(8,128)(2,1)S(1)}, u32[]{:S(2)}, u32[]{:S(2)}) async-start(bf16[32,96,128]{2,1,0:T(8,128)(2,1)} %outgoing.1.after_hbm), calls=%async_computation.1 | async-start | bytes 1572864 | tf_op jit(solution)/shard_map/all_to_all | solution.py:472
  54.2 5.3 %collective-permute-start.2 = (f32[32,128]{1,0:T(8,128)S(1)}, f32[32,128]{1,0:T(8,128)S(1)}, u32[]{:S(2)}, u32[]{:S(2)}) collective-permute-start(f32[32,128]{1,0:T(8,128)S(1)} %summed.1.own_ref), channel_id=1, source_target_pairs={{0,96},{32,64},{64,32},{96,0},{1,97},{33,65},{65,33},{97,1},{2,98}... | collective-permute-start | bytes 49160 | tf_op jit(solution)/shard_map/ppermute | solution.py:489
  58.0 4.4 %collective-permute-start.1 = (f32[32,128]{1,0:T(8,128)S(1)}, f32[32,128]{1,0:T(8,128)S(1)}, u32[]{:S(2)}, u32[]{:S(2)}) collective-permute-start(f32[32,128]{1,0:T(8,128)S(1)} %summed.1.own_ref), channel_id=1, source_target_pairs={{0,64},{32,96},{64,0},{96,32},{1,65},{33,97},{65,1},{97,33},{2,66}... | collective-permute-start | bytes 49160 | tf_op jit(solution)/shard_map/ppermute | solution.py:489
  58.0 4.4 %collective-permute-start = (f32[32,128]{1,0:T(8,128)S(1)}, f32[32,128]{1,0:T(8,128)S(1)}, u32[]{:S(2)}, u32[]{:S(2)}) collective-permute-start(f32[32,128]{1,0:T(8,128)S(1)} %summed.1.own_ref), channel_id=1, source_target_pairs={{0,32},{32,0},{64,96},{96,64},{1,33},{33,1},{65,97},{97,65},{2,34}... | collective-permute-start | bytes 49160 | tf_op jit(solution)/shard_map/ppermute | solution.py:489
  68.3 13.1 %all-to-all-start.3 = ((bf16[32,32,128]{2,1,0:T(8,128)(2,1)}), bf16[32,32,128]{2,1,0:T(8,128)(2,1)S(1)}, u32[]{:S(2)}, u32[]{:S(2)}) async-start(bf16[32,32,128]{2,1,0:T(8,128)(2,1)} %tied.1), calls=%async_computation.3 | async-start | bytes 524288 | tf_op jit(solution)/shard_map/all_to_all | solution.py:472

commit v8 on v7

--- a/solution.py
+++ b/solution.py
@@ -13,7 +13,7 @@
 TILE = 128
 ROWS = 512
 FINE = 256
-INDEX_ROWS = 8
+INDEX_ROWS = 16
 GATHER_STEPS = 4
 NN = (((1,), (0,)), ((), ()))
 NT = (((1,), (1,)), ((), ()))
@@ -128,7 +128,7 @@
 
 def index_digits(cap, got_ref):
     peers = got_ref.shape[0]
-    coded = got_ref[:, 2 * cap :, :].astype(F32).reshape(peers * INDEX_ROWS, TILE).astype(BF)
+    coded = got_ref[:, 2 * cap :, :].reshape(peers * INDEX_ROWS, TILE)
     pick_row = lax.broadcasted_iota(jnp.int32, (peers, peers * INDEX_ROWS), 1)
     pick_peer = lax.broadcasted_iota(jnp.int32, (peers, peers * INDEX_ROWS), 0) * INDEX_ROWS
     high = dot(mask(pick_row == pick_peer), coded, NN).astype(BF)

time: 83.1 us -> 83.8 us (level)
  no operation moved by 1% of the time
where the time goes in v8:
time: 83.8 us; the launch traced here: 83.3 us
  Pallas kernels  31.6 us (38%)
  starting transfers between devices  25.5 us (30%)
  waiting for transfers between devices  25.4 us (30%)
    pallas_call x8, Pallas kernels, call(): pl.pallas_call(kernel, name=name, in_specs=[VMEM if k < near else HBM for...  31.6 us
    all_to_all x4, waiting for transfers between devices, exchange(): return lax.all_to_all(x, 'dom', split_axis=0, concat_axis=0, tiled=True)  21.7 us
    all_to_all x4, starting transfers between devices, exchange(): return lax.all_to_all(x, 'dom', split_axis=0, concat_axis=0, tiled=True)  21 us
    ppermute x3, starting transfers between devices, body(): lax.ppermute(own, 'group', [(k, k ^ other) for k in groups])  4.5 us
    ppermute x3, waiting for transfers between devices, body(): lax.ppermute(own, 'group', [(k, k ^ other) for k in groups])  3.72 us
  transfers between devices with their start and end apart: 7, of which 6 were waited for; matrix products, arithmetic and copies ran while one was open for 0% of the time, Pallas kernels for 22%

profile of v8, /device:TPU:1, one launch (start us, length us, event | category | flops | bytes accessed | tf_op | source)
XLA Modules:
  0.0 83.3 jit_solution(5714922262826214717)
XLA Ops:
  0.6 6.9 %scatter.1 = bf16[32,112,128]{2,1,0:T(8,128)(2,1)} custom-call(s32[1,32]{1,0:T(1,128)} %counts_hbm.3, s32[1,32,48]{2,1,0:T(8,128)} %rows_hbm.1, s32[1,8192]{1,0:T(1,128)} %src_hbm.3, s32[1,8192]{1,0:T(1,128)} %slot_hbm.3, bf16[2048,256]{1,0:T(8,128)(2,1)} %feats_hbm.3), custom_call_target="tpu_custom_call" | custom-call | flops 1000000000 | bytes 1120384 | tf_op jit(solution)/shard_map/scatter/pallas_call | solution.py:318
  7.5 8.6 %all-to-all-start = ((bf16[32,112,128]{2,1,0:T(8,128)(2,1)}), bf16[32,112,128]{2,1,0:T(8,128)(2,1)S(1)}, u32[]{:S(2)}, u32[]{:S(2)}) async-start(bf16[32,112,128]{2,1,0:T(8,128)(2,1)} %scatter.1), calls=%async_computation | async-start | bytes 1835008 | tf_op jit(solution)/shard_map/all_to_all | solution.py:472
  16.1 0.0 copy-start.1
  16.1 0.0 copy-start.2
  16.2 0.0 copy-start.3
  16.2 5.5 %adjacency.1.adj_hbm = bf16[2048,1536]{1,0:T(8,128)(2,1)} custom-call(s32[1,8192]{1,0:T(1,128)} %src_hbm.3, s32[1,8192]{1,0:T(1,128)} %slot_hbm.3), custom_call_target="tpu_custom_call" | custom-call | flops 6000000000 | bytes 65536 | tf_op jit(solution)/shard_map/adjacency/pallas_call | solution.py:318
  21.6 10.3 %all-to-all-done.got_ref = bf16[32,112,128]{2,1,0:T(8,128)(2,1)S(1)} async-done(((bf16[32,112,128]{2,1,0:T(8,128)(2,1)}), bf16[32,112,128]{2,1,0:T(8,128)(2,1)S(1)}, u32[]{:S(2)}, u32[]{:S(2)}) %all-to-all-start) | async-done | bytes 917536 | tf_op jit(solution)/shard_map/all_to_all | solution.py:472
  31.9 0.0 copy-done.1
  31.9 0.0 copy-done.2
  31.9 0.0 copy-done.3
  31.9 5.6 %masters.1 = (bf16[2048,256]{1,0:T(8,128)(2,1)}, bf16[2048,256]{1,0:T(8,128)(2,1)}, f32[2048,256]{1,0:T(8,128)}, bf16[32,32,128]{2,1,0:T(8,128)(2,1)}) custom-call(bf16[32,112,128]{2,1,0:T(8,128)(2,1)S(1)} %all-to-all-done.got_ref, bf16[256,256]{1,0:T(8,128)(2,1)S(1)} %copy-done.1, bf16[256,256]{1,0:T(8,128)(2,1)S(1)} %copy-done.2, ...), custom_call_target="tpu_custom_call" | custom-call | flops 1000000000 | bytes 10616896 | tf_op jit(solution)/shard_map/masters/pallas_call | solution.py:318
  37.5 0.0 copy-start
  37.5 0.0 copy-start.4
  37.5 4.1 %all-to-all-start.2 = ((bf16[32,32,128]{2,1,0:T(8,128)(2,1)}), bf16[32,32,128]{2,1,0:T(8,128)(2,1)S(1)}, u32[]{:S(2)}, u32[]{:S(2)}) async-start(bf16[32,32,128]{2,1,0:T(8,128)(2,1)} %get-tuple-element.13), calls=%async_computation.2 | async-start | bytes 524288 | tf_op jit(solution)/shard_map/all_to_all | solution.py:472
  41.6 5.7 %outgoing.1.after_hbm = bf16[32,96,128]{2,1,0:T(8,128)(2,1)} custom-call(bf16[32,112,128]{2,1,0:T(8,128)(2,1)S(1)} %all-to-all-done.got_ref, bf16[256,256]{1,0:T(8,128)(2,1)S(1)} %copy-done.2, bf16[2048,256]{1,0:T(8,128)(2,1)} %get-tuple-element.11.gp_hbm.gp_ref, f32[2048,256]{1,0:T(8,128)} %get-tuple-element.12.agg_hbm), custom_call_target="tpu_custom_call" | custom-call | flops 1000000000 | bytes 4194304 | tf_op jit(solution)/shard_map/outgoing/pallas_call | solution.py:318
  47.3 3.3 %all-to-all-done.2.parts_ref = bf16[32,32,128]{2,1,0:T(8,128)(2,1)S(1)} async-done(((bf16[32,32,128]{2,1,0:T(8,128)(2,1)}), bf16[32,32,128]{2,1,0:T(8,128)(2,1)S(1)}, u32[]{:S(2)}, u32[]{:S(2)}) %all-to-all-start.2) | async-done | bytes 262176 | tf_op jit(solution)/shard_map/all_to_all | solution.py:472
  50.6 4.3 %all-to-all-start.1 = ((bf16[32,96,128]{2,1,0:T(8,128)(2,1)}), bf16[32,96,128]{2,1,0:T(8,128)(2,1)S(1)}, u32[]{:S(2)}, u32[]{:S(2)}) async-start(bf16[32,96,128]{2,1,0:T(8,128)(2,1)} %outgoing.1.after_hbm), calls=%async_computation.1 | async-start | bytes 1572864 | tf_op jit(solution)/shard_map/all_to_all | solution.py:472
  54.9 0.1 summed.1.own_ref
  54.9 3.8 %collective-permute-start.2 = (f32[32,128]{1,0:T(8,128)S(1)}, f32[32,128]{1,0:T(8,128)S(1)}, u32[]{:S(2)}, u32[]{:S(2)}) collective-permute-start(f32[32,128]{1,0:T(8,128)S(1)} %summed.1.own_ref), channel_id=1, source_target_pairs={{0,96},{32,64},{64,32},{96,0},{1,97},{33,65},{65,33},{97,1},{2,98}... | collective-permute-start | bytes 49160 | tf_op jit(solution)/shard_map/ppermute | solution.py:489
  58.8 0.0 collective-permute-start.1
  58.8 0.7 collective-permute-start
  59.4 0.8 collective-permute-done.2.across_ref
  60.2 3.0 %collective-permute-done.1.far_ref = f32[32,128]{1,0:T(8,128)S(1)} collective-permute-done((f32[32,128]{1,0:T(8,128)S(1)}, f32[32,128]{1,0:T(8,128)S(1)}, u32[]{:S(2)}, u32[]{:S(2)}) %collective-permute-start.1) | collective-permute-done | bytes 16416 | tf_op jit(solution)/shard_map/ppermute | solution.py:489
  63.1 0.0 collective-permute-done.near_ref
  63.1 0.7 shares.1.values_hbm
  63.9 5.2 %all-to-all-done.1.got_ref.after_hbm = bf16[32,96,128]{2,1,0:T(8,128)(2,1)S(1)} async-done(((bf16[32,96,128]{2,1,0:T(8,128)(2,1)}), bf16[32,96,128]{2,1,0:T(8,128)(2,1)S(1)}, u32[]{:S(2)}, u32[]{:S(2)}) %all-to-all-start.1) | async-done | bytes 786464 | tf_op jit(solution)/shard_map/all_to_all | solution.py:472
  69.1 4.1 %all-to-all-start.3 = ((bf16[32,32,128]{2,1,0:T(8,128)(2,1)}), bf16[32,32,128]{2,1,0:T(8,128)(2,1)S(1)}, u32[]{:S(2)}, u32[]{:S(2)}) async-start(bf16[32,32,128]{2,1,0:T(8,128)(2,1)} %tied.1), calls=%async_computation.3 | async-start | bytes 524288 | tf_op jit(solution)/shard_map/all_to_all | solution.py:472
  73.2 0.0 copy-done
  73.2 0.0 copy-done.4
  73.2 6.0 %back.1 = bf16[2048,256]{1,0:T(8,128)(2,1)} custom-call(bf16[32,96,128]{2,1,0:T(8,128)(2,1)S(1)} %all-to-all-done.1.got_ref.after_hbm, bf16[2048,256]{1,0:T(8,128)(2,1)S(1)} %copy-done, bf16[256,256]{1,0:T(8,128)(2,1)S(1)} %copy-done.1, s32[1,32]{1,0:T(1,128)S(1)} %copy-done.4, bf16[2048,1536]{1,0:T(8,128)(2,1)} %adjacency.1.adj_hbm), custom_call_target="tpu_custom_call" | custom-call | flops 1000000000 | bytes 8257664 | tf_op jit(solution)/shard_map/back/pallas_call | solution.py:318
  79.3 2.9 %all-to-all-done.3.sum_ref = bf16[32,32,128]{2,1,0:T(8,128)(2,1)S(1)} async-done(((bf16[32,32,128]{2,1,0:T(8,128)(2,1)}), bf16[32,32,128]{2,1,0:T(8,128)(2,1)S(1)}, u32[]{:S(2)}, u32[]{:S(2)}) %all-to-all-start.3) | async-done | bytes 262176 | tf_op jit(solution)/shard_map/all_to_all | solution.py:472
  82.2 1.1 %update.1 = (f32[256,256]{1,0:T(8,128)}, f32[256,256]{1,0:T(8,128)}) custom-call(bf16[32,32,128]{2,1,0:T(8,128)(2,1)S(1)} %all-to-all-done.3.sum_ref, bf16[256,256]{1,0:T(8,128)(2,1)S(1)} %copy-done.1, bf16[256,256]{1,0:T(8,128)(2,1)S(1)} %copy-done.2), custom_call_target="tpu_custom_call" | custom-call | flops 1000000000 | bytes 524288 | tf_op jit(solution)/shard_map/update/pallas_call | solution.py:318
  (1 shorter events, 0.0 us)
Async XLA Ops:
  7.5 24.4 %all-to-all-start = ((bf16[32,112,128]{2,1,0:T(8,128)(2,1)}), bf16[32,112,128]{2,1,0:T(8,128)(2,1)S(1)}, u32[]{:S(2)}, u32[]{:S(2)}) async-start(bf16[32,112,128]{2,1,0:T(8,128)(2,1)} %scatter.1), calls=%async_computation | async-start | bytes 1835008 | tf_op jit(solution)/shard_map/all_to_all | solution.py:472
  16.1 15.8 %copy-start.1 = (bf16[256,256]{1,0:T(8,128)(2,1)S(1)}, bf16[256,256]{1,0:T(8,128)(2,1)}, u32[]{:S(2)}) copy-start(bf16[256,256]{1,0:T(8,128)(2,1)} %ws_ref.5) | copy-start | bytes 393220
  16.1 15.7 %copy-start.2 = (bf16[256,256]{1,0:T(8,128)(2,1)S(1)}, bf16[256,256]{1,0:T(8,128)(2,1)}, u32[]{:S(2)}) copy-start(bf16[256,256]{1,0:T(8,128)(2,1)} %wn_ref.5) | copy-start | bytes 393220
  16.2 15.7 %copy-start.3 = (s32[16]{0:T(128)S(1)}, s32[16]{0:T(128)}, u32[]{:S(2)}) copy-start(s32[16]{0:T(128)} %ages_hbm.1) | copy-start | bytes 196
  37.5 35.7 %copy-start = (bf16[2048,256]{1,0:T(8,128)(2,1)S(1)}, bf16[2048,256]{1,0:T(8,128)(2,1)}, u32[]{:S(2)}) copy-start(bf16[2048,256]{1,0:T(8,128)(2,1)} %get-tuple-element.11.gp_hbm.gp_ref) | copy-start | bytes 3145732
  37.5 35.7 %copy-start.4 = (s32[1,32]{1,0:T(1,128)S(1)}, s32[1,32]{1,0:T(1,128)}, u32[]{:S(2)}) copy-start(s32[1,32]{1,0:T(1,128)} %counts_hbm.3) | copy-start | bytes 388
  37.5 13.1 %all-to-all-start.2 = ((bf16[32,32,128]{2,1,0:T(8,128)(2,1)}), bf16[32,32,128]{2,1,0:T(8,128)(2,1)S(1)}, u32[]{:S(2)}, u32[]{:S(2)}) async-start(bf16[32,32,128]{2,1,0:T(8,128)(2,1)} %get-tuple-element.13), calls=%async_computation.2 | async-start | bytes 524288 | tf_op jit(solution)/shard_map/all_to_all | solution.py:472
  50.6 18.5 %all-to-all-start.1 = ((bf16[32,96,128]{2,1,0:T(8,128)(2,1)}), bf16[32,96,128]{2,1,0:T(8,128)(2,1)S(1)}, u32[]{:S(2)}, u32[]{:S(2)}) async-start(bf16[32,96,128]{2,1,0:T(8,128)(2,1)} %outgoing.1.after_hbm), calls=%async_computation.1 | async-start | bytes 1572864 | tf_op jit(solution)/shard_map/all_to_all | solution.py:472
  54.9 5.3 %collective-permute-start.2 = (f32[32,128]{1,0:T(8,128)S(1)}, f32[32,128]{1,0:T(8,128)S(1)}, u32[]{:S(2)}, u32[]{:S(2)}) collective-permute-start(f32[32,128]{1,0:T(8,128)S(1)} %summed.1.own_ref), channel_id=1, source_target_pairs={{0,96},{32,64},{64,32},{96,0},{1,97},{33,65},{65,33},{97,1},{2,98}... | collective-permute-start | bytes 49160 | tf_op jit(solution)/shard_map/ppermute | solution.py:489
  58.8 4.4 %collective-permute-start.1 = (f32[32,128]{1,0:T(8,128)S(1)}, f32[32,128]{1,0:T(8,128)S(1)}, u32[]{:S(2)}, u32[]{:S(2)}) collective-permute-start(f32[32,128]{1,0:T(8,128)S(1)} %summed.1.own_ref), channel_id=1, source_target_pairs={{0,64},{32,96},{64,0},{96,32},{1,65},{33,97},{65,1},{97,33},{2,66}... | collective-permute-start | bytes 49160 | tf_op jit(solution)/shard_map/ppermute | solution.py:489
  58.8 4.4 %collective-permute-start = (f32[32,128]{1,0:T(8,128)S(1)}, f32[32,128]{1,0:T(8,128)S(1)}, u32[]{:S(2)}, u32[]{:S(2)}) collective-permute-start(f32[32,128]{1,0:T(8,128)S(1)} %summed.1.own_ref), channel_id=1, source_target_pairs={{0,32},{32,0},{64,96},{96,64},{1,33},{33,1},{65,97},{97,65},{2,34}... | collective-permute-start | bytes 49160 | tf_op jit(solution)/shard_map/ppermute | solution.py:489
  69.1 13.1 %all-to-all-start.3 = ((bf16[32,32,128]{2,1,0:T(8,128)(2,1)}), bf16[32,32,128]{2,1,0:T(8,128)(2,1)S(1)}, u32[]{:S(2)}, u32[]{:S(2)}) async-start(bf16[32,32,128]{2,1,0:T(8,128)(2,1)} %tied.1), calls=%async_computation.3 | async-start | bytes 524288 | tf_op jit(solution)/shard_map/all_to_all | solution.py:472

commit v9 on v8

--- a/solution.py
+++ b/solution.py
@@ -149,7 +149,7 @@
     hidden_hbm,
     gp_hbm,
     agg_hbm,
-    share_ref,
+    share_hbm,
     arr_ref,
     ages_ref,
     feats_ref,
@@ -158,6 +158,7 @@
     hidden_ref,
     gp_ref,
     agg_ref,
+    share_ref,
     sems,
     out_sems,
 ):
@@ -217,6 +218,9 @@
     share = 2 * width // peers
     share_ref[:, :share, :] = total[:, :TILE].reshape(peers, share, TILE)
     share_ref[:, share:, :] = total[:, TILE:].reshape(peers, share, TILE)
+    copy = pltpu.make_async_copy(share_ref, share_hbm, out_sems.at[len(outs)])
+    copy.start()
+    outs.append(copy)
     for copy in outs:
         copy.wait()
 
@@ -392,7 +396,7 @@
             shape((verts, width), F32),
             shape((peers, 2 * share, TILE)),
         ],
-        (3,),
+        (),
         [
             pltpu.VMEM((peers * cap, width), BF),
             pltpu.SMEM(ages.shape, jnp.int32),
@@ -402,8 +406,9 @@
             like(feats),
             like(feats),
             pltpu.VMEM((verts, width), F32),
+            pltpu.VMEM((peers, 2 * share, TILE), BF),
             pltpu.SemaphoreType.DMA((4,)),
-            pltpu.SemaphoreType.DMA((3 * (verts // FINE),)),
+            pltpu.SemaphoreType.DMA((3 * (verts // FINE) + 1,)),
         ],
         limit=52,
     )

time: 83.8 us -> 83.3 us (level)
  no operation moved by 1% of the time
where the time goes in v9:
time: 83.3 us; the launch traced here: 82.8 us
  Pallas kernels  31.1 us (37%)
  starting transfers between devices  25.5 us (31%)
  waiting for transfers between devices  25.4 us (30%)
    pallas_call x8, Pallas kernels, call(): pl.pallas_call(kernel, name=name, in_specs=[VMEM if k < near else HBM for...  31.1 us
    all_to_all x4, waiting for transfers between devices, exchange(): return lax.all_to_all(x, 'dom', split_axis=0, concat_axis=0, tiled=True)  21.7 us
    all_to_all x4, starting transfers between devices, exchange(): return lax.all_to_all(x, 'dom', split_axis=0, concat_axis=0, tiled=True)  21 us
    ppermute x3, starting transfers between devices, body(): lax.ppermute(own, 'group', [(k, k ^ other) for k in groups])  4.5 us
    ppermute x3, waiting for transfers between devices, body(): lax.ppermute(own, 'group', [(k, k ^ other) for k in groups])  3.72 us
  transfers between devices with their start and end apart: 7, of which 6 were waited for; matrix products, arithmetic and copies ran while one was open for 0% of the time, Pallas kernels for 22%

profile of v9, /device:TPU:1, one launch (start us, length us, event | category | flops | bytes accessed | tf_op | source)
XLA Modules:
  0.0 82.8 jit_solution(12510248789086205284)
XLA Ops:
  0.6 6.9 %scatter.1 = bf16[32,112,128]{2,1,0:T(8,128)(2,1)} custom-call(s32[1,32]{1,0:T(1,128)} %counts_hbm.3, s32[1,32,48]{2,1,0:T(8,128)} %rows_hbm.1, s32[1,8192]{1,0:T(1,128)} %src_hbm.3, s32[1,8192]{1,0:T(1,128)} %slot_hbm.3, bf16[2048,256]{1,0:T(8,128)(2,1)} %feats_hbm.3), custom_call_target="tpu_custom_call" | custom-call | flops 1000000000 | bytes 1120384 | tf_op jit(solution)/shard_map/scatter/pallas_call | solution.py:322
  7.5 8.6 %all-to-all-start = ((bf16[32,112,128]{2,1,0:T(8,128)(2,1)}), bf16[32,112,128]{2,1,0:T(8,128)(2,1)S(1)}, u32[]{:S(2)}, u32[]{:S(2)}) async-start(bf16[32,112,128]{2,1,0:T(8,128)(2,1)} %scatter.1), calls=%async_computation | async-start | bytes 1835008 | tf_op jit(solution)/shard_map/all_to_all | solution.py:477
  16.1 0.0 copy-start.1
  16.1 0.0 copy-start.2
  16.2 0.0 copy-start.3
  16.2 5.5 %adjacency.1.adj_hbm = bf16[2048,1536]{1,0:T(8,128)(2,1)} custom-call(s32[1,8192]{1,0:T(1,128)} %src_hbm.3, s32[1,8192]{1,0:T(1,128)} %slot_hbm.3), custom_call_target="tpu_custom_call" | custom-call | flops 6000000000 | bytes 65536 | tf_op jit(solution)/shard_map/adjacency/pallas_call | solution.py:322
  21.6 10.3 %all-to-all-done.got_ref = bf16[32,112,128]{2,1,0:T(8,128)(2,1)S(1)} async-done(((bf16[32,112,128]{2,1,0:T(8,128)(2,1)}), bf16[32,112,128]{2,1,0:T(8,128)(2,1)S(1)}, u32[]{:S(2)}, u32[]{:S(2)}) %all-to-all-start) | async-done | bytes 917536 | tf_op jit(solution)/shard_map/all_to_all | solution.py:477
  31.9 0.0 copy-done.1
  31.9 0.0 copy-done.2
  31.9 0.0 copy-done.3
  31.9 5.1 %masters.1 = (bf16[2048,256]{1,0:T(8,128)(2,1)}, bf16[2048,256]{1,0:T(8,128)(2,1)}, f32[2048,256]{1,0:T(8,128)}, bf16[32,32,128]{2,1,0:T(8,128)(2,1)}) custom-call(bf16[32,112,128]{2,1,0:T(8,128)(2,1)S(1)} %all-to-all-done.got_ref, bf16[256,256]{1,0:T(8,128)(2,1)S(1)} %copy-done.1, bf16[256,256]{1,0:T(8,128)(2,1)S(1)} %copy-done.2, ...), custom_call_target="tpu_custom_call" | custom-call | flops 1000000000 | bytes 10616896 | tf_op jit(solution)/shard_map/masters/pallas_call | solution.py:322
  37.0 0.0 copy-start
  37.0 0.0 copy-start.4
  37.0 4.1 %all-to-all-start.2 = ((bf16[32,32,128]{2,1,0:T(8,128)(2,1)}), bf16[32,32,128]{2,1,0:T(8,128)(2,1)S(1)}, u32[]{:S(2)}, u32[]{:S(2)}) async-start(bf16[32,32,128]{2,1,0:T(8,128)(2,1)} %get-tuple-element.13), calls=%async_computation.2 | async-start | bytes 524288 | tf_op jit(solution)/shard_map/all_to_all | solution.py:477
  41.1 5.7 %outgoing.1.after_hbm = bf16[32,96,128]{2,1,0:T(8,128)(2,1)} custom-call(bf16[32,112,128]{2,1,0:T(8,128)(2,1)S(1)} %all-to-all-done.got_ref, bf16[256,256]{1,0:T(8,128)(2,1)S(1)} %copy-done.2, bf16[2048,256]{1,0:T(8,128)(2,1)} %get-tuple-element.11.gp_hbm.gp_ref, f32[2048,256]{1,0:T(8,128)} %get-tuple-element.12.agg_hbm), custom_call_target="tpu_custom_call" | custom-call | flops 1000000000 | bytes 4194304 | tf_op jit(solution)/shard_map/outgoing/pallas_call | solution.py:322
  46.9 3.3 %all-to-all-done.2.parts_ref = bf16[32,32,128]{2,1,0:T(8,128)(2,1)S(1)} async-done(((bf16[32,32,128]{2,1,0:T(8,128)(2,1)}), bf16[32,32,128]{2,1,0:T(8,128)(2,1)S(1)}, u32[]{:S(2)}, u32[]{:S(2)}) %all-to-all-start.2) | async-done | bytes 262176 | tf_op jit(solution)/shard_map/all_to_all | solution.py:477
  50.1 4.3 %all-to-all-start.1 = ((bf16[32,96,128]{2,1,0:T(8,128)(2,1)}), bf16[32,96,128]{2,1,0:T(8,128)(2,1)S(1)}, u32[]{:S(2)}, u32[]{:S(2)}) async-start(bf16[32,96,128]{2,1,0:T(8,128)(2,1)} %outgoing.1.after_hbm), calls=%async_computation.1 | async-start | bytes 1572864 | tf_op jit(solution)/shard_map/all_to_all | solution.py:477
  54.4 0.1 summed.1.own_ref
  54.4 3.8 %collective-permute-start.2 = (f32[32,128]{1,0:T(8,128)S(1)}, f32[32,128]{1,0:T(8,128)S(1)}, u32[]{:S(2)}, u32[]{:S(2)}) collective-permute-start(f32[32,128]{1,0:T(8,128)S(1)} %summed.1.own_ref), channel_id=1, source_target_pairs={{0,96},{32,64},{64,32},{96,0},{1,97},{33,65},{65,33},{97,1},{2,98}... | collective-permute-start | bytes 49160 | tf_op jit(solution)/shard_map/ppermute | solution.py:494
  58.3 0.0 collective-permute-start.1
  58.3 0.7 collective-permute-start
  59.0 0.8 collective-permute-done.2.across_ref
  59.7 3.0 %collective-permute-done.1.far_ref = f32[32,128]{1,0:T(8,128)S(1)} collective-permute-done((f32[32,128]{1,0:T(8,128)S(1)}, f32[32,128]{1,0:T(8,128)S(1)}, u32[]{:S(2)}, u32[]{:S(2)}) %collective-permute-start.1) | collective-permute-done | bytes 16416 | tf_op jit(solution)/shard_map/ppermute | solution.py:494
  62.7 0.0 collective-permute-done.near_ref
  62.7 0.7 shares.1.values_hbm
  63.4 5.2 %all-to-all-done.1.got_ref.after_hbm = bf16[32,96,128]{2,1,0:T(8,128)(2,1)S(1)} async-done(((bf16[32,96,128]{2,1,0:T(8,128)(2,1)}), bf16[32,96,128]{2,1,0:T(8,128)(2,1)S(1)}, u32[]{:S(2)}, u32[]{:S(2)}) %all-to-all-start.1) | async-done | bytes 786464 | tf_op jit(solution)/shard_map/all_to_all | solution.py:477
  68.6 4.1 %all-to-all-start.3 = ((bf16[32,32,128]{2,1,0:T(8,128)(2,1)}), bf16[32,32,128]{2,1,0:T(8,128)(2,1)S(1)}, u32[]{:S(2)}, u32[]{:S(2)}) async-start(bf16[32,32,128]{2,1,0:T(8,128)(2,1)} %tied.1), calls=%async_computation.3 | async-start | bytes 524288 | tf_op jit(solution)/shard_map/all_to_all | solution.py:477
  72.7 0.0 copy-done
  72.7 0.0 copy-done.4
  72.7 6.0 %back.1 = bf16[2048,256]{1,0:T(8,128)(2,1)} custom-call(bf16[32,96,128]{2,1,0:T(8,128)(2,1)S(1)} %all-to-all-done.1.got_ref.after_hbm, bf16[2048,256]{1,0:T(8,128)(2,1)S(1)} %copy-done, bf16[256,256]{1,0:T(8,128)(2,1)S(1)} %copy-done.1, s32[1,32]{1,0:T(1,128)S(1)} %copy-done.4, bf16[2048,1536]{1,0:T(8,128)(2,1)} %adjacency.1.adj_hbm), custom_call_target="tpu_custom_call" | custom-call | flops 1000000000 | bytes 8257664 | tf_op jit(solution)/shard_map/back/pallas_call | solution.py:322
  78.8 2.9 %all-to-all-done.3.sum_ref = bf16[32,32,128]{2,1,0:T(8,128)(2,1)S(1)} async-done(((bf16[32,32,128]{2,1,0:T(8,128)(2,1)}), bf16[32,32,128]{2,1,0:T(8,128)(2,1)S(1)}, u32[]{:S(2)}, u32[]{:S(2)}) %all-to-all-start.3) | async-done | bytes 262176 | tf_op jit(solution)/shard_map/all_to_all | solution.py:477
  81.7 1.1 %update.1 = (f32[256,256]{1,0:T(8,128)}, f32[256,256]{1,0:T(8,128)}) custom-call(bf16[32,32,128]{2,1,0:T(8,128)(2,1)S(1)} %all-to-all-done.3.sum_ref, bf16[256,256]{1,0:T(8,128)(2,1)S(1)} %copy-done.1, bf16[256,256]{1,0:T(8,128)(2,1)S(1)} %copy-done.2), custom_call_target="tpu_custom_call" | custom-call | flops 1000000000 | bytes 524288 | tf_op jit(solution)/shard_map/update/pallas_call | solution.py:322
  (1 shorter events, 0.0 us)
Async XLA Ops:
  7.5 24.4 %all-to-all-start = ((bf16[32,112,128]{2,1,0:T(8,128)(2,1)}), bf16[32,112,128]{2,1,0:T(8,128)(2,1)S(1)}, u32[]{:S(2)}, u32[]{:S(2)}) async-start(bf16[32,112,128]{2,1,0:T(8,128)(2,1)} %scatter.1), calls=%async_computation | async-start | bytes 1835008 | tf_op jit(solution)/shard_map/all_to_all | solution.py:477
  16.1 15.8 %copy-start.1 = (bf16[256,256]{1,0:T(8,128)(2,1)S(1)}, bf16[256,256]{1,0:T(8,128)(2,1)}, u32[]{:S(2)}) copy-start(bf16[256,256]{1,0:T(8,128)(2,1)} %ws_ref.5) | copy-start | bytes 393220
  16.1 15.7 %copy-start.2 = (bf16[256,256]{1,0:T(8,128)(2,1)S(1)}, bf16[256,256]{1,0:T(8,128)(2,1)}, u32[]{:S(2)}) copy-start(bf16[256,256]{1,0:T(8,128)(2,1)} %wn_ref.5) | copy-start | bytes 393220
  16.2 15.7 %copy-start.3 = (s32[16]{0:T(128)S(1)}, s32[16]{0:T(128)}, u32[]{:S(2)}) copy-start(s32[16]{0:T(128)} %ages_hbm.1) | copy-start | bytes 196
  37.0 35.7 %copy-start = (bf16[2048,256]{1,0:T(8,128)(2,1)S(1)}, bf16[2048,256]{1,0:T(8,128)(2,1)}, u32[]{:S(2)}) copy-start(bf16[2048,256]{1,0:T(8,128)(2,1)} %get-tuple-element.11.gp_hbm.gp_ref) | copy-start | bytes 3145732
  37.0 35.7 %copy-start.4 = (s32[1,32]{1,0:T(1,128)S(1)}, s32[1,32]{1,0:T(1,128)}, u32[]{:S(2)}) copy-start(s32[1,32]{1,0:T(1,128)} %counts_hbm.3) | copy-start | bytes 388
  37.0 13.1 %all-to-all-start.2 = ((bf16[32,32,128]{2,1,0:T(8,128)(2,1)}), bf16[32,32,128]{2,1,0:T(8,128)(2,1)S(1)}, u32[]{:S(2)}, u32[]{:S(2)}) async-start(bf16[32,32,128]{2,1,0:T(8,128)(2,1)} %get-tuple-element.13), calls=%async_computation.2 | async-start | bytes 524288 | tf_op jit(solution)/shard_map/all_to_all | solution.py:477
  50.1 18.5 %all-to-all-start.1 = ((bf16[32,96,128]{2,1,0:T(8,128)(2,1)}), bf16[32,96,128]{2,1,0:T(8,128)(2,1)S(1)}, u32[]{:S(2)}, u32[]{:S(2)}) async-start(bf16[32,96,128]{2,1,0:T(8,128)(2,1)} %outgoing.1.after_hbm), calls=%async_computation.1 | async-start | bytes 1572864 | tf_op jit(solution)/shard_map/all_to_all | solution.py:477
  54.4 5.3 %collective-permute-start.2 = (f32[32,128]{1,0:T(8,128)S(1)}, f32[32,128]{1,0:T(8,128)S(1)}, u32[]{:S(2)}, u32[]{:S(2)}) collective-permute-start(f32[32,128]{1,0:T(8,128)S(1)} %summed.1.own_ref), channel_id=1, source_target_pairs={{0,96},{32,64},{64,32},{96,0},{1,97},{33,65},{65,33},{97,1},{2,98}... | collective-permute-start | bytes 49160 | tf_op jit(solution)/shard_map/ppermute | solution.py:494
  58.3 4.4 %collective-permute-start.1 = (f32[32,128]{1,0:T(8,128)S(1)}, f32[32,128]{1,0:T(8,128)S(1)}, u32[]{:S(2)}, u32[]{:S(2)}) collective-permute-start(f32[32,128]{1,0:T(8,128)S(1)} %summed.1.own_ref), channel_id=1, source_target_pairs={{0,64},{32,96},{64,0},{96,32},{1,65},{33,97},{65,1},{97,33},{2,66}... | collective-permute-start | bytes 49160 | tf_op jit(solution)/shard_map/ppermute | solution.py:494
  58.3 4.4 %collective-permute-start = (f32[32,128]{1,0:T(8,128)S(1)}, f32[32,128]{1,0:T(8,128)S(1)}, u32[]{:S(2)}, u32[]{:S(2)}) collective-permute-start(f32[32,128]{1,0:T(8,128)S(1)} %summed.1.own_ref), channel_id=1, source_target_pairs={{0,32},{32,0},{64,96},{96,64},{1,33},{33,1},{65,97},{97,65},{2,34}... | collective-permute-start | bytes 49160 | tf_op jit(solution)/shard_map/ppermute | solution.py:494
  68.6 13.1 %all-to-all-start.3 = ((bf16[32,32,128]{2,1,0:T(8,128)(2,1)}), bf16[32,32,128]{2,1,0:T(8,128)(2,1)S(1)}, u32[]{:S(2)}, u32[]{:S(2)}) async-start(bf16[32,32,128]{2,1,0:T(8,128)(2,1)} %tied.1), calls=%async_computation.3 | async-start | bytes 524288 | tf_op jit(solution)/shard_map/all_to_all | solution.py:477
